TPU v7x, 32 devices: a whole 2x2x4 slice. The times are simulated.
32 devices in a mesh: dp: 2 (over x), space: 16 (over z, y, core).
Axes of the slice: x: 2, y: 2, z: 4, core: 2. Of those that a mesh axis runs over, the one named last changes fastest.
Arguments:
- crop: bfloat16 [2, 4, 64, 64, 64], P('dp', None, 'space'), may hold values from -6 to 6
- filter_one: bfloat16 [3, 3, 3, 4, 32], replicated, may hold values from -0.625 to 0.625
- filter_two: bfloat16 [3, 3, 3, 32, 64], replicated, may hold values from -0.21875 to 0.21875
- cotangent: bfloat16 [2, 64, 16, 16, 16], P('dp', None, 'space'), may hold values from -3 to 3
Outputs:
- features: bfloat16 [2, 64, 16, 16, 16], P('dp', None, 'space')
- grad_one: float32 [3, 3, 3, 4, 32], replicated
- grad_two: float32 [3, 3, 3, 32, 64], replicated
All inputs are finite; a program needn't handle non-finite values.
Results may differ from a plain program's by a relative error of at most 0.0045.
The roundings to bfloat16 on the way count: a program that leaves them out, or rounds other values in their place, can miss the bound.
Values may be sent and summed in bfloat16 or wider, within the bound.
No kernel may reach another device: no remote copies, remote signals or barrier semaphores. Data moves between devices by JAX's collectives and lax.ppermute only.
A program may use at most 128 MiB of HBM per device.

v0:
```python
import functools

import jax
import jax.numpy as jnp
from jax import lax
from jax.experimental import pallas as pl
from jax.experimental.pallas import tpu as pltpu
from jax.sharding import PartitionSpec as P

F32 = jnp.float32
BF16 = jnp.bfloat16
LANES = 256
VMEM = pl.BlockSpec(memory_space=pltpu.VMEM)


def iota(shape, axis):
    return lax.broadcasted_iota(jnp.int32, shape, axis)


def mm(a, b):
    return jnp.dot(a, b, preferred_element_type=F32)


def mm_nt(a, b):
    return lax.dot_general(a, b, (((1,), (1,)), ((), ())), preferred_element_type=F32)


def mm_tn(a, b):
    return lax.dot_general(a, b, (((0,), (0,)), ((), ())), preferred_element_type=F32)


def one_hot(mask):
    return jnp.where(mask, 1.0, 0.0).astype(BF16)


def blocks_kernel(crop_ref, cot_ref, out_ref, rows_ref):
    parity = lax.rem(lax.axis_index("space"), 2)
    row, col = iota((64, 1024), 0), iota((64, 1024), 1)
    spread = one_hot(row == 4 * lax.rem(col, 16) + col // LANES)
    own = (row // 4) == lax.rem(col, LANES) // 16
    for i in range(4):
        for p in range(4):
            wide = jnp.where(own, mm(crop_ref[0, i, p], spread), 0.0)
            part = wide[0:8]
            for k in range(1, 8):
                part = part + wide[8 * k : 8 * k + 8]
            for rr in range(4):
                at = rr * 128 + (i * 4 + p) * 8
                rows_ref[at : at + 8, :] = part[:, rr * LANES : (rr + 1) * LANES]
    n, m = iota((384, 512), 0), iota((384, 512), 1)
    m_rr, m_i, m_p, m_qq = m // 128, lax.rem(m, 128) // 32, lax.rem(m // 8, 4), lax.rem(m, 4)
    body = (
        (n < 256)
        & (n // 64 == m_qq)
        & (lax.rem(n // 16, 4) == m_rr)
        & (lax.rem(n // 4, 4) == m_p)
        & (lax.rem(n, 4) == m_i)
    )
    e = lax.rem(n, 64)
    plane = jnp.where(n < 320, 3 * parity, 3 - 3 * parity)
    edge = (
        (n >= 256)
        & (e // 16 == m_qq)
        & (lax.rem(e // 4, 4) == m_rr)
        & (plane == m_p)
        & (lax.rem(e, 4) == m_i)
    )
    packed = mm(one_hot(body | edge), rows_ref[...].astype(BF16)).astype(BF16)
    out_ref[0:256, :] = packed[0:256]
    out_ref[320:448, :] = packed[256:384]
    flat = cot_ref[0, :, 0].reshape(1024, 16)
    row, col = iota((16, LANES), 0), iota((16, LANES), 1)
    wide = mm(flat, one_hot(row == lax.rem(col, 16)))
    own = lax.rem(iota((1024, LANES), 0), 16) == iota((1024, LANES), 1) // 16
    wide = jnp.where(own, wide, 0.0).astype(BF16)
    gather = one_hot(iota((64, 1024), 0) == iota((64, 1024), 1) // 16)
    out_ref[256:320, :] = mm(gather, wide).astype(BF16)


def matrices_kernel(f1_ref, f2_ref, w1_ref, w2_ref, wb_ref, sh_ref):
    col = iota((1, 4096), 1)
    half, dp, dq, dr = col // 2048, lax.rem(col // 1024, 2), lax.rem(col // 512, 2), lax.rem(col // 256, 2)
    b = lax.rem(col // 64, 4) - dq
    c = lax.rem(col // 16, 4) - dr
    a = lax.rem(lax.rem(col // 4, 4) + 1 + 2 * half, 4) - dp
    inside = (a >= 0) & (a < 3) & (b >= 0) & (b < 3) & (c >= 0) & (c < 3)
    wanted = jnp.where(inside, (a * 9 + b * 3 + c) * 4 + lax.rem(col, 4), -1)
    place = one_hot(iota((108, 4096), 0) == wanted)
    w1 = mm_tn(f1_ref[...], place).astype(BF16)
    for k in range(16):
        w1_ref[k * 32 : (k + 1) * 32, :] = w1[:, k * LANES : (k + 1) * LANES]

    row, col = iota((96, 256), 0), iota((96, 256), 1)
    place = one_hot((lax.rem(row, 32) == lax.rem(col, 32)) & (lax.rem(col // 32, 4) == row // 32 + col // 128))
    for a in range(3):
        for b in range(3):
            at = (a * 9 + b * 3) * 32
            both = mm_tn(f2_ref[at : at + 96, :], place).astype(BF16)
            for fq in range(2):
                lane = a * 512 + (b + fq) * 128
                w2_ref[fq * 128 : fq * 128 + 64, lane : lane + 128] = both[:, 0:128]
                w2_ref[fq * 128 + 64 : fq * 128 + 128, lane : lane + 128] = both[:, 128:256]
        for fq in range(2):
            lane = a * 512 + (0 if fq else 3) * 128
            w2_ref[fq * 128 : fq * 128 + 128, lane : lane + 128] = jnp.zeros((128, 128), BF16)

    none = jnp.zeros((32, 64), BF16)
    for a in range(3):
        for b in range(3):
            at = ((2 - a) * 9 + (2 - b) * 3) * 32
            taps = [f2_ref[at + 32 * k : at + 32 * k + 32, :] for k in (2, 1, 0)]
            for er in range(2):
                block = jnp.concatenate([none] + taps if er else taps + [none], axis=1)
                for eq in range(2):
                    lane = a * 1024 + (b + eq) * 256
                    at_row = (eq * 2 + er) * 32
                    wb_ref[at_row : at_row + 32, lane : lane + 256] = block
        for eq in range(2):
            lane = a * 1024 + (0 if eq else 3) * 256
            wb_ref[eq * 64 : eq * 64 + 64, lane : lane + 256] = jnp.zeros((64, 256), BF16)

    k, lane = iota((LANES, LANES), 0), iota((LANES, LANES), 1)
    sh_ref[0] = one_hot(k == lane - 16)
    sh_ref[1] = one_hot(k == lane + 16)
    sh_ref[2] = one_hot((k == lane - 1) & (lax.rem(lane, 16) != 0))
    sh_ref[3] = one_hot((k == lane + 1) & (lax.rem(lane, 16) != 15))


def main_kernel(own_ref, near_ref, far_ref, fwd_ref, w1_ref, w2_ref, wb_ref, sh_ref,
                feat_ref, keep_ref, send_ref,
                mg, xt, z1, a_ext, g_ext, taps, pack):
    index = lax.axis_index("space")
    parity = lax.rem(index, 2)
    even = parity == 0
    has_left = jnp.where(index > 0, 1.0, 0.0)
    has_right = jnp.where(index < lax.axis_size("space") - 1, 1.0, 0.0)
    pick = jnp.where(even, 1.0, 0.0)

    def choose(x, y):
        return (x.astype(F32) * pick + y.astype(F32) * (1.0 - pick)).astype(BF16)

    near, far = near_ref[0:320, :], far_ref[0:320, :]
    left, right = choose(far, near), choose(near, far)
    edge_far, edge_fwd = far_ref[384:448, :], fwd_ref[...]
    edge_left, edge_right = choose(edge_far, edge_fwd), choose(edge_fwd, edge_far)
    own = own_ref[0:256, :]

    rows = iota((256, LANES), 0)
    is_last, is_first = one_hot(lax.rem(rows // 4, 4) == 3), one_hot(lax.rem(rows // 4, 4) == 0)
    n, m = iota((256, 64), 0), iota((256, 64), 1)
    same = (n // 16 == m // 4) & (lax.rem(n, 4) == lax.rem(m, 4))
    last_left = mm(one_hot(same & (lax.rem(n // 4, 4) == 3)), edge_left).astype(BF16)
    first_right = mm(one_hot(same & (lax.rem(n // 4, 4) == 0)), edge_right).astype(BF16)
    blocks = (left[0:256], own, right[0:256])
    not_last, not_first = 1 - is_last, 1 - is_first
    for k in range(3):
        before = last_left if k == 0 else blocks[k - 1] * is_last
        after = first_right if k == 2 else blocks[k + 1] * is_first
        mg[2 * k] = blocks[k] * not_last + before
        mg[2 * k + 1] = blocks[k] * not_first + after

    for k in range(6):
        for qq in range(4):
            at = ((qq + 1) * 6 + 1) * 16
            xt[k, at : at + 64, :] = mg[k, qq * 64 : qq * 64 + 64, :]
    up = mm(mg[:, 192:256, :].reshape(384, LANES), sh_ref[0]).astype(BF16)
    down = mm(mg[:, 0:64, :].reshape(384, LANES), sh_ref[1]).astype(BF16)
    for k in range(6):
        xt[k, 16:80, :] = up[k * 64 : k * 64 + 64]
        xt[k, 496:560, :] = down[k * 64 : k * 64 + 64]
    last_r = jnp.concatenate([xt[k, (q * 6 + 4) * 16 : (q * 6 + 5) * 16, :] for k in range(6) for q in range(6)], axis=0)
    first_r = jnp.concatenate([xt[k, (q * 6 + 1) * 16 : (q * 6 + 2) * 16, :] for k in range(6) for q in range(6)], axis=0)
    up = mm(last_r, sh_ref[2]).astype(BF16)
    down = mm(first_r, sh_ref[3]).astype(BF16)
    for k in range(6):
        for q in range(6):
            at = (k * 6 + q) * 16
            xt[k, q * 96 : q * 96 + 16, :] = up[at : at + 16]
            xt[k, q * 96 + 80 : q * 96 + 96, :] = down[at : at + 16]

    def patch(k, eq, er):
        parts = []
        for b in range(4):
            at = ((2 * eq + b) * 6 + 2 * er) * 16
            parts.append(xt[k, at : at + 64, :])
        return jnp.concatenate(parts, axis=0)

    for k in range(6):
        for eq in range(2):
            for er in range(2):
                z = mm(w1_ref[(k % 2) * 256 : (k % 2) * 256 + 256, :], patch(k, eq, er))
                if k // 2 == 1:
                    z1[(k % 2) * 4 + eq * 2 + er] = z
                act = jnp.where(z > 0, z, 0.3 * z)
                total = act[0:32]
                for d in range(1, 8):
                    total = total + act[d * 32 : d * 32 + 32]
                total = total * 0.125
                if k // 2 == 0:
                    total = total * has_left
                if k // 2 == 2:
                    total = total * has_right
                at = ((eq + 1) * 4 + er + 1) * 32
                a_ext[k, at : at + 32, :] = total.astype(BF16)

    def extend(ref, planes, size):
        for source, target, matrix in ((2, 0, 0), (1, 3, 1)):
            at, to = (source * 4 + 1) * size, (target * 4 + 1) * size
            block = ref[:, at : at + 2 * size, :].reshape(planes * 2 * size, LANES)
            moved = mm(block, sh_ref[matrix]).astype(BF16)
            ref[:, to : to + 2 * size, :] = moved.reshape(planes, 2 * size, LANES)
        for source, target, matrix in ((2, 0, 2), (1, 3, 3)):
            block = jnp.concatenate(
                [ref[k, (q * 4 + source) * size : (q * 4 + source + 1) * size, :] for k in range(planes) for q in range(4)],
                axis=0,
            )
            moved = mm(block, sh_ref[matrix]).astype(BF16)
            for k in range(planes):
                for q in range(4):
                    at = (k * 4 + q) * size
                    ref[k, (q * 4 + target) * size : (q * 4 + target + 1) * size, :] = moved[at : at + size]

    extend(a_ext, 6, 32)

    feats = jnp.zeros((64, LANES), F32)
    cots = (left[256:320], own_ref[256:320, :], own_ref[256:320, :], right[256:320])
    for t in range(4):
        z = mm(w2_ref[...], a_ext[t : t + 3].reshape(1536, LANES))
        cot = cots[t].astype(F32)
        full, low = cot * 0.125, 0.3 * cot * 0.125
        for f in range(4):
            zf = z[f * 64 : f * 64 + 64]
            if t in (1, 2):
                feats = feats + jnp.where(zf > 0, zf, 0.3 * zf)
            at = ((f // 2 + 1) * 4 + f % 2 + 1) * 64
            g_ext[t, at : at + 64, :] = jnp.where(zf > 0, full, low).astype(BF16)
    feat_ref[...] = (feats * 0.125).astype(BF16)

    lane = iota((48, 128), 1)
    for a in range(3):
        acc = jnp.zeros((384, 128), F32)
        for t in range(2):
            for fq in range(2):
                maps = a_ext[t + 1 + a, fq * 128 : fq * 128 + 384, :]
                at = ((fq + 1) * 4 + 1) * 64
                acc = acc + mm_nt(maps, g_ext[t + 1, at : at + 128, :])
        for b in range(3):
            block = acc[b * 128 : b * 128 + 128]
            swapped = pltpu.roll(block, 64, 1)
            for h in range(2):
                chunk = (a * 3 + b) * 2 + h
                lo = h * 48
                if chunk < 9:
                    value = block[lo : lo + 48] + swapped[lo + 32 : lo + 80]
                    pack[chunk * 48 : chunk * 48 + 48, 0:64] = value[:, 0:64]
                else:
                    value = swapped[lo : lo + 48] + block[lo + 32 : lo + 80]
                    pack[(chunk - 9) * 48 : (chunk - 8) * 48, 64:128] = value[:, 64:128]

    extend(g_ext, 4, 64)

    for s in range(2):
        back = mm(wb_ref[...], g_ext[s : s + 3].reshape(3072, LANES))
        acc = jnp.zeros((256, 256), F32)
        for eq in range(2):
            for er in range(2):
                part = back[(eq * 2 + er) * 32 : (eq * 2 + er) * 32 + 32]
                full, low = part * 0.125, 0.3 * part * 0.125
                z = z1[s * 4 + eq * 2 + er].reshape(8, 32, LANES)
                grad = jnp.where(z > 0, full[None], low[None]).astype(BF16).reshape(256, LANES)
                acc = acc + mm_nt(patch(2 + s, eq, er), grad)
        cells = acc.reshape(16, 16, 256)
        turn = 12 if s == 0 else 4
        cells = jnp.concatenate([cells[:, turn:], cells[:, :turn]], axis=1).reshape(256, 256)
        if s == 0:
            taps[0:256, :] = cells
        else:
            taps[0:256, :] = taps[0:256, :] + cells
    taps[256:288, :] = jnp.zeros((32, 256), F32)
    total = jnp.zeros((192, 32), F32)
    for d in range(8):
        off = (d // 2 % 2) * 64 + (d % 2) * 16 + (d // 4) * 4
        total = total + taps[off : off + 192, d * 32 : d * 32 + 32]
    pack[432:480, :] = jnp.concatenate([total[k * 48 : k * 48 + 48] for k in range(4)], axis=1)

    keep_ref[...] = pack[pl.ds(pl.multiple_of(parity * 240, 8), 240), :]
    send_ref[...] = pack[pl.ds(pl.multiple_of(240 - parity * 240, 8), 240), :]


def finish_kernel(mine_ref, other_ref, one_ref, two_ref, both):
    parity = lax.rem(lax.axis_index("space"), 2)
    both[pl.ds(pl.multiple_of(parity * 240, 8), 240), :] = mine_ref[...]
    both[pl.ds(pl.multiple_of(240 - parity * 240, 8), 240), :] = other_ref[...]
    two_ref[0:432, :] = both[0:432, 0:64]
    two_ref[432:864, :] = both[0:432, 64:128]
    for a in range(3):
        for b in range(3):
            for c in range(3):
                at = b * 64 + c * 16 + a * 4
                k, row = at // 48, at % 48
                one_ref[a * 9 + b * 3 + c] = both[432 + row : 436 + row, k * 32 : k * 32 + 32]


def call(kernel, outs, scratch=(), flops=0, size=0):
    return pl.pallas_call(
        kernel,
        out_shape=outs,
        out_specs=jax.tree.map(lambda _: VMEM, outs),
        scratch_shapes=list(scratch),
        compiler_params=pltpu.CompilerParams(vmem_limit_bytes=48 * 1024 * 1024),
        cost_estimate=pl.CostEstimate(flops=flops, bytes_accessed=size, transcendentals=0),
    )


def shape(dims, dtype):
    return jax.ShapeDtypeStruct(dims, dtype)


def pair_perm(pairs):
    return [(i, j) for i, j in pairs] + [(j, i) for i, j in pairs]


def total_over_mesh(keep, send, n_dp, n_space):
    axes = ("dp", "space")
    size = n_dp * n_space
    near = [(i, i ^ 1) for i in range(size)]
    mine = keep + lax.ppermute(send, axes, near)
    bits = [b for b in (1 << k for k in range(1, 31)) if b < size]
    order = {0: bits[::-1], 1: bits[1::-1] + bits[:1:-1]}
    for step in range(len(bits)):
        perm = [(i, i ^ order[i % 2][step]) for i in range(size)]
        mine = mine + lax.ppermute(mine, axes, perm)
    return mine, lax.ppermute(mine, axes, near)


def local(n_dp, n_space, crop, filter_one, filter_two, cotangent):
    near = [(i, i ^ 1) for i in range(n_space)]
    across = pair_perm([(i, i + 1) for i in range(1, n_space - 1, 2)])
    with jax.named_scope("blocks"):
        own = call(blocks_kernel, shape((448, LANES), BF16), [pltpu.VMEM((512, LANES), F32)])(crop, cotangent)
    with jax.named_scope("halo"):
        beside = lax.ppermute(own, "space", near)
        out = jnp.concatenate([own[:384], beside[384:]], axis=0)
        beyond = lax.ppermute(out, "space", across)
        forward = lax.ppermute(beyond[320:384], "space", near)
    with jax.named_scope("matrices"):
        w1, w2, wb, shifts = call(
            matrices_kernel,
            (shape((512, 256), BF16), shape((256, 1536), BF16), shape((128, 3072), BF16), shape((4, LANES, LANES), BF16)),
            flops=500_000_000, size=2_500_000,
        )(filter_one.reshape(108, 32), filter_two.reshape(864, 64))
    with jax.named_scope("sections"):
        feats, keep, send = call(
            main_kernel,
            (shape((64, LANES), BF16), shape((240, 128), F32), shape((240, 128), F32)),
            [
                pltpu.VMEM((6, 256, LANES), BF16),
                pltpu.VMEM((6, 576, LANES), BF16),
                pltpu.VMEM((8, 256, LANES), F32),
                pltpu.VMEM((6, 512, LANES), BF16),
                pltpu.VMEM((4, 1024, LANES), BF16),
                pltpu.VMEM((288, 256), F32),
                pltpu.VMEM((480, 128), F32),
            ],
            flops=5_000_000_000, size=6_000_000,
        )(own, beside, beyond, forward, w1, w2, wb, shifts)
    with jax.named_scope("total"):
        mine, other = total_over_mesh(keep, send, n_dp, n_space)
        one, two = call(
            finish_kernel,
            (shape((27, 4, 32), F32), shape((864, 64), F32)),
            [pltpu.VMEM((480, 128), F32)],
        )(mine, other)
    features = feats.reshape(1, 64, 1, 16, 16)
    return features, one.reshape(3, 3, 3, 4, 32), two.reshape(3, 3, 3, 32, 64)


def solution(mesh):
    n_dp, n_space = mesh.shape["dp"], mesh.shape["space"]
    assert n_space % 2 == 0 and (n_dp * n_space) & (n_dp * n_space - 1) == 0, "mesh sizes"
    placed = (P("dp", None, "space", None, None), P(), P(), P("dp", None, "space", None, None))
    return jax.shard_map(
        functools.partial(local, n_dp, n_space),
        mesh=mesh,
        in_specs=placed,
        out_specs=(P("dp", None, "space", None, None), P(), P()),
        check_vma=False,
    )
```

profile of v0, /device:TPU:0, one launch (start us, length us, event | category | flops | bytes accessed | tf_op | source)
XLA Modules:
  0.0 49.4 jit_solution(308861744193300732)
XLA Ops:
  0.6 0.0 copy-start
  0.6 1.1 %copy.9.cot_ref = bf16[1,64,1,16,16]{4,3,2,1,0:T(8,128)(2,1)S(1)} copy(bf16[1,64,1,16,16]{1,4,3,2,0:T(8,128)(2,1)} %param.7) | data formatting | bytes 65536 | tf_op args[3]
  1.8 0.0 copy-done
  1.8 1.2 %blocks.1.own_ref = bf16[448,256]{1,0:T(8,128)(2,1)S(1)} custom-call(bf16[1,4,4,64,64]{4,3,2,1,0:T(8,128)(2,1)S(1)} %copy-done, bf16[1,64,1,16,16]{4,3,2,1,0:T(8,128)(2,1)S(1)} %copy.9.cot_ref), custom_call_target="tpu_custom_call" | custom-call | tf_op jit(solution)/shard_map/blocks/pallas_call | solution.py:340
  2.9 0.5 %collective-permute-start = (bf16[448,256]{1,0:T(8,128)(2,1)S(1)}, bf16[448,256]{1,0:T(8,128)(2,1)S(1)}, u32[]{:S(2)}, u32[]{:S(2)}) collective-permute-start(bf16[448,256]{1,0:T(8,128)(2,1)S(1)} %blocks.1.own_ref), channel_id=1, source_target_pairs={{0,1},{1,0},{2,3},{3,2},{4,5},{5,4},{6,7},{7,6},{8,9},{9,8},{10,11... | collective-permute-start | bytes 688136 | tf_op jit(solution)/shard_map/halo/ppermute | solution.py:342
  3.5 1.1 %collective-permute-done.near_ref = bf16[448,256]{1,0:T(8,128)(2,1)S(1)} collective-permute-done((bf16[448,256]{1,0:T(8,128)(2,1)S(1)}, bf16[448,256]{1,0:T(8,128)(2,1)S(1)}, u32[]{:S(2)}, u32[]{:S(2)}) %collective-permute-start) | collective-permute-done | bytes 229408 | tf_op jit(solution)/shard_map/halo/ppermute | solution.py:342
  4.6 0.0 copy-start.2
  4.6 0.0 copy-start.1
  4.6 0.8 %collective-permute-start.1 = (bf16[448,256]{1,0:T(8,128)(2,1)S(1)}, bf16[448,256]{1,0:T(8,128)(2,1)S(1)}, u32[]{:S(2)}, u32[]{:S(2)}) collective-permute-start(bf16[448,256]{1,0:T(8,128)(2,1)S(1)} %pad_maximum_fusion), channel_id=1, source_target_pairs={{1,2},{3,4},{5,6},{7,8},{9,10},{11,12},{13,14},{2,1},{4,3},{6,5},{... | collective-permute-start | bytes 688136 | tf_op jit(solution)/shard_map/halo/ppermute | solution.py:344
  5.4 0.0 copy-done.2
  5.5 0.0 collective-permute-done.1.far_ref
  5.5 9.6 %collective-permute-start.2 = (bf16[64,256]{1,0:T(8,128)(2,1)S(1)}, bf16[64,256]{1,0:T(8,128)(2,1)S(1)}, u32[]{:S(2)}, u32[]{:S(2)}) collective-permute-start(bf16[64,256]{1,0:T(8,128)(2,1)S(1)} %slice.14), channel_id=1, source_target_pairs={{0,1},{1,0},{2,3},{3,2},{4,5},{5,4},{6,7},{7,6},{8,9},{9,8},{10,11... | collective-permute-start | bytes 98312 | tf_op jit(solution)/shard_map/halo/ppermute | solution.py:345
  15.1 0.0 copy-done.1
  15.1 0.7 %matrices.1 = (bf16[512,256]{1,0:T(8,128)(2,1)S(1)}, bf16[256,1536]{1,0:T(8,128)(2,1)S(1)}, bf16[128,3072]{1,0:T(8,128)(2,1)S(1)}, bf16[4,256,256]{2,1,0:T(8,128)(2,1)S(1)}) custom-call(bf16[108,32]{1,0:T(8,128)(2,1)S(1)} %reshape.21.f1_ref, bf16[864,64]{1,0:T(8,128)(2,1)S(1)} %bitcast.4), custom_call_target="tpu_custom_call" | custom-call | flops 500000000 | bytes 2500000 | tf_op jit(solution)/shard_map/matrices/pallas_call | solution.py:347
  15.8 0.1 collective-permute-done.2.fwd_ref
  15.9 5.7 %sections.1 = (bf16[64,256]{1,0:T(8,128)(2,1)S(1)}, f32[240,128]{1,0:T(8,128)S(1)}, f32[240,128]{1,0:T(8,128)S(1)}) custom-call(bf16[448,256]{1,0:T(8,128)(2,1)S(1)} %blocks.1.own_ref, bf16[448,256]{1,0:T(8,128)(2,1)S(1)} %collective-permute-done.near_ref, bf16[448,256]{1,0:T(8,128)(2,1)S(1)} %collective-permute-done.1.far_ref, ...), custom_call_target="tpu_custom_call" | custom-call | flops 5000000000 | bytes 6000000 | tf_op jit(solution)/shard_map/sections/pallas_call | solution.py:353
  21.6 0.4 collective-permute-start.3
  22.1 1.0 %collective-permute-done.3 = f32[240,128]{1,0:T(8,128)S(1)} collective-permute-done((f32[240,128]{1,0:T(8,128)S(1)}, f32[240,128]{1,0:T(8,128)S(1)}, u32[]{:S(2)}, u32[]{:S(2)}) %collective-permute-start.3) | collective-permute-done | bytes 122912 | tf_op jit(solution)/shard_map/total/ppermute | solution.py:327
  23.1 1.6 %collective-permute-start.4 = (f32[240,128]{1,0:T(8,128)S(1)}, f32[240,128]{1,0:T(8,128)S(1)}, u32[]{:S(2)}, u32[]{:S(2)}) collective-permute-start(f32[240,128]{1,0:T(8,128)S(1)} %add.15), channel_id=1, source_target_pairs={{0,16},{1,5},{2,18},{3,7},{4,20},{5,1},{6,22},{7,3},{8,24},{9,13},... | collective-permute-start | bytes 368648 | tf_op jit(solution)/shard_map/total/ppermute | solution.py:332
  24.6 3.4 %collective-permute-done.4 = f32[240,128]{1,0:T(8,128)S(1)} collective-permute-done((f32[240,128]{1,0:T(8,128)S(1)}, f32[240,128]{1,0:T(8,128)S(1)}, u32[]{:S(2)}, u32[]{:S(2)}) %collective-permute-start.4) | collective-permute-done | bytes 122912 | tf_op jit(solution)/shard_map/total/ppermute | solution.py:332
  28.0 3.6 %collective-permute-start.5 = (f32[240,128]{1,0:T(8,128)S(1)}, f32[240,128]{1,0:T(8,128)S(1)}, u32[]{:S(2)}, u32[]{:S(2)}) collective-permute-start(f32[240,128]{1,0:T(8,128)S(1)} %add.16), channel_id=1, source_target_pairs={{0,8},{1,3},{2,10},{3,1},{4,12},{5,7},{6,14},{7,5},{8,0},{9,11},{1... | collective-permute-start | bytes 368648 | tf_op jit(solution)/shard_map/total/ppermute | solution.py:332
  31.7 2.9 %collective-permute-done.5 = f32[240,128]{1,0:T(8,128)S(1)} collective-permute-done((f32[240,128]{1,0:T(8,128)S(1)}, f32[240,128]{1,0:T(8,128)S(1)}, u32[]{:S(2)}, u32[]{:S(2)}) %collective-permute-start.5) | collective-permute-done | bytes 122912 | tf_op jit(solution)/shard_map/total/ppermute | solution.py:332
  34.5 2.4 %collective-permute-start.6 = (f32[240,128]{1,0:T(8,128)S(1)}, f32[240,128]{1,0:T(8,128)S(1)}, u32[]{:S(2)}, u32[]{:S(2)}) collective-permute-start(f32[240,128]{1,0:T(8,128)S(1)} %add.17), channel_id=1, source_target_pairs={{0,4},{1,17},{2,6},{3,19},{4,0},{5,21},{6,2},{7,23},{8,12},{9,25},... | collective-permute-start | bytes 368648 | tf_op jit(solution)/shard_map/total/ppermute | solution.py:332
  36.9 4.0 %collective-permute-done.6 = f32[240,128]{1,0:T(8,128)S(1)} collective-permute-done((f32[240,128]{1,0:T(8,128)S(1)}, f32[240,128]{1,0:T(8,128)S(1)}, u32[]{:S(2)}, u32[]{:S(2)}) %collective-permute-start.6) | collective-permute-done | bytes 122912 | tf_op jit(solution)/shard_map/total/ppermute | solution.py:332
  40.9 3.3 %collective-permute-start.7 = (f32[240,128]{1,0:T(8,128)S(1)}, f32[240,128]{1,0:T(8,128)S(1)}, u32[]{:S(2)}, u32[]{:S(2)}) collective-permute-start(f32[240,128]{1,0:T(8,128)S(1)} %add.18), channel_id=1, source_target_pairs={{0,2},{1,9},{2,0},{3,11},{4,6},{5,13},{6,4},{7,15},{8,10},{9,1},{1... | collective-permute-start | bytes 368648 | tf_op jit(solution)/shard_map/total/ppermute | solution.py:332
  44.2 2.9 %collective-permute-done.7 = f32[240,128]{1,0:T(8,128)S(1)} collective-permute-done((f32[240,128]{1,0:T(8,128)S(1)}, f32[240,128]{1,0:T(8,128)S(1)}, u32[]{:S(2)}, u32[]{:S(2)}) %collective-permute-start.7) | collective-permute-done | bytes 122912 | tf_op jit(solution)/shard_map/total/ppermute | solution.py:332
  47.1 0.1 collective-permute-start.8
  47.2 0.7 %copy.10 = bf16[64,256]{0,1:T(8,128)(2,1)} copy(bf16[64,256]{1,0:T(8,128)(2,1)S(1)} %get-tuple-element.16) | data formatting | bytes 65536 | tf_op jit(solution)/shard_map/sections/pallas_call | solution.py:353
  47.9 0.6 %collective-permute-done.8.other_ref = f32[240,128]{1,0:T(8,128)S(1)} collective-permute-done((f32[240,128]{1,0:T(8,128)S(1)}, f32[240,128]{1,0:T(8,128)S(1)}, u32[]{:S(2)}, u32[]{:S(2)}) %collective-permute-start.8) | collective-permute-done | bytes 122912 | tf_op jit(solution)/shard_map/total/ppermute | solution.py:333
  48.5 0.9 %total.1 = (f32[27,4,32]{2,1,0:T(4,128)}, f32[864,64]{1,0:T(8,128)}) custom-call(f32[240,128]{1,0:T(8,128)S(1)} %add.19.mine_ref, f32[240,128]{1,0:T(8,128)S(1)} %collective-permute-done.8.other_ref), custom_call_target="tpu_custom_call" | custom-call | tf_op jit(solution)/shard_map/total/pallas_call | solution.py:369
  (10 shorter events, 0.1 us)
Async XLA Ops:
  0.6 1.1 %copy-start = (bf16[1,4,4,64,64]{4,3,2,1,0:T(8,128)(2,1)S(1)}, bf16[1,4,4,64,64]{4,3,2,1,0:T(8,128)(2,1)}, u32[]{:S(2)}) copy-start(bf16[1,4,4,64,64]{4,3,2,1,0:T(8,128)(2,1)} %crop_ref.1) | copy-start | bytes 393220
  2.9 1.6 %collective-permute-start = (bf16[448,256]{1,0:T(8,128)(2,1)S(1)}, bf16[448,256]{1,0:T(8,128)(2,1)S(1)}, u32[]{:S(2)}, u32[]{:S(2)}) collective-permute-start(bf16[448,256]{1,0:T(8,128)(2,1)S(1)} %blocks.1.own_ref), channel_id=1, source_target_pairs={{0,1},{1,0},{2,3},{3,2},{4,5},{5,4},{6,7},{7,6},{8,9},{9,8},{10,11... | collective-permute-start | bytes 688136 | tf_op jit(solution)/shard_map/halo/ppermute | solution.py:342
  4.6 0.8 %copy-start.2 = (bf16[3,3,3,4,32]{4,3,2,1,0:T(4,128)(2,1)S(1)}, bf16[3,3,3,4,32]{4,3,2,1,0:T(4,128)(2,1)}, u32[]{:S(2)}) copy-start(bf16[3,3,3,4,32]{4,3,2,1,0:T(4,128)(2,1)} %param.5) | copy-start | bytes 20740
  4.6 10.5 %copy-start.1 = (bf16[3,3,3,32,64]{4,3,2,1,0:T(8,128)(2,1)S(1)}, bf16[3,3,3,32,64]{4,3,2,1,0:T(8,128)(2,1)}, u32[]{:S(2)}) copy-start(bf16[3,3,3,32,64]{4,3,2,1,0:T(8,128)(2,1)} %param.6) | copy-start | bytes 331780
  4.6 0.9 %collective-permute-start.1 = (bf16[448,256]{1,0:T(8,128)(2,1)S(1)}, bf16[448,256]{1,0:T(8,128)(2,1)S(1)}, u32[]{:S(2)}, u32[]{:S(2)}) collective-permute-start(bf16[448,256]{1,0:T(8,128)(2,1)S(1)} %pad_maximum_fusion), channel_id=1, source_target_pairs={{1,2},{3,4},{5,6},{7,8},{9,10},{11,12},{13,14},{2,1},{4,3},{6,5},{... | collective-permute-start | bytes 688136 | tf_op jit(solution)/shard_map/halo/ppermute | solution.py:344
  5.5 10.4 %collective-permute-start.2 = (bf16[64,256]{1,0:T(8,128)(2,1)S(1)}, bf16[64,256]{1,0:T(8,128)(2,1)S(1)}, u32[]{:S(2)}, u32[]{:S(2)}) collective-permute-start(bf16[64,256]{1,0:T(8,128)(2,1)S(1)} %slice.14), channel_id=1, source_target_pairs={{0,1},{1,0},{2,3},{3,2},{4,5},{5,4},{6,7},{7,6},{8,9},{9,8},{10,11... | collective-permute-start | bytes 98312 | tf_op jit(solution)/shard_map/halo/ppermute | solution.py:345
  21.6 1.4 %collective-permute-start.3 = (f32[240,128]{1,0:T(8,128)S(1)}, f32[240,128]{1,0:T(8,128)S(1)}, u32[]{:S(2)}, u32[]{:S(2)}) collective-permute-start(f32[240,128]{1,0:T(8,128)S(1)} %get-tuple-element.18), channel_id=1, source_target_pairs={{0,1},{1,0},{2,3},{3,2},{4,5},{5,4},{6,7},{7,6},{8,9},{9,8},{10,11... | collective-permute-start | bytes 368648 | tf_op jit(solution)/shard_map/total/ppermute | solution.py:327
  23.1 4.9 %collective-permute-start.4 = (f32[240,128]{1,0:T(8,128)S(1)}, f32[240,128]{1,0:T(8,128)S(1)}, u32[]{:S(2)}, u32[]{:S(2)}) collective-permute-start(f32[240,128]{1,0:T(8,128)S(1)} %add.15), channel_id=1, source_target_pairs={{0,16},{1,5},{2,18},{3,7},{4,20},{5,1},{6,22},{7,3},{8,24},{9,13},... | collective-permute-start | bytes 368648 | tf_op jit(solution)/shard_map/total/ppermute | solution.py:332
  28.0 6.5 %collective-permute-start.5 = (f32[240,128]{1,0:T(8,128)S(1)}, f32[240,128]{1,0:T(8,128)S(1)}, u32[]{:S(2)}, u32[]{:S(2)}) collective-permute-start(f32[240,128]{1,0:T(8,128)S(1)} %add.16), channel_id=1, source_target_pairs={{0,8},{1,3},{2,10},{3,1},{4,12},{5,7},{6,14},{7,5},{8,0},{9,11},{1... | collective-permute-start | bytes 368648 | tf_op jit(solution)/shard_map/total/ppermute | solution.py:332
  34.5 6.4 %collective-permute-start.6 = (f32[240,128]{1,0:T(8,128)S(1)}, f32[240,128]{1,0:T(8,128)S(1)}, u32[]{:S(2)}, u32[]{:S(2)}) collective-permute-start(f32[240,128]{1,0:T(8,128)S(1)} %add.17), channel_id=1, source_target_pairs={{0,4},{1,17},{2,6},{3,19},{4,0},{5,21},{6,2},{7,23},{8,12},{9,25},... | collective-permute-start | bytes 368648 | tf_op jit(solution)/shard_map/total/ppermute | solution.py:332
  40.9 6.2 %collective-permute-start.7 = (f32[240,128]{1,0:T(8,128)S(1)}, f32[240,128]{1,0:T(8,128)S(1)}, u32[]{:S(2)}, u32[]{:S(2)}) collective-permute-start(f32[240,128]{1,0:T(8,128)S(1)} %add.18), channel_id=1, source_target_pairs={{0,2},{1,9},{2,0},{3,11},{4,6},{5,13},{6,4},{7,15},{8,10},{9,1},{1... | collective-permute-start | bytes 368648 | tf_op jit(solution)/shard_map/total/ppermute | solution.py:332
  47.1 1.4 %collective-permute-start.8 = (f32[240,128]{1,0:T(8,128)S(1)}, f32[240,128]{1,0:T(8,128)S(1)}, u32[]{:S(2)}, u32[]{:S(2)}) collective-permute-start(f32[240,128]{1,0:T(8,128)S(1)} %add.19.mine_ref), channel_id=1, source_target_pairs={{0,1},{1,0},{2,3},{3,2},{4,5},{5,4},{6,7},{7,6},{8,9},{9,8},{10,11... | collective-permute-start | bytes 368648 | tf_op jit(solution)/shard_map/total/ppermute | solution.py:333
where the time goes:
time: 49.6 us; the launch traced here: 49.4 us
  starting transfers between devices  22.3 us (45%)
  waiting for transfers between devices  15.9 us (32%)
  Pallas kernels  8.51 us (17%)
  local copies, waits for them, and re-layouts  1.92 us (4%)
  between operations  0.75 us (2%)
    ppermute x4, waiting for transfers between devices, total_over_mesh(): mine = mine + lax.ppermute(mine, axes, perm)  13.1 us
    ppermute x4, starting transfers between devices, total_over_mesh(): mine = mine + lax.ppermute(mine, axes, perm)  10.9 us
    ppermute x1, starting transfers between devices, local(): forward = lax.ppermute(beyond[320:384], 'space', near)  9.59 us
    pallas_call x1, Pallas kernels, local(): call(main_kernel, (shape((64, LANES), BF16), shape((240, 128), F32), shap...  5.7 us
    pallas_call x1, Pallas kernels, local(): call(blocks_kernel, shape((448, LANES), BF16), [pltpu.VMEM((512, LANES),...  1.15 us
    unnamed x7, local copies, waits for them, and re-layouts  1.14 us
    ppermute x1, waiting for transfers between devices, local(): beside = lax.ppermute(own, 'space', near)  1.1 us
  transfers between devices with their start and end apart: 9, of which 8 were waited for; matrix products, arithmetic and copies ran while one was open for 2% of the time, Pallas kernels for 2%

commit v1 on v0

v1 whole, which is shorter than its diff:
```python
import functools

import jax
import jax.numpy as jnp
from jax import lax
from jax.experimental import pallas as pl
from jax.experimental.pallas import tpu as pltpu
from jax.sharding import PartitionSpec as P

F32 = jnp.float32
BF16 = jnp.bfloat16
LANES = 256
VMEM = pl.BlockSpec(memory_space=pltpu.VMEM)


def iota(shape, axis):
    return lax.broadcasted_iota(jnp.int32, shape, axis)


def mm(a, b):
    return jnp.dot(a, b, preferred_element_type=F32)


def mm_nt(a, b):
    return lax.dot_general(a, b, (((1,), (1,)), ((), ())), preferred_element_type=F32)


def mm_tn(a, b):
    return lax.dot_general(a, b, (((0,), (0,)), ((), ())), preferred_element_type=F32)


def one_hot(mask):
    return jnp.where(mask, 1.0, 0.0).astype(BF16)


def blocks_kernel(crop_ref, own_ref, edge_ref, rows_ref):
    parity = lax.rem(lax.axis_index("space"), 2)
    row, col = iota((64, 1024), 0), iota((64, 1024), 1)
    spread = one_hot(row == 4 * lax.rem(col, 16) + col // LANES)
    own = (row // 4) == lax.rem(col, LANES) // 16
    for i in range(4):
        for p in range(4):
            wide = jnp.where(own, mm(crop_ref[0, i, p], spread), 0.0)
            part = wide[0:8]
            for k in range(1, 8):
                part = part + wide[8 * k : 8 * k + 8]
            for rr in range(4):
                at = rr * 128 + (i * 4 + p) * 8
                rows_ref[at : at + 8, :] = part[:, rr * LANES : (rr + 1) * LANES]
    n, m = iota((320, 512), 0), iota((320, 512), 1)
    m_rr, m_i, m_p, m_qq = m // 128, lax.rem(m, 128) // 32, lax.rem(m // 8, 4), lax.rem(m, 4)
    body = (
        (n < 256)
        & (n // 64 == m_qq)
        & (lax.rem(n // 16, 4) == m_rr)
        & (lax.rem(n // 4, 4) == m_p)
        & (lax.rem(n, 4) == m_i)
    )
    e = n - 256
    edge = (
        (n >= 256)
        & (e // 16 == m_qq)
        & (lax.rem(e // 4, 4) == m_rr)
        & (3 - 3 * parity == m_p)
        & (lax.rem(e, 4) == m_i)
    )
    packed = mm(one_hot(body | edge), rows_ref[...].astype(BF16)).astype(BF16)
    own_ref[...] = packed[0:256]
    edge_ref[...] = packed[256:320]


def matrices(f1_ref, f2_ref, w1_ref, w2_ref, wb_ref, sh_ref):
    col = iota((1, 4096), 1)
    half, dp, dq, dr = col // 2048, lax.rem(col // 1024, 2), lax.rem(col // 512, 2), lax.rem(col // 256, 2)
    b = lax.rem(col // 64, 4) - dq
    c = lax.rem(col // 16, 4) - dr
    a = lax.rem(lax.rem(col // 4, 4) + 1 + 2 * half, 4) - dp
    inside = (a >= 0) & (a < 3) & (b >= 0) & (b < 3) & (c >= 0) & (c < 3)
    wanted = jnp.where(inside, (a * 9 + b * 3 + c) * 4 + lax.rem(col, 4), -1)
    place = one_hot(iota((108, 4096), 0) == wanted)
    w1 = mm_tn(f1_ref[...], place).astype(BF16)
    for k in range(16):
        w1_ref[k * 32 : (k + 1) * 32, :] = w1[:, k * LANES : (k + 1) * LANES]

    row, col = iota((96, 256), 0), iota((96, 256), 1)
    place = one_hot((lax.rem(row, 32) == lax.rem(col, 32)) & (lax.rem(col // 32, 4) == row // 32 + col // 128))
    for a in range(3):
        for b in range(3):
            at = (a * 9 + b * 3) * 32
            both = mm_tn(f2_ref[at : at + 96, :], place).astype(BF16)
            for fq in range(2):
                lane = a * 512 + (b + fq) * 128
                w2_ref[fq * 128 : fq * 128 + 64, lane : lane + 128] = both[:, 0:128]
                w2_ref[fq * 128 + 64 : fq * 128 + 128, lane : lane + 128] = both[:, 128:256]
        for fq in range(2):
            lane = a * 512 + (0 if fq else 3) * 128
            w2_ref[fq * 128 : fq * 128 + 128, lane : lane + 128] = jnp.zeros((128, 128), BF16)

    none = jnp.zeros((32, 64), BF16)
    for a in range(3):
        for b in range(3):
            at = ((2 - a) * 9 + (2 - b) * 3) * 32
            taps = [f2_ref[at + 32 * k : at + 32 * k + 32, :] for k in (2, 1, 0)]
            for er in range(2):
                block = jnp.concatenate([none] + taps if er else taps + [none], axis=1)
                for eq in range(2):
                    lane = a * 1024 + (b + eq) * 256
                    at_row = (eq * 2 + er) * 32
                    wb_ref[at_row : at_row + 32, lane : lane + 256] = block
        for eq in range(2):
            lane = a * 1024 + (0 if eq else 3) * 256
            wb_ref[eq * 64 : eq * 64 + 64, lane : lane + 256] = jnp.zeros((64, 256), BF16)

    k, lane = iota((LANES, LANES), 0), iota((LANES, LANES), 1)
    sh_ref[0] = one_hot(k == lane - 16)
    sh_ref[1] = one_hot(k == lane + 16)
    sh_ref[2] = one_hot((k == lane - 1) & (lax.rem(lane, 16) != 0))
    sh_ref[3] = one_hot((k == lane + 1) & (lax.rem(lane, 16) != 15))


def near_half():
    return 1 - lax.rem(lax.axis_index("space"), 2)


def plane_rows(half):
    plane = 3 - 3 * half
    return one_hot(lax.rem(iota((256, LANES), 0) // 4, 4) == plane)


def merge(block, other, rows):
    return block * (1 - rows) + other * rows


def spread(count, mg, xt, sh_ref):
    for k in range(count):
        for qq in range(4):
            at = ((qq + 1) * 6 + 1) * 16
            xt[k, at : at + 64, :] = mg[k, qq * 64 : qq * 64 + 64, :]
    up = mm(mg[:, 192:256, :].reshape(count * 64, LANES), sh_ref[0]).astype(BF16)
    down = mm(mg[:, 0:64, :].reshape(count * 64, LANES), sh_ref[1]).astype(BF16)
    for k in range(count):
        xt[k, 16:80, :] = up[k * 64 : k * 64 + 64]
        xt[k, 496:560, :] = down[k * 64 : k * 64 + 64]
    cells = [(k, q) for k in range(count) for q in range(6)]
    last = jnp.concatenate([xt[k, (q * 6 + 4) * 16 : (q * 6 + 5) * 16, :] for k, q in cells], axis=0)
    first = jnp.concatenate([xt[k, (q * 6 + 1) * 16 : (q * 6 + 2) * 16, :] for k, q in cells], axis=0)
    up = mm(last, sh_ref[2]).astype(BF16)
    down = mm(first, sh_ref[3]).astype(BF16)
    for n, (k, q) in enumerate(cells):
        xt[k, q * 96 : q * 96 + 16, :] = up[n * 16 : n * 16 + 16]
        xt[k, q * 96 + 80 : q * 96 + 96, :] = down[n * 16 : n * 16 + 16]


def patch(xt, k, eq, er):
    parts = []
    for b in range(4):
        at = ((2 * eq + b) * 6 + 2 * er) * 16
        parts.append(xt[k, at : at + 64, :])
    return jnp.concatenate(parts, axis=0)


def first_maps(xt, k, half, w1_ref, put, z_ref=None, scale=0.125):
    weights = w1_ref[pl.ds(pl.multiple_of(half * 256, 256), 256), :]
    for eq in range(2):
        for er in range(2):
            z = mm(weights, patch(xt, k, eq, er))
            if z_ref is not None:
                z_ref[eq * 2 + er] = z
            act = jnp.where(z > 0, z, 0.3 * z)
            total = act[0:32]
            for d in range(1, 8):
                total = total + act[d * 32 : d * 32 + 32]
            put((eq * 2 + er) * 32, (total * scale).astype(BF16))


def near_kernel(own_ref, near_ref, f1_ref, f2_ref,
                w1_ref, w2_ref, wb_ref, sh_ref, xt_ref, z_ref, maps_ref, mg, xt):
    matrices(f1_ref, f2_ref, w1_ref, w2_ref, wb_ref, sh_ref)
    half = near_half()
    own, near = own_ref[0:256, :], near_ref[0:256, :]
    mg[0] = merge(own, near, plane_rows(half))
    mg[1] = merge(near, own, plane_rows(1 - half))
    spread(2, mg, xt, sh_ref)
    xt_ref[...] = xt[0]

    def put(k):
        def store(at, rows):
            maps_ref[k, at : at + 32, :] = rows
        return store

    first_maps(xt, 0, half, w1_ref, put(0), z_ref)
    first_maps(xt, 1, 1 - half, w1_ref, put(1))


def far_kernel(own_ref, far_ref, w1_ref, sh_ref, xt_ref, z_ref, maps_ref, mg, xt):
    index = lax.axis_index("space")
    half = 1 - near_half()
    own, far = own_ref[0:256, :], far_ref[0:256, :]
    rows = plane_rows(half)
    n, m = iota((256, 64), 0), iota((256, 64), 1)
    same = (n // 16 == m // 4) & (lax.rem(n, 4) == lax.rem(m, 4)) & (lax.rem(n // 4, 4) == 3 - 3 * half)
    beyond = mm(one_hot(same), far_ref[320:384, :]).astype(BF16)
    mg[0] = merge(own, far, rows)
    mg[1] = merge(far, own, plane_rows(1 - half))
    mg[2] = merge(far, beyond, rows)
    spread(3, mg, xt, sh_ref)
    xt_ref[...] = xt[0]
    end = jnp.where(half == 0, index == 0, index == lax.axis_size("space") - 1)
    scale = jnp.where(end, 0.0, 0.125)

    def put(k):
        def store(at, rows):
            maps_ref[k, at : at + 32, :] = rows
        return store

    first_maps(xt, 0, half, w1_ref, put(0), z_ref)
    first_maps(xt, 1, 1 - half, w1_ref, put(1), scale=scale)
    first_maps(xt, 2, half, w1_ref, put(2), scale=scale)


def extend(ref, planes, size, sh_ref):
    for source, target, matrix in ((2, 0, 0), (1, 3, 1)):
        at, to = (source * 4 + 1) * size, (target * 4 + 1) * size
        block = ref[:, at : at + 2 * size, :].reshape(planes * 2 * size, LANES)
        moved = mm(block, sh_ref[matrix]).astype(BF16)
        ref[:, to : to + 2 * size, :] = moved.reshape(planes, 2 * size, LANES)
    cells = [(k, q) for k in range(planes) for q in range(4)]
    for source, target, matrix in ((2, 0, 2), (1, 3, 3)):
        block = jnp.concatenate(
            [ref[k, (q * 4 + source) * size : (q * 4 + source + 1) * size, :] for k, q in cells], axis=0
        )
        moved = mm(block, sh_ref[matrix]).astype(BF16)
        for n, (k, q) in enumerate(cells):
            ref[k, (q * 4 + target) * size : (q * 4 + target + 1) * size, :] = moved[n * size : (n + 1) * size]


def rest_kernel(own_ref, near_ref, far_ref, fwd_ref, w1_ref, w2_ref, wb_ref, sh_ref,
                xt_near, z_near, maps_near, xt_far, z_far, maps_far,
                feat_ref, keep_ref, send_ref,
                mg, xt, a_ext, g_ext, cells, taps, pack):
    half = near_half()
    parity = 1 - half

    mg[0] = merge(near_ref[0:256, :], fwd_ref[...], plane_rows(half))
    spread(1, mg, xt, sh_ref)

    def place(k):
        def store(at, rows):
            to = ((at // 64 + 1) * 4 + 1) * 32 + at % 64
            a_ext[k, to : to + rows.shape[0], :] = rows
        return store

    def order(k):
        return jnp.where(half == 1, k, 5 - k)

    first_maps(xt, 0, half, w1_ref, place(order(5)))
    for k, plane in ((3, maps_near[0]), (4, maps_near[1]), (2, maps_far[0]), (1, maps_far[1]), (0, maps_far[2])):
        for eq in range(2):
            place(order(k))(eq * 64, plane[eq * 64 : eq * 64 + 64])
    extend(a_ext, 6, 32, sh_ref)

    feats = jnp.zeros((64, LANES), F32)
    near_cot, far_cot = near_ref[256:320, :].astype(F32), far_ref[256:320, :].astype(F32)
    own_cot = own_ref[256:320, :].astype(F32)
    pick = jnp.where(half == 1, 1.0, 0.0)
    left_cot = far_cot * pick + near_cot * (1.0 - pick)
    right_cot = near_cot * pick + far_cot * (1.0 - pick)
    for t, cot in enumerate((left_cot, own_cot, own_cot, right_cot)):
        z = mm(w2_ref[...], a_ext[t : t + 3].reshape(1536, LANES))
        full, low = cot * 0.125, 0.3 * cot * 0.125
        for f in range(4):
            zf = z[f * 64 : f * 64 + 64]
            if t in (1, 2):
                feats = feats + jnp.where(zf > 0, zf, 0.3 * zf)
            at = ((f // 2 + 1) * 4 + f % 2 + 1) * 64
            g_ext[t, at : at + 64, :] = jnp.where(zf > 0, full, low).astype(BF16)
    feat_ref[...] = (feats * 0.125).astype(BF16)

    for a in range(3):
        acc = jnp.zeros((384, 128), F32)
        for t in range(2):
            for fq in range(2):
                maps = a_ext[t + 1 + a, fq * 128 : fq * 128 + 384, :]
                at = ((fq + 1) * 4 + 1) * 64
                acc = acc + mm_nt(maps, g_ext[t + 1, at : at + 128, :])
        for b in range(3):
            block = acc[b * 128 : b * 128 + 128]
            swapped = pltpu.roll(block, 64, 1)
            for h in range(2):
                chunk = (a * 3 + b) * 2 + h
                lo = h * 48
                if chunk < 9:
                    value = block[lo : lo + 48] + swapped[lo + 32 : lo + 80]
                    pack[chunk * 48 : chunk * 48 + 48, 0:64] = value[:, 0:64]
                else:
                    value = swapped[lo : lo + 48] + block[lo + 32 : lo + 80]
                    pack[(chunk - 9) * 48 : (chunk - 8) * 48, 64:128] = value[:, 64:128]

    extend(g_ext, 4, 64, sh_ref)

    for which, x_ref, z_ref in ((half, xt_near, z_near), (1 - half, xt_far, z_far)):
        back = mm(wb_ref[...], g_ext[pl.ds(which, 3)].reshape(3072, LANES))
        acc = jnp.zeros((256, 256), F32)
        for eq in range(2):
            for er in range(2):
                part = back[(eq * 2 + er) * 32 : (eq * 2 + er) * 32 + 32]
                full, low = part * 0.125, 0.3 * part * 0.125
                z = z_ref[eq * 2 + er].reshape(8, 32, LANES)
                grad = jnp.where(z > 0, full[None], low[None]).astype(BF16).reshape(256, LANES)
                crop = jnp.concatenate(
                    [x_ref[((2 * eq + b) * 6 + 2 * er) * 16 : ((2 * eq + b) * 6 + 2 * er + 4) * 16, :] for b in range(4)],
                    axis=0,
                )
                acc = acc + mm_nt(crop, grad)
        cells[which] = acc
    first, second = cells[0].reshape(16, 16, 256), cells[1].reshape(16, 16, 256)
    first = first + jnp.concatenate([second[:, 8:], second[:, :8]], axis=1)
    taps[0:256, :] = jnp.concatenate([first[:, 12:], first[:, :12]], axis=1).reshape(256, 256)
    taps[256:288, :] = jnp.zeros((32, 256), F32)
    total = jnp.zeros((192, 32), F32)
    for d in range(8):
        off = (d // 2 % 2) * 64 + (d % 2) * 16 + (d // 4) * 4
        total = total + taps[off : off + 192, d * 32 : d * 32 + 32]
    pack[432:480, :] = jnp.concatenate([total[k * 48 : k * 48 + 48] for k in range(4)], axis=1)

    keep_ref[...] = pack[pl.ds(pl.multiple_of(parity * 240, 8), 240), :]
    send_ref[...] = pack[pl.ds(pl.multiple_of(240 - parity * 240, 8), 240), :]


def features_kernel(feat_ref, out_ref):
    same = one_hot(iota((LANES, LANES), 0) == iota((LANES, LANES), 1))
    out_ref[...] = mm_nt(same, feat_ref[...]).astype(BF16)


def finish_kernel(mine_ref, other_ref, one_ref, two_ref, both):
    parity = lax.rem(lax.axis_index("space"), 2)
    both[pl.ds(pl.multiple_of(parity * 240, 8), 240), :] = mine_ref[...]
    both[pl.ds(pl.multiple_of(240 - parity * 240, 8), 240), :] = other_ref[...]
    two_ref[0:432, :] = both[0:432, 0:64]
    two_ref[432:864, :] = both[0:432, 64:128]
    for a in range(3):
        for b in range(3):
            for c in range(3):
                at = b * 64 + c * 16 + a * 4
                k, row = at // 48, at % 48
                one_ref[a * 9 + b * 3 + c] = both[432 + row : 436 + row, k * 32 : k * 32 + 32]


def call(kernel, outs, scratch=(), flops=0, size=0, **specs):
    return pl.pallas_call(
        kernel,
        **specs,
        out_shape=outs,
        out_specs=jax.tree.map(lambda _: VMEM, outs),
        scratch_shapes=list(scratch),
        compiler_params=pltpu.CompilerParams(vmem_limit_bytes=16 * 1024 * 1024),
        cost_estimate=pl.CostEstimate(flops=flops, bytes_accessed=size, transcendentals=0),
    )


def shape(dims, dtype):
    return jax.ShapeDtypeStruct(dims, dtype)


def both_ways(pairs):
    return [(i, j) for i, j in pairs] + [(j, i) for i, j in pairs]


def total_over_mesh(keep, send, n_dp, n_space):
    axes = ("dp", "space")
    size = n_dp * n_space
    near = [(i, i ^ 1) for i in range(size)]
    mine = keep + lax.ppermute(send, axes, near)
    bits = [1 << k for k in range(1, 31) if 1 << k < size]
    bits = bits[-1:] + bits[:-1]
    groups = [bits[k : k + 2] for k in range(0, len(bits), 2)]
    middle = len(groups) // 2
    turned = groups[middle:] + groups[:middle]
    if [len(g) for g in groups] != [len(g) for g in turned]:
        turned = groups
    for even, odd in zip(groups, turned):
        masks = [even + [even[0] ^ even[-1]], odd + [odd[0] ^ odd[-1]]]
        count = 3 if len(even) == 2 else 1
        parts = [
            lax.ppermute(mine, axes, [(i, i ^ masks[i % 2][k]) for i in range(size)]) for k in range(count)
        ]
        mine = mine + parts[0]
        if count == 3:
            mine = mine + (parts[1] + parts[2])
    return mine, lax.ppermute(mine, axes, near)


def local(n_dp, n_space, crop, filter_one, filter_two, cotangent):
    near = [(i, i ^ 1) for i in range(n_space)]
    across = both_ways([(i, i + 1) for i in range(1, n_space - 1, 2)])
    with jax.named_scope("blocks"):
        own, edge = call(
            blocks_kernel,
            (shape((256, LANES), BF16), shape((64, LANES), BF16)),
            [pltpu.VMEM((512, LANES), F32)],
        )(crop)
        own, cot = lax.optimization_barrier((own, cotangent.transpose(0, 2, 3, 4, 1).reshape(LANES, 64)))
        cot = cot.T
    with jax.named_scope("halo"):
        beyond = lax.ppermute(jnp.concatenate([own, cot, lax.ppermute(edge, "space", near)], axis=0), "space", across)
        own = jnp.concatenate([own, cot], axis=0)
        beside = lax.ppermute(own, "space", near)
    with jax.named_scope("near"):
        w1, w2, wb, shifts, xt_near, z_near, maps_near = call(
            near_kernel,
            (
                shape((512, 256), BF16),
                shape((256, 1536), BF16),
                shape((128, 3072), BF16),
                shape((4, LANES, LANES), BF16),
                shape((576, LANES), BF16),
                shape((4, 256, LANES), F32),
                shape((2, 128, LANES), BF16),
            ),
            [pltpu.VMEM((2, 256, LANES), BF16), pltpu.VMEM((2, 576, LANES), BF16)],
            flops=1_000_000_000,
            size=4_000_000,
        )(own, beside, filter_one.reshape(108, 32), filter_two.reshape(864, 64))
    beyond, xt_near = lax.optimization_barrier((beyond, xt_near))
    with jax.named_scope("far"):
        forward = lax.ppermute(beyond[:256], "space", near)
        xt_far, z_far, maps_far = call(
            far_kernel,
            (shape((576, LANES), BF16), shape((4, 256, LANES), F32), shape((3, 128, LANES), BF16)),
            [pltpu.VMEM((3, 256, LANES), BF16), pltpu.VMEM((3, 576, LANES), BF16)],
            flops=1_000_000_000,
            size=3_000_000,
        )(own, beyond, w1, shifts)
    with jax.named_scope("rest"):
        feats, keep, send = call(
            rest_kernel,
            (shape((64, LANES), BF16), shape((240, 128), F32), shape((240, 128), F32)),
            [
                pltpu.VMEM((1, 256, LANES), BF16),
                pltpu.VMEM((1, 576, LANES), BF16),
                pltpu.VMEM((6, 512, LANES), BF16),
                pltpu.VMEM((4, 1024, LANES), BF16),
                pltpu.VMEM((2, 256, 256), F32),
                pltpu.VMEM((288, 256), F32),
                pltpu.VMEM((480, 128), F32),
            ],
            flops=4_000_000_000,
            size=6_000_000,
        )(own, beside, beyond, forward, w1, w2, wb, shifts, xt_near, z_near, maps_near, xt_far, z_far, maps_far)
    with jax.named_scope("total"):
        mine, other = total_over_mesh(keep, send, n_dp, n_space)
        one, two = call(
            finish_kernel,
            (shape((27, 4, 32), F32), shape((864, 64), F32)),
            [pltpu.VMEM((480, 128), F32)],
        )(mine, other)
        feats = call(features_kernel, shape((LANES, 64), BF16), flops=10_000_000, size=1_000_000)(feats)
    features = feats.reshape(1, 1, 16, 16, 64).transpose(0, 4, 1, 2, 3)
    return features, one.reshape(3, 3, 3, 4, 32), two.reshape(3, 3, 3, 32, 64)


def solution(mesh):
    n_dp, n_space = mesh.shape["dp"], mesh.shape["space"]
    assert n_space % 2 == 0 and (n_dp * n_space) & (n_dp * n_space - 1) == 0, "mesh sizes"
    placed = (P("dp", None, "space", None, None), P(), P(), P("dp", None, "space", None, None))
    return jax.shard_map(
        functools.partial(local, n_dp, n_space),
        mesh=mesh,
        in_specs=placed,
        out_specs=(P("dp", None, "space", None, None), P(), P()),
        check_vma=False,
    )
```

time: 49.6 us -> 42.5 us (0.86)
  starting transfers between devices: 22.3 us -> 18.4 us
  waiting for transfers between devices: 15.9 us -> 12 us
  Pallas kernels: 8.51 us -> 9.95 us
  local copies, waits for them, and re-layouts: 1.92 us -> 1.08 us
    ppermute x6 -> x9, starting transfers between devices: 21.3 us -> 17.8 us  [the longest x6 8.97 us: total_over_mesh(): lax.ppermute(mine, axes, [(i, i ^ masks[i % 2][k]) for i in range(size)])]
    ppermute x6 -> x9, waiting for transfers between devices: 13.2 us -> 10.5 us  [the longest x6 9.84 us: total_over_mesh(): lax.ppermute(mine, axes, [(i, i ^ masks[i % 2][k]) for i in range(size)])]
    pallas_call x3 -> x5, Pallas kernels: 7.59 us -> 9.03 us  [the longest x1 5.11 us: local(): call(rest_kernel, (shape((64, LANES), BF16), shape((240, 128), F32), shap...]
    ppermute x1, waiting for transfers between devices: 1.1 us -> 0.01 us  [local(): beside = lax.ppermute(own, 'space', near)]
    pallas_call x1 -> x0, local copies, waits for them, and re-layouts: 0.73 us -> none  [local(): call(main_kernel, (shape((64, LANES), BF16), shape((240, 128), F32), shap...]
    unnamed x7 -> x8, local copies, waits for them, and re-layouts: 1.14 us -> 0.96 us
  transfers between devices with their start and end apart: 9 -> 12, of which waited for: 8 -> 8; matrix products, arithmetic and copies ran while one was open for 2% -> 0% of each run, Pallas kernels for 2% -> 7%
where the time goes in v1:
time: 42.5 us; the launch traced here: 42.3 us
  starting transfers between devices  18.4 us (43%)
  waiting for transfers between devices  12 us (28%)
  Pallas kernels  9.95 us (23%)
  local copies, waits for them, and re-layouts  1.08 us (3%)
  between operations  0.77 us (2%)
    ppermute x6, waiting for transfers between devices, total_over_mesh(): lax.ppermute(mine, axes, [(i, i ^ masks[i % 2][k]) for i in range(size)])  9.84 us
    ppermute x6, starting transfers between devices, total_over_mesh(): lax.ppermute(mine, axes, [(i, i ^ masks[i % 2][k]) for i in range(size)])  8.97 us
    ppermute x1, starting transfers between devices, local(): forward = lax.ppermute(beyond[:256], 'space', near)  7.61 us
    pallas_call x1, Pallas kernels, local(): call(rest_kernel, (shape((64, LANES), BF16), shape((240, 128), F32), shap...  5.11 us
    pallas_call x1, Pallas kernels, local(): call(near_kernel, (shape((512, 256), BF16), shape((256, 1536), BF16), sha...  1.28 us
    ppermute x1, waiting for transfers between devices, total_over_mesh(): mine = keep + lax.ppermute(send, axes, near)  0.98 us
    unnamed x8, local copies, waits for them, and re-layouts  0.96 us
    pallas_call x1, Pallas kernels, local(): call(blocks_kernel, (shape((256, LANES), BF16), shape((64, LANES), BF16))...  0.94 us
  transfers between devices with their start and end apart: 12, of which 8 were waited for; matrix products, arithmetic and copies ran while one was open for 0% of the time, Pallas kernels for 7%

profile of v1, /device:TPU:0, one launch (start us, length us, event | category | flops | bytes accessed | tf_op | source)
XLA Modules:
  0.0 42.3 jit_solution(7139351633688316624)
XLA Ops:
  0.6 0.0 copy-start
  0.6 0.9 %copy-done = bf16[1,4,4,64,64]{4,3,2,1,0:T(8,128)(2,1)S(1)} copy-done((bf16[1,4,4,64,64]{4,3,2,1,0:T(8,128)(2,1)S(1)}, bf16[1,4,4,64,64]{4,3,2,1,0:T(8,128)(2,1)}, u32[]{:S(2)}) %copy-start) | copy-done | bytes 131096
  1.6 0.0 copy-start.2
  1.6 0.9 %blocks.1 = (bf16[256,256]{1,0:T(8,128)(2,1)S(1)}, bf16[64,256]{1,0:T(8,128)(2,1)S(1)}) custom-call(bf16[1,4,4,64,64]{4,3,2,1,0:T(8,128)(2,1)S(1)} %copy-done), custom_call_target="tpu_custom_call" | custom-call | tf_op jit(solution)/shard_map/blocks/pallas_call | solution.py:397
  2.5 0.5 %collective-permute-start.1 = (bf16[64,256]{1,0:T(8,128)(2,1)S(1)}, bf16[64,256]{1,0:T(8,128)(2,1)S(1)}, u32[]{:S(2)}, u32[]{:S(2)}) collective-permute-start(bf16[64,256]{1,0:T(8,128)(2,1)S(1)} %get-tuple-element.27), channel_id=1, source_target_pairs={{0,1},{1,0},{2,3},{3,2},{4,5},{5,4},{6,7},{7,6},{8,9},{9,8},{10,11... | collective-permute-start | bytes 98312 | tf_op jit(solution)/shard_map/halo/ppermute | solution.py:405
  3.0 0.0 copy-done.2
  3.1 0.1 copy.8
  3.2 0.0 copy-start.3
  3.2 0.0 copy-start.1
  3.2 0.1 collective-permute-start
  3.3 0.6 %collective-permute-done.1 = bf16[64,256]{1,0:T(8,128)(2,1)S(1)} collective-permute-done((bf16[64,256]{1,0:T(8,128)(2,1)S(1)}, bf16[64,256]{1,0:T(8,128)(2,1)S(1)}, u32[]{:S(2)}, u32[]{:S(2)}) %collective-permute-start.1) | collective-permute-done | bytes 32800 | tf_op jit(solution)/shard_map/halo/ppermute | solution.py:405
  3.9 0.7 %collective-permute-start.2 = (bf16[384,256]{1,0:T(8,128)(2,1)S(1)}, bf16[384,256]{1,0:T(8,128)(2,1)S(1)}, u32[]{:S(2)}, u32[]{:S(2)}) collective-permute-start(bf16[384,256]{1,0:T(8,128)(2,1)S(1)} %pad_maximum_fusion), channel_id=1, source_target_pairs={{1,2},{3,4},{5,6},{7,8},{9,10},{11,12},{13,14},{2,1},{4,3},{6,5},{... | collective-permute-start | bytes 589832 | tf_op jit(solution)/shard_map/halo/ppermute | solution.py:405
  4.6 0.0 copy-done.3
  4.6 0.0 collective-permute-done.near_ref
  4.7 0.0 copy-done.1
  4.7 1.3 %near.1 = (bf16[512,256]{1,0:T(8,128)(2,1)S(1)}, bf16[256,1536]{1,0:T(8,128)(2,1)S(1)}, bf16[128,3072]{1,0:T(8,128)(2,1)S(1)}, bf16[4,256,256]{2,1,0:T(8,128)(2,...) custom-call(bf16[320,256]{1,0:T(8,128)(2,1)S(1)} %pad_maximum_fusion.1.own_ref, ...), custom_call_target="tpu_custom_call" | custom-call | flops 1000000000 | bytes 4000000 | tf_op jit(solution)/shard_map/near/pallas_call | solution.py:409
  6.0 0.0 collective-permute-done.2.far_ref
  6.0 7.6 %collective-permute-start.3 = (bf16[256,256]{1,0:T(8,128)(2,1)S(1)}, bf16[256,256]{1,0:T(8,128)(2,1)S(1)}, u32[]{:S(2)}, u32[]{:S(2)}) collective-permute-start(bf16[256,256]{1,0:T(8,128)(2,1)S(1)} %slice.3), channel_id=1, source_target_pairs={{0,1},{1,0},{2,3},{3,2},{4,5},{5,4},{6,7},{7,6},{8,9},{9,8},{10,11... | collective-permute-start | bytes 393224 | tf_op jit(solution)/shard_map/far/ppermute | solution.py:426
  13.6 0.9 %far.1 = (bf16[576,256]{1,0:T(8,128)(2,1)S(1)}, f32[4,256,256]{2,1,0:T(8,128)S(1)}, bf16[3,128,256]{2,1,0:T(8,128)(2,1)S(1)}) custom-call(bf16[320,256]{1,0:T(8,128)(2,1)S(1)} %pad_maximum_fusion.1.own_ref, bf16[384,256]{1,0:T(8,128)(2,1)S(1)} %collective-permute-done.2.far_ref, bf16[512,256]{1,0:T(8,128)(2,1)S(1)} %get-tuple-element.30.w1_ref, ...), custom_call_target="tpu_custom_call" | custom-call | flops 1000000000 | bytes 3000000 | tf_op jit(solution)/shard_map/far/pallas_call | solution.py:427
  14.5 0.1 collective-permute-done.3.fwd_ref
  14.6 5.1 %rest.1 = (bf16[64,256]{1,0:T(8,128)(2,1)S(1)}, f32[240,128]{1,0:T(8,128)S(1)}, f32[240,128]{1,0:T(8,128)S(1)}) custom-call(bf16[320,256]{1,0:T(8,128)(2,1)S(1)} %pad_maximum_fusion.1.own_ref, bf16[320,256]{1,0:T(8,128)(2,1)S(1)} %collective-permute-done.near_ref, bf16[384,256]{1,0:T(8,128)(2,1)S(1)} %collective-permute-done.2.far_ref, ...), custom_call_target="tpu_custom_call" | custom-call | flops 4000000000 | bytes 6000000 | tf_op jit(solution)/shard_map/rest/pallas_call | solution.py:435
  19.7 0.4 %collective-permute-start.4 = (f32[240,128]{1,0:T(8,128)S(1)}, f32[240,128]{1,0:T(8,128)S(1)}, u32[]{:S(2)}, u32[]{:S(2)}) collective-permute-start(f32[240,128]{1,0:T(8,128)S(1)} %get-tuple-element.42), channel_id=1, source_target_pairs={{0,1},{1,0},{2,3},{3,2},{4,5},{5,4},{6,7},{7,6},{8,9},{9,8},{10,11... | collective-permute-start | bytes 368648 | tf_op jit(solution)/shard_map/total/ppermute | solution.py:373
  20.1 1.0 %collective-permute-done.4 = f32[240,128]{1,0:T(8,128)S(1)} collective-permute-done((f32[240,128]{1,0:T(8,128)S(1)}, f32[240,128]{1,0:T(8,128)S(1)}, u32[]{:S(2)}, u32[]{:S(2)}) %collective-permute-start.4) | collective-permute-done | bytes 122912 | tf_op jit(solution)/shard_map/total/ppermute | solution.py:373
  21.1 3.7 %collective-permute-start.7 = (f32[240,128]{1,0:T(8,128)S(1)}, f32[240,128]{1,0:T(8,128)S(1)}, u32[]{:S(2)}, u32[]{:S(2)}) collective-permute-start(f32[240,128]{1,0:T(8,128)S(1)} %add.21), channel_id=1, source_target_pairs={{0,18},{1,13},{2,16},{3,15},{4,22},{5,9},{6,20},{7,11},{8,26},{9,5... | collective-permute-start | bytes 368648 | tf_op jit(solution)/shard_map/total/ppermute | solution.py:385
  24.8 0.0 collective-permute-start.6
  24.8 0.6 %collective-permute-start.5 = (f32[240,128]{1,0:T(8,128)S(1)}, f32[240,128]{1,0:T(8,128)S(1)}, u32[]{:S(2)}, u32[]{:S(2)}) collective-permute-start(f32[240,128]{1,0:T(8,128)S(1)} %add.21), channel_id=1, source_target_pairs={{0,16},{1,5},{2,18},{3,7},{4,20},{5,1},{6,22},{7,3},{8,24},{9,13},... | collective-permute-start | bytes 368648 | tf_op jit(solution)/shard_map/total/ppermute | solution.py:385
  25.5 2.2 %collective-permute-done.7 = f32[240,128]{1,0:T(8,128)S(1)} collective-permute-done((f32[240,128]{1,0:T(8,128)S(1)}, f32[240,128]{1,0:T(8,128)S(1)}, u32[]{:S(2)}, u32[]{:S(2)}) %collective-permute-start.7) | collective-permute-done | bytes 122912 | tf_op jit(solution)/shard_map/total/ppermute | solution.py:385
  27.7 2.0 %collective-permute-done.6 = f32[240,128]{1,0:T(8,128)S(1)} collective-permute-done((f32[240,128]{1,0:T(8,128)S(1)}, f32[240,128]{1,0:T(8,128)S(1)}, u32[]{:S(2)}, u32[]{:S(2)}) %collective-permute-start.6) | collective-permute-done | bytes 122912 | tf_op jit(solution)/shard_map/total/ppermute | solution.py:385
  29.7 0.0 collective-permute-done.5
  29.8 4.0 %collective-permute-start.10 = (f32[240,128]{1,0:T(8,128)S(1)}, f32[240,128]{1,0:T(8,128)S(1)}, u32[]{:S(2)}, u32[]{:S(2)}) collective-permute-start(f32[240,128]{1,0:T(8,128)S(1)} %add_add_fusion.1), channel_id=1, source_target_pairs={{0,12},{1,19},{2,14},{3,17},{4,8},{5,23},{6,10},{7,21},{8,4},{9,27... | collective-permute-start | bytes 368648 | tf_op jit(solution)/shard_map/total/ppermute | solution.py:385
  33.7 0.0 collective-permute-start.9
  33.7 0.6 %collective-permute-start.8 = (f32[240,128]{1,0:T(8,128)S(1)}, f32[240,128]{1,0:T(8,128)S(1)}, u32[]{:S(2)}, u32[]{:S(2)}) collective-permute-start(f32[240,128]{1,0:T(8,128)S(1)} %add_add_fusion.1), channel_id=1, source_target_pairs={{0,4},{1,17},{2,6},{3,19},{4,0},{5,21},{6,2},{7,23},{8,12},{9,25},... | collective-permute-start | bytes 368648 | tf_op jit(solution)/shard_map/total/ppermute | solution.py:385
  34.4 2.3 %collective-permute-done.10 = f32[240,128]{1,0:T(8,128)S(1)} collective-permute-done((f32[240,128]{1,0:T(8,128)S(1)}, f32[240,128]{1,0:T(8,128)S(1)}, u32[]{:S(2)}, u32[]{:S(2)}) %collective-permute-start.10) | collective-permute-done | bytes 122912 | tf_op jit(solution)/shard_map/total/ppermute | solution.py:385
  36.7 3.3 %collective-permute-done.9 = f32[240,128]{1,0:T(8,128)S(1)} collective-permute-done((f32[240,128]{1,0:T(8,128)S(1)}, f32[240,128]{1,0:T(8,128)S(1)}, u32[]{:S(2)}, u32[]{:S(2)}) %collective-permute-start.9) | collective-permute-done | bytes 122912 | tf_op jit(solution)/shard_map/total/ppermute | solution.py:385
  40.0 0.0 collective-permute-done.8
  40.0 0.1 collective-permute-start.11
  40.1 0.8 %total.2 = bf16[256,64]{1,0:T(8,128)(2,1)} custom-call(bf16[64,256]{1,0:T(8,128)(2,1)S(1)} %get-tuple-element.40.feat_ref), custom_call_target="tpu_custom_call" | custom-call | flops 10000000 | bytes 1000000 | tf_op jit(solution)/shard_map/total/pallas_call | solution.py:457
  40.9 0.5 %collective-permute-done.11.other_ref = f32[240,128]{1,0:T(8,128)S(1)} collective-permute-done((f32[240,128]{1,0:T(8,128)S(1)}, f32[240,128]{1,0:T(8,128)S(1)}, u32[]{:S(2)}, u32[]{:S(2)}) %collective-permute-start.11) | collective-permute-done | bytes 122912 | tf_op jit(solution)/shard_map/total/ppermute | solution.py:390
  41.4 0.9 %total.3 = (f32[27,4,32]{2,1,0:T(4,128)}, f32[864,64]{1,0:T(8,128)}) custom-call(f32[240,128]{1,0:T(8,128)S(1)} %add_add_fusion.mine_ref, f32[240,128]{1,0:T(8,128)S(1)} %collective-permute-done.11.other_ref), custom_call_target="tpu_custom_call" | custom-call | tf_op jit(solution)/shard_map/total/pallas_call | solution.py:452
  (7 shorter events, 0.2 us)
Async XLA Ops:
  0.6 1.0 %copy-start = (bf16[1,4,4,64,64]{4,3,2,1,0:T(8,128)(2,1)S(1)}, bf16[1,4,4,64,64]{4,3,2,1,0:T(8,128)(2,1)}, u32[]{:S(2)}) copy-start(bf16[1,4,4,64,64]{4,3,2,1,0:T(8,128)(2,1)} %crop_ref.1) | copy-start | bytes 393220
  1.6 1.5 %copy-start.2 = (bf16[1,64,1,16,16]{1,4,3,2,0:T(8,128)(2,1)S(1)}, bf16[1,64,1,16,16]{1,4,3,2,0:T(8,128)(2,1)}, u32[]{:S(2)}) copy-start(bf16[1,64,1,16,16]{1,4,3,2,0:T(8,128)(2,1)} %param.7) | copy-start | bytes 98308
  2.5 1.4 %collective-permute-start.1 = (bf16[64,256]{1,0:T(8,128)(2,1)S(1)}, bf16[64,256]{1,0:T(8,128)(2,1)S(1)}, u32[]{:S(2)}, u32[]{:S(2)}) collective-permute-start(bf16[64,256]{1,0:T(8,128)(2,1)S(1)} %get-tuple-element.27), channel_id=1, source_target_pairs={{0,1},{1,0},{2,3},{3,2},{4,5},{5,4},{6,7},{7,6},{8,9},{9,8},{10,11... | collective-permute-start | bytes 98312 | tf_op jit(solution)/shard_map/halo/ppermute | solution.py:405
  3.2 1.4 %copy-start.3 = (bf16[3,3,3,4,32]{4,3,2,1,0:T(4,128)(2,1)S(1)}, bf16[3,3,3,4,32]{4,3,2,1,0:T(4,128)(2,1)}, u32[]{:S(2)}) copy-start(bf16[3,3,3,4,32]{4,3,2,1,0:T(4,128)(2,1)} %param.5) | copy-start | bytes 20740
  3.2 1.5 %copy-start.1 = (bf16[3,3,3,32,64]{4,3,2,1,0:T(8,128)(2,1)S(1)}, bf16[3,3,3,32,64]{4,3,2,1,0:T(8,128)(2,1)}, u32[]{:S(2)}) copy-start(bf16[3,3,3,32,64]{4,3,2,1,0:T(8,128)(2,1)} %param.6) | copy-start | bytes 331780
  3.2 1.5 %collective-permute-start = (bf16[320,256]{1,0:T(8,128)(2,1)S(1)}, bf16[320,256]{1,0:T(8,128)(2,1)S(1)}, u32[]{:S(2)}, u32[]{:S(2)}) collective-permute-start(bf16[320,256]{1,0:T(8,128)(2,1)S(1)} %pad_maximum_fusion.1.own_ref), channel_id=1, source_target_pairs={{0,1},{1,0},{2,3},{3,2},{4,5},{5,4},{6,7},{7,6},{8,9},{9,8},{10,11... | collective-permute-start | bytes 491528 | tf_op jit(solution)/shard_map/halo/ppermute | solution.py:407
  3.9 2.0 %collective-permute-start.2 = (bf16[384,256]{1,0:T(8,128)(2,1)S(1)}, bf16[384,256]{1,0:T(8,128)(2,1)S(1)}, u32[]{:S(2)}, u32[]{:S(2)}) collective-permute-start(bf16[384,256]{1,0:T(8,128)(2,1)S(1)} %pad_maximum_fusion), channel_id=1, source_target_pairs={{1,2},{3,4},{5,6},{7,8},{9,10},{11,12},{13,14},{2,1},{4,3},{6,5},{... | collective-permute-start | bytes 589832 | tf_op jit(solution)/shard_map/halo/ppermute | solution.py:405
  6.0 8.6 %collective-permute-start.3 = (bf16[256,256]{1,0:T(8,128)(2,1)S(1)}, bf16[256,256]{1,0:T(8,128)(2,1)S(1)}, u32[]{:S(2)}, u32[]{:S(2)}) collective-permute-start(bf16[256,256]{1,0:T(8,128)(2,1)S(1)} %slice.3), channel_id=1, source_target_pairs={{0,1},{1,0},{2,3},{3,2},{4,5},{5,4},{6,7},{7,6},{8,9},{9,8},{10,11... | collective-permute-start | bytes 393224 | tf_op jit(solution)/shard_map/far/ppermute | solution.py:426
  19.7 1.4 %collective-permute-start.4 = (f32[240,128]{1,0:T(8,128)S(1)}, f32[240,128]{1,0:T(8,128)S(1)}, u32[]{:S(2)}, u32[]{:S(2)}) collective-permute-start(f32[240,128]{1,0:T(8,128)S(1)} %get-tuple-element.42), channel_id=1, source_target_pairs={{0,1},{1,0},{2,3},{3,2},{4,5},{5,4},{6,7},{7,6},{8,9},{9,8},{10,11... | collective-permute-start | bytes 368648 | tf_op jit(solution)/shard_map/total/ppermute | solution.py:373
  21.1 6.6 %collective-permute-start.7 = (f32[240,128]{1,0:T(8,128)S(1)}, f32[240,128]{1,0:T(8,128)S(1)}, u32[]{:S(2)}, u32[]{:S(2)}) collective-permute-start(f32[240,128]{1,0:T(8,128)S(1)} %add.21), channel_id=1, source_target_pairs={{0,18},{1,13},{2,16},{3,15},{4,22},{5,9},{6,20},{7,11},{8,26},{9,5... | collective-permute-start | bytes 368648 | tf_op jit(solution)/shard_map/total/ppermute | solution.py:385
  24.8 4.9 %collective-permute-start.6 = (f32[240,128]{1,0:T(8,128)S(1)}, f32[240,128]{1,0:T(8,128)S(1)}, u32[]{:S(2)}, u32[]{:S(2)}) collective-permute-start(f32[240,128]{1,0:T(8,128)S(1)} %add.21), channel_id=1, source_target_pairs={{0,2},{1,9},{2,0},{3,11},{4,6},{5,13},{6,4},{7,15},{8,10},{9,1},{1... | collective-permute-start | bytes 368648 | tf_op jit(solution)/shard_map/total/ppermute | solution.py:385
  24.8 4.9 %collective-permute-start.5 = (f32[240,128]{1,0:T(8,128)S(1)}, f32[240,128]{1,0:T(8,128)S(1)}, u32[]{:S(2)}, u32[]{:S(2)}) collective-permute-start(f32[240,128]{1,0:T(8,128)S(1)} %add.21), channel_id=1, source_target_pairs={{0,16},{1,5},{2,18},{3,7},{4,20},{5,1},{6,22},{7,3},{8,24},{9,13},... | collective-permute-start | bytes 368648 | tf_op jit(solution)/shard_map/total/ppermute | solution.py:385
  29.8 6.9 %collective-permute-start.10 = (f32[240,128]{1,0:T(8,128)S(1)}, f32[240,128]{1,0:T(8,128)S(1)}, u32[]{:S(2)}, u32[]{:S(2)}) collective-permute-start(f32[240,128]{1,0:T(8,128)S(1)} %add_add_fusion.1), channel_id=1, source_target_pairs={{0,12},{1,19},{2,14},{3,17},{4,8},{5,23},{6,10},{7,21},{8,4},{9,27... | collective-permute-start | bytes 368648 | tf_op jit(solution)/shard_map/total/ppermute | solution.py:385
  33.7 6.2 %collective-permute-start.9 = (f32[240,128]{1,0:T(8,128)S(1)}, f32[240,128]{1,0:T(8,128)S(1)}, u32[]{:S(2)}, u32[]{:S(2)}) collective-permute-start(f32[240,128]{1,0:T(8,128)S(1)} %add_add_fusion.1), channel_id=1, source_target_pairs={{0,8},{1,3},{2,10},{3,1},{4,12},{5,7},{6,14},{7,5},{8,0},{9,11},{1... | collective-permute-start | bytes 368648 | tf_op jit(solution)/shard_map/total/ppermute | solution.py:385
  33.7 6.2 %collective-permute-start.8 = (f32[240,128]{1,0:T(8,128)S(1)}, f32[240,128]{1,0:T(8,128)S(1)}, u32[]{:S(2)}, u32[]{:S(2)}) collective-permute-start(f32[240,128]{1,0:T(8,128)S(1)} %add_add_fusion.1), channel_id=1, source_target_pairs={{0,4},{1,17},{2,6},{3,19},{4,0},{5,21},{6,2},{7,23},{8,12},{9,25},... | collective-permute-start | bytes 368648 | tf_op jit(solution)/shard_map/total/ppermute | solution.py:385
  40.0 1.4 %collective-permute-start.11 = (f32[240,128]{1,0:T(8,128)S(1)}, f32[240,128]{1,0:T(8,128)S(1)}, u32[]{:S(2)}, u32[]{:S(2)}) collective-permute-start(f32[240,128]{1,0:T(8,128)S(1)} %add_add_fusion.mine_ref), channel_id=1, source_target_pairs={{0,1},{1,0},{2,3},{3,2},{4,5},{5,4},{6,7},{7,6},{8,9},{9,8},{10,11... | collective-permute-start | bytes 368648 | tf_op jit(solution)/shard_map/total/ppermute | solution.py:390

commit v2 on v1

--- a/solution.py
+++ b/solution.py
@@ -103,13 +103,17 @@
             taps = [f2_ref[at + 32 * k : at + 32 * k + 32, :] for k in (2, 1, 0)]
             for er in range(2):
                 block = jnp.concatenate([none] + taps if er else taps + [none], axis=1)
-                for eq in range(2):
-                    lane = a * 1024 + (b + eq) * 256
-                    at_row = (eq * 2 + er) * 32
-                    wb_ref[at_row : at_row + 32, lane : lane + 256] = block
-        for eq in range(2):
-            lane = a * 1024 + (0 if eq else 3) * 256
-            wb_ref[eq * 64 : eq * 64 + 64, lane : lane + 256] = jnp.zeros((64, 256), BF16)
+                for s in range(2):
+                    for eq in range(2):
+                        lane = (a + s) * 1024 + (b + eq) * 256
+                        row = (s * 4 + eq * 2 + er) * 32
+                        wb_ref[row : row + 32, lane : lane + 256] = block
+        for s in range(2):
+            for eq in range(2):
+                lane = (a + s) * 1024 + (0 if eq else 3) * 256
+                wb_ref[s * 128 + eq * 64 : s * 128 + eq * 64 + 64, lane : lane + 256] = jnp.zeros((64, 256), BF16)
+    wb_ref[0:128, 3072:4096] = jnp.zeros((128, 1024), BF16)
+    wb_ref[128:256, 0:1024] = jnp.zeros((128, 1024), BF16)
 
     k, lane = iota((LANES, LANES), 0), iota((LANES, LANES), 1)
     sh_ref[0] = one_hot(k == lane - 16)
@@ -120,6 +124,14 @@
 
 def near_half():
     return 1 - lax.rem(lax.axis_index("space"), 2)
+
+
+def share():
+    index = lax.axis_index("dp") * lax.axis_size("space") + lax.axis_index("space")
+    bits = 0
+    for k in range((lax.axis_size("dp") * lax.axis_size("space")).bit_length()):
+        bits = bits + lax.rem(index // (1 << k), 2)
+    return lax.rem(bits, 2)
 
 
 def plane_rows(half):
@@ -195,18 +207,19 @@
 def far_kernel(own_ref, far_ref, w1_ref, sh_ref, xt_ref, z_ref, maps_ref, mg, xt):
     index = lax.axis_index("space")
     half = 1 - near_half()
-    own, far = own_ref[0:256, :], far_ref[0:256, :]
+    end = jnp.where(half == 0, index == 0, index == lax.axis_size("space") - 1)
+    inside = jnp.where(end, 0.0, 1.0)
+    own, far = own_ref[0:256, :], far_ref[0:256, :] * inside.astype(BF16)
     rows = plane_rows(half)
     n, m = iota((256, 64), 0), iota((256, 64), 1)
     same = (n // 16 == m // 4) & (lax.rem(n, 4) == lax.rem(m, 4)) & (lax.rem(n // 4, 4) == 3 - 3 * half)
-    beyond = mm(one_hot(same), far_ref[320:384, :]).astype(BF16)
+    beyond = (mm(one_hot(same), far_ref[320:384, :]) * inside).astype(BF16)
     mg[0] = merge(own, far, rows)
     mg[1] = merge(far, own, plane_rows(1 - half))
     mg[2] = merge(far, beyond, rows)
     spread(3, mg, xt, sh_ref)
     xt_ref[...] = xt[0]
-    end = jnp.where(half == 0, index == 0, index == lax.axis_size("space") - 1)
-    scale = jnp.where(end, 0.0, 0.125)
+    scale = inside * 0.125
 
     def put(k):
         def store(at, rows):
@@ -234,14 +247,15 @@
             ref[k, (q * 4 + target) * size : (q * 4 + target + 1) * size, :] = moved[n * size : (n + 1) * size]
 
 
-def rest_kernel(own_ref, near_ref, far_ref, fwd_ref, w1_ref, w2_ref, wb_ref, sh_ref,
-                xt_near, z_near, maps_near, xt_far, z_far, maps_far,
-                feat_ref, keep_ref, send_ref,
-                mg, xt, a_ext, g_ext, cells, taps, pack):
+def second_kernel(own_ref, near_ref, far_ref, fwd_ref, w1_ref, w2_ref, sh_ref, maps_near, maps_far,
+                  feat_ref, keep_ref, send_ref, g_ext,
+                  mg, xt, a_ext, pack):
     half = near_half()
-    parity = 1 - half
-
-    mg[0] = merge(near_ref[0:256, :], fwd_ref[...], plane_rows(half))
+    index, last = lax.axis_index("space"), lax.axis_size("space") - 1
+    has_far = jnp.where((index == 0) | (index == last), 0.0, 1.0)
+    near_has_far = jnp.where((index == 1) | (index == last - 1), 0.0, 1.0)
+
+    mg[0] = merge(near_ref[0:256, :], fwd_ref[...] * near_has_far.astype(BF16), plane_rows(half))
     spread(1, mg, xt, sh_ref)
 
     def place(k):
@@ -260,7 +274,7 @@
     extend(a_ext, 6, 32, sh_ref)
 
     feats = jnp.zeros((64, LANES), F32)
-    near_cot, far_cot = near_ref[256:320, :].astype(F32), far_ref[256:320, :].astype(F32)
+    near_cot, far_cot = near_ref[256:320, :].astype(F32), far_ref[256:320, :].astype(F32) * has_far
     own_cot = own_ref[256:320, :].astype(F32)
     pick = jnp.where(half == 1, 1.0, 0.0)
     left_cot = far_cot * pick + near_cot * (1.0 - pick)
@@ -296,10 +310,17 @@
                     value = swapped[lo : lo + 48] + block[lo + 32 : lo + 80]
                     pack[(chunk - 9) * 48 : (chunk - 8) * 48, 64:128] = value[:, 64:128]
 
+    which = share()
+    keep_ref[...] = pack[pl.ds(pl.multiple_of(which * 216, 8), 216), :]
+    send_ref[...] = pack[pl.ds(pl.multiple_of(216 - which * 216, 8), 216), :]
     extend(g_ext, 4, 64, sh_ref)
 
+
+def first_kernel(g_ext, wb_ref, xt_near, z_near, xt_far, z_far, one_ref, both, cells, taps):
+    half = near_half()
+    both[...] = mm(wb_ref[...], g_ext[...].reshape(4096, LANES))
     for which, x_ref, z_ref in ((half, xt_near, z_near), (1 - half, xt_far, z_far)):
-        back = mm(wb_ref[...], g_ext[pl.ds(which, 3)].reshape(3072, LANES))
+        back = both[pl.ds(pl.multiple_of(which * 128, 128), 128), :]
         acc = jnp.zeros((256, 256), F32)
         for eq in range(2):
             for er in range(2):
@@ -321,10 +342,9 @@
     for d in range(8):
         off = (d // 2 % 2) * 64 + (d % 2) * 16 + (d // 4) * 4
         total = total + taps[off : off + 192, d * 32 : d * 32 + 32]
-    pack[432:480, :] = jnp.concatenate([total[k * 48 : k * 48 + 48] for k in range(4)], axis=1)
-
-    keep_ref[...] = pack[pl.ds(pl.multiple_of(parity * 240, 8), 240), :]
-    send_ref[...] = pack[pl.ds(pl.multiple_of(240 - parity * 240, 8), 240), :]
+    rows = [total[b * 64 + c * 16 : b * 64 + c * 16 + 12] for b in range(3) for c in range(3)]
+    rows = jnp.concatenate(rows + [jnp.zeros((20, 32), F32)], axis=0)
+    one_ref[...] = jnp.concatenate([rows[k * 28 : k * 28 + 32] for k in range(4)], axis=1)
 
 
 def features_kernel(feat_ref, out_ref):
@@ -332,18 +352,19 @@
     out_ref[...] = mm_nt(same, feat_ref[...]).astype(BF16)
 
 
-def finish_kernel(mine_ref, other_ref, one_ref, two_ref, both):
-    parity = lax.rem(lax.axis_index("space"), 2)
-    both[pl.ds(pl.multiple_of(parity * 240, 8), 240), :] = mine_ref[...]
-    both[pl.ds(pl.multiple_of(240 - parity * 240, 8), 240), :] = other_ref[...]
-    two_ref[0:432, :] = both[0:432, 0:64]
-    two_ref[432:864, :] = both[0:432, 64:128]
+def finish_kernel(mine_ref, other_ref, one_ref, two_ref, both, one):
+    which = share()
+    both[pl.ds(pl.multiple_of(which * 216, 8), 216), :] = mine_ref[0:216, :]
+    both[pl.ds(pl.multiple_of(216 - which * 216, 8), 216), :] = other_ref[0:216, :]
+    one[...] = mine_ref[216:248, :] + other_ref[216:248, :]
+    two_ref[0:432, :] = both[:, 0:64]
+    two_ref[432:864, :] = both[:, 64:128]
     for a in range(3):
         for b in range(3):
             for c in range(3):
-                at = b * 64 + c * 16 + a * 4
-                k, row = at // 48, at % 48
-                one_ref[a * 9 + b * 3 + c] = both[432 + row : 436 + row, k * 32 : k * 32 + 32]
+                at = (b * 3 + c) * 12 + a * 4
+                k, row = at // 28, at % 28
+                one_ref[a * 9 + b * 3 + c] = one[row : row + 4, k * 32 : k * 32 + 32]
 
 
 def call(kernel, outs, scratch=(), flops=0, size=0, **specs):
@@ -366,11 +387,10 @@
     return [(i, j) for i, j in pairs] + [(j, i) for i, j in pairs]
 
 
-def total_over_mesh(keep, send, n_dp, n_space):
+def total_over_mesh(mine, feats, n_dp, n_space):
     axes = ("dp", "space")
     size = n_dp * n_space
-    near = [(i, i ^ 1) for i in range(size)]
-    mine = keep + lax.ppermute(send, axes, near)
+    shares = [bin(i).count("1") % 2 for i in range(size)]
     bits = [1 << k for k in range(1, 31) if 1 << k < size]
     bits = bits[-1:] + bits[:-1]
     groups = [bits[k : k + 2] for k in range(0, len(bits), 2)]
@@ -378,21 +398,29 @@
     turned = groups[middle:] + groups[:middle]
     if [len(g) for g in groups] != [len(g) for g in turned]:
         turned = groups
-    for even, odd in zip(groups, turned):
-        masks = [even + [even[0] ^ even[-1]], odd + [odd[0] ^ odd[-1]]]
+    for step, (even, odd) in enumerate(zip(groups, turned)):
+        masks = [[b | 1 for b in group] + [group[0] ^ group[-1]] for group in (even, odd)]
         count = 3 if len(even) == 2 else 1
         parts = [
-            lax.ppermute(mine, axes, [(i, i ^ masks[i % 2][k]) for i in range(size)]) for k in range(count)
+            lax.ppermute(mine, axes, [(i, i ^ masks[shares[i]][k]) for i in range(size)]) for k in range(count)
         ]
+        if step == len(groups) - 1:
+            feats = call(features_kernel, shape((LANES, 64), BF16), flops=10_000_000, size=1_000_000)(feats)
+            parts[-1], feats = lax.optimization_barrier((parts[-1], feats))
         mine = mine + parts[0]
         if count == 3:
             mine = mine + (parts[1] + parts[2])
-    return mine, lax.ppermute(mine, axes, near)
+        if step == 0:
+            mine, feats = lax.optimization_barrier((mine, feats))
+    return mine, lax.ppermute(mine, axes, [(i, i ^ 1) for i in range(size)]), feats
 
 
 def local(n_dp, n_space, crop, filter_one, filter_two, cotangent):
     near = [(i, i ^ 1) for i in range(n_space)]
-    across = both_ways([(i, i + 1) for i in range(1, n_space - 1, 2)])
+    pairs = [(k * n_space + i, k * n_space + i + 1) for k in range(n_dp) for i in range(1, n_space - 1, 2)]
+    if n_dp % 2 == 0:
+        pairs += [(k * n_space + i, (k + 1) * n_space + i) for k in range(0, n_dp, 2) for i in (0, n_space - 1)]
+    across = both_ways(pairs)
     with jax.named_scope("blocks"):
         own, edge = call(
             blocks_kernel,
@@ -402,7 +430,7 @@
         own, cot = lax.optimization_barrier((own, cotangent.transpose(0, 2, 3, 4, 1).reshape(LANES, 64)))
         cot = cot.T
     with jax.named_scope("halo"):
-        beyond = lax.ppermute(jnp.concatenate([own, cot, lax.ppermute(edge, "space", near)], axis=0), "space", across)
+        beyond = lax.ppermute(jnp.concatenate([own, cot, lax.ppermute(edge, "space", near)], axis=0), ("dp", "space"), across)
         own = jnp.concatenate([own, cot], axis=0)
         beside = lax.ppermute(own, "space", near)
     with jax.named_scope("near"):
@@ -411,7 +439,7 @@
             (
                 shape((512, 256), BF16),
                 shape((256, 1536), BF16),
-                shape((128, 3072), BF16),
+                shape((256, 4096), BF16),
                 shape((4, LANES, LANES), BF16),
                 shape((576, LANES), BF16),
                 shape((4, 256, LANES), F32),
@@ -431,30 +459,41 @@
             flops=1_000_000_000,
             size=3_000_000,
         )(own, beyond, w1, shifts)
-    with jax.named_scope("rest"):
-        feats, keep, send = call(
-            rest_kernel,
-            (shape((64, LANES), BF16), shape((240, 128), F32), shape((240, 128), F32)),
+    with jax.named_scope("second"):
+        feats, keep, send, g_ext = call(
+            second_kernel,
+            (
+                shape((64, LANES), BF16),
+                shape((216, 128), F32),
+                shape((216, 128), F32),
+                shape((4, 1024, LANES), BF16),
+            ),
             [
                 pltpu.VMEM((1, 256, LANES), BF16),
                 pltpu.VMEM((1, 576, LANES), BF16),
                 pltpu.VMEM((6, 512, LANES), BF16),
-                pltpu.VMEM((4, 1024, LANES), BF16),
-                pltpu.VMEM((2, 256, 256), F32),
-                pltpu.VMEM((288, 256), F32),
-                pltpu.VMEM((480, 128), F32),
+                pltpu.VMEM((432, 128), F32),
             ],
             flops=4_000_000_000,
             size=6_000_000,
-        )(own, beside, beyond, forward, w1, w2, wb, shifts, xt_near, z_near, maps_near, xt_far, z_far, maps_far)
+        )(own, beside, beyond, forward, w1, w2, shifts, maps_near, maps_far)
+        received = lax.ppermute(send, "space", near)
+    with jax.named_scope("first"):
+        one = call(
+            first_kernel,
+            shape((32, 128), F32),
+            [pltpu.VMEM((256, LANES), F32), pltpu.VMEM((2, 256, 256), F32), pltpu.VMEM((288, 256), F32)],
+            flops=4_000_000_000,
+            size=6_000_000,
+        )(g_ext, wb, xt_near, z_near, xt_far, z_far)
     with jax.named_scope("total"):
-        mine, other = total_over_mesh(keep, send, n_dp, n_space)
+        mine = jnp.concatenate([keep + received, one], axis=0)
+        mine, other, feats = total_over_mesh(mine, feats, n_dp, n_space)
         one, two = call(
             finish_kernel,
             (shape((27, 4, 32), F32), shape((864, 64), F32)),
-            [pltpu.VMEM((480, 128), F32)],
+            [pltpu.VMEM((432, 128), F32), pltpu.VMEM((32, 128), F32)],
         )(mine, other)
-        feats = call(features_kernel, shape((LANES, 64), BF16), flops=10_000_000, size=1_000_000)(feats)
     features = feats.reshape(1, 1, 16, 16, 64).transpose(0, 4, 1, 2, 3)
     return features, one.reshape(3, 3, 3, 4, 32), two.reshape(3, 3, 3, 32, 64)
 

time: 42.5 us -> 39.3 us (0.925)
  starting transfers between devices: 18.4 us -> 13.5 us
  local copies, waits for them, and re-layouts: 1.08 us -> 3.57 us
  waiting for transfers between devices: 12 us -> 11 us
    ppermute x1, starting transfers between devices: 7.61 us -> 1.28 us  [local(): forward = lax.ppermute(beyond[:256], 'space', near)]
    ppermute x1, starting transfers between devices: 0.67 us -> 3 us  [local(): lax.ppermute(jnp.concatenate([own, cot, lax.ppermute(edge, 'space', near)...]
    ppermute x8, waiting for transfers between devices: 11.3 us -> 10.3 us  [the longest x6 9.1 us: total_over_mesh(): lax.ppermute(mine, axes, [(i, i ^ masks[shares[i]][k]) for i in range(siz...]
    unnamed x8 -> x4, local copies, waits for them, and re-layouts: 0.96 us -> 1.87 us
    ppermute x8, starting transfers between devices: 9.47 us -> 8.58 us  [the longest x6 7.97 us: total_over_mesh(): lax.ppermute(mine, axes, [(i, i ^ masks[shares[i]][k]) for i in range(siz...]
    optimization_barrier x1, local copies, waits for them, and re-layouts: 0.09 us -> 0.92 us  [local(): lax.optimization_barrier((own, cotangent.transpose(0, 2, 3, 4, 1).reshape...]
    reshape x1, local copies, waits for them, and re-layouts: 0.03 us -> 0.77 us  [local(): filter_one.reshape(108, 32)]
    ppermute x1, waiting for transfers between devices: 0.6 us -> 0.01 us  [local(): lax.ppermute(edge, 'space', near)]
  transfers between devices with their start and end apart: 12 -> 12, of which waited for: 8 -> 7; matrix products, arithmetic and copies ran while one was open for 0% -> 4% of each run, Pallas kernels for 7% -> 13%
where the time goes in v2:
time: 39.3 us; the launch traced here: 39 us
  starting transfers between devices  13.5 us (34%)
  waiting for transfers between devices  11 us (28%)
  Pallas kernels  10.1 us (26%)
  local copies, waits for them, and re-layouts  3.57 us (9%)
  between operations  0.74 us (2%)
    ppermute x6, waiting for transfers between devices, total_over_mesh(): lax.ppermute(mine, axes, [(i, i ^ masks[shares[i]][k]) for i in range(siz...  9.1 us
    ppermute x6, starting transfers between devices, total_over_mesh(): lax.ppermute(mine, axes, [(i, i ^ masks[shares[i]][k]) for i in range(siz...  7.97 us
    pallas_call x1, Pallas kernels, local(): call(second_kernel, (shape((64, LANES), BF16), shape((216, 128), F32), sh...  3.14 us
    ppermute x1, starting transfers between devices, local(): lax.ppermute(jnp.concatenate([own, cot, lax.ppermute(edge, 'space', near)...  3 us
    pallas_call x1, Pallas kernels, local(): call(first_kernel, shape((32, 128), F32), [pltpu.VMEM((256, LANES), F32),...  2.03 us
    unnamed x4, local copies, waits for them, and re-layouts  1.87 us
    pallas_call x1, Pallas kernels, local(): call(near_kernel, (shape((512, 256), BF16), shape((256, 1536), BF16), sha...  1.36 us
    ppermute x1, starting transfers between devices, local(): forward = lax.ppermute(beyond[:256], 'space', near)  1.28 us
  transfers between devices with their start and end apart: 12, of which 7 were waited for; matrix products, arithmetic and copies ran while one was open for 4% of the time, Pallas kernels for 13%

profile of v2, /device:TPU:0, one launch (start us, length us, event | category | flops | bytes accessed | tf_op | source)
XLA Modules:
  0.0 39.0 jit_solution(3543402869917501433)
XLA Ops:
  0.6 0.0 copy-start
  0.6 0.9 %copy-done = bf16[1,4,4,64,64]{4,3,2,1,0:T(8,128)(2,1)S(1)} copy-done((bf16[1,4,4,64,64]{4,3,2,1,0:T(8,128)(2,1)S(1)}, bf16[1,4,4,64,64]{4,3,2,1,0:T(8,128)(2,1)}, u32[]{:S(2)}) %copy-start) | copy-done | bytes 131096
  1.6 0.9 %blocks.1 = (bf16[256,256]{1,0:T(8,128)(2,1)S(1)}, bf16[64,256]{1,0:T(8,128)(2,1)S(1)}) custom-call(bf16[1,4,4,64,64]{4,3,2,1,0:T(8,128)(2,1)S(1)} %copy-done), custom_call_target="tpu_custom_call" | custom-call | tf_op jit(solution)/shard_map/blocks/pallas_call | solution.py:425
  2.5 0.5 %collective-permute-start.1 = (bf16[64,256]{1,0:T(8,128)(2,1)S(1)}, bf16[64,256]{1,0:T(8,128)(2,1)S(1)}, u32[]{:S(2)}, u32[]{:S(2)}) collective-permute-start(bf16[64,256]{1,0:T(8,128)(2,1)S(1)} %get-tuple-element.32), channel_id=1, source_target_pairs={{0,1},{1,0},{2,3},{3,2},{4,5},{5,4},{6,7},{7,6},{8,9},{9,8},{10,11... | collective-permute-start | bytes 98312 | tf_op jit(solution)/shard_map/halo/ppermute | solution.py:433
  3.0 0.9 %copy.8 = bf16[256,64]{0,1:T(8,128)(2,1)S(1)} copy(bf16[256,64]{1,0:T(8,128)(2,1)} %bitcast.13) | data formatting | bytes 65536 | tf_op jit(solution)/shard_map/blocks/optimization_barrier | solution.py:430
  4.0 0.1 collective-permute-start
  4.1 0.0 collective-permute-done.1
  4.1 3.0 %collective-permute-start.2 = (bf16[384,256]{1,0:T(8,128)(2,1)S(1)}, bf16[384,256]{1,0:T(8,128)(2,1)S(1)}, u32[]{:S(2)}, u32[]{:S(2)}) collective-permute-start(bf16[384,256]{1,0:T(8,128)(2,1)S(1)} %pad_maximum_fusion), channel_id=1, source_target_pairs={{1,2},{3,4},{5,6},{7,8},{9,10},{11,12},{13,14},{17,18},{19,20},{21... | collective-permute-start | bytes 589832 | tf_op jit(solution)/shard_map/halo/ppermute | solution.py:433
  7.1 0.8 %reshape.25.f1_ref = bf16[108,32]{1,0:T(8,128)(2,1)S(1)} reshape(bf16[3,3,3,4,32]{4,3,2,1,0:T(4,128)(2,1)} %param.5) | data formatting | bytes 13824 | tf_op jit(solution)/shard_map/near/reshape | solution.py:451
  7.9 0.0 collective-permute-done.near_ref
  7.9 0.0 copy-start.1
  7.9 0.9 %copy-done.1 = bf16[3,3,3,32,64]{4,3,2,1,0:T(8,128)(2,1)S(1)} copy-done((bf16[3,3,3,32,64]{4,3,2,1,0:T(8,128)(2,1)S(1)}, bf16[3,3,3,32,64]{4,3,2,1,0:T(8,128)(2,1)}, u32[]{:S(2)}) %copy-start.1) | copy-done | bytes 110616
  8.9 1.4 %near.1 = (bf16[512,256]{1,0:T(8,128)(2,1)S(1)}, bf16[256,1536]{1,0:T(8,128)(2,1)S(1)}, bf16[256,4096]{1,0:T(8,128)(2,1)S(1)}, bf16[4,256,256]{2,1,0:T(8,128)(2,...) custom-call(bf16[320,256]{1,0:T(8,128)(2,1)S(1)} %pad_maximum_fusion.1.own_ref, ...), custom_call_target="tpu_custom_call" | custom-call | flops 1000000000 | bytes 4000000 | tf_op jit(solution)/shard_map/near/pallas_call | solution.py:437
  10.2 0.6 %collective-permute-done.2.far_ref = bf16[384,256]{1,0:T(8,128)(2,1)S(1)} collective-permute-done((bf16[384,256]{1,0:T(8,128)(2,1)S(1)}, bf16[384,256]{1,0:T(8,128)(2,1)S(1)}, u32[]{:S(2)}, u32[]{:S(2)}) %collective-permute-start.2) | collective-permute-done | bytes 196640 | tf_op jit(solution)/shard_map/halo/ppermute | solution.py:433
  10.8 1.3 %collective-permute-start.3 = (bf16[256,256]{1,0:T(8,128)(2,1)S(1)}, bf16[256,256]{1,0:T(8,128)(2,1)S(1)}, u32[]{:S(2)}, u32[]{:S(2)}) collective-permute-start(bf16[256,256]{1,0:T(8,128)(2,1)S(1)} %slice.3), channel_id=1, source_target_pairs={{0,1},{1,0},{2,3},{3,2},{4,5},{5,4},{6,7},{7,6},{8,9},{9,8},{10,11... | collective-permute-start | bytes 393224 | tf_op jit(solution)/shard_map/far/ppermute | solution.py:454
  12.1 0.9 %far.1 = (bf16[576,256]{1,0:T(8,128)(2,1)S(1)}, f32[4,256,256]{2,1,0:T(8,128)S(1)}, bf16[3,128,256]{2,1,0:T(8,128)(2,1)S(1)}) custom-call(bf16[320,256]{1,0:T(8,128)(2,1)S(1)} %pad_maximum_fusion.1.own_ref, bf16[384,256]{1,0:T(8,128)(2,1)S(1)} %collective-permute-done.2.far_ref, bf16[512,256]{1,0:T(8,128)(2,1)S(1)} %get-tuple-element.35.w1_ref, ...), custom_call_target="tpu_custom_call" | custom-call | flops 1000000000 | bytes 3000000 | tf_op jit(solution)/shard_map/far/pallas_call | solution.py:455
  13.0 0.1 collective-permute-done.3.fwd_ref
  13.1 3.1 %second.1 = (bf16[64,256]{1,0:T(8,128)(2,1)S(1)}, f32[216,128]{1,0:T(8,128)S(1)}, f32[216,128]{1,0:T(8,128)S(1)}, bf16[4,1024,256]{2,1,0:T(8,128)(2,1)S(1)}) custom-call(bf16[320,256]{1,0:T(8,128)(2,1)S(1)} %pad_maximum_fusion.1.own_ref, bf16[320,256]{1,0:T(8,128)(2,1)S(1)} %collective-permute-done.near_ref, ...), custom_call_target="tpu_custom_call" | custom-call | flops 4000000000 | bytes 6000000 | tf_op jit(solution)/shard_map/second/pallas_call | solution.py:463
  16.2 0.4 %collective-permute-start.4 = (f32[216,128]{1,0:T(8,128)S(1)}, f32[216,128]{1,0:T(8,128)S(1)}, u32[]{:S(2)}, u32[]{:S(2)}) collective-permute-start(f32[216,128]{1,0:T(8,128)S(1)} %get-tuple-element.41), channel_id=1, source_target_pairs={{0,1},{1,0},{2,3},{3,2},{4,5},{5,4},{6,7},{7,6},{8,9},{9,8},{10,11... | collective-permute-start | bytes 331784 | tf_op jit(solution)/shard_map/second/ppermute | solution.py:480
  16.7 2.0 %first.1 = f32[32,128]{1,0:T(8,128)S(1)} custom-call(bf16[4,1024,256]{2,1,0:T(8,128)(2,1)S(1)} %get-tuple-element.42.g_ext, bf16[256,4096]{1,0:T(8,128)(2,1)S(1)} %get-tuple-element.43.wb_ref, bf16[576,256]{1,0:T(8,128)(2,1)S(1)} %get-tuple-element.44.xt_near, f32[4,256,256]{2,1,0:T(8,128)S(1)} %get-tuple-element.45.z_near, ...), custom_call_target="tpu_custom_call" | custom-call | flops 4000000000 | bytes 6000000 | tf_op jit(solution)/shard_map/first/pallas_call | solution.py:482
  18.7 0.0 collective-permute-done.4
  18.7 2.5 %collective-permute-start.6 = (f32[248,128]{1,0:T(8,128)S(1)}, f32[248,128]{1,0:T(8,128)S(1)}, u32[]{:S(2)}, u32[]{:S(2)}) collective-permute-start(f32[248,128]{1,0:T(8,128)S(1)} %pad_maximum_fusion.2), channel_id=1, source_target_pairs={{0,3},{1,8},{2,11},{3,0},{4,13},{5,6},{6,5},{7,14},{8,1},{9,10},{1... | collective-permute-start | bytes 380936 | tf_op jit(solution)/shard_map/total/ppermute | solution.py:405
  21.3 1.0 %collective-permute-start.7 = (f32[248,128]{1,0:T(8,128)S(1)}, f32[248,128]{1,0:T(8,128)S(1)}, u32[]{:S(2)}, u32[]{:S(2)}) collective-permute-start(f32[248,128]{1,0:T(8,128)S(1)} %pad_maximum_fusion.2), channel_id=1, source_target_pairs={{0,18},{1,13},{2,14},{3,17},{4,8},{5,23},{6,20},{7,11},{8,4},{9,27... | collective-permute-start | bytes 380936 | tf_op jit(solution)/shard_map/total/ppermute | solution.py:405
  22.3 0.2 collective-permute-start.5
  22.5 2.5 %collective-permute-done.6 = f32[248,128]{1,0:T(8,128)S(1)} collective-permute-done((f32[248,128]{1,0:T(8,128)S(1)}, f32[248,128]{1,0:T(8,128)S(1)}, u32[]{:S(2)}, u32[]{:S(2)}) %collective-permute-start.6) | collective-permute-done | bytes 127008 | tf_op jit(solution)/shard_map/total/ppermute | solution.py:405
  25.1 2.0 %collective-permute-done.7 = f32[248,128]{1,0:T(8,128)S(1)} collective-permute-done((f32[248,128]{1,0:T(8,128)S(1)}, f32[248,128]{1,0:T(8,128)S(1)}, u32[]{:S(2)}, u32[]{:S(2)}) %collective-permute-start.7) | collective-permute-done | bytes 127008 | tf_op jit(solution)/shard_map/total/ppermute | solution.py:405
  27.1 0.0 collective-permute-done.5
  27.1 3.3 %collective-permute-start.8 = (f32[248,128]{1,0:T(8,128)S(1)}, f32[248,128]{1,0:T(8,128)S(1)}, u32[]{:S(2)}, u32[]{:S(2)}) collective-permute-start(f32[248,128]{1,0:T(8,128)S(1)} %add_add_fusion.1), channel_id=1, source_target_pairs={{0,12},{1,19},{2,16},{3,15},{4,22},{5,9},{6,10},{7,21},{8,26},{9,5... | collective-permute-start | bytes 380936 | tf_op jit(solution)/shard_map/total/ppermute | solution.py:405
  30.4 0.0 collective-permute-start.10
  30.4 0.9 %collective-permute-start.9 = (f32[248,128]{1,0:T(8,128)S(1)}, f32[248,128]{1,0:T(8,128)S(1)}, u32[]{:S(2)}, u32[]{:S(2)}) collective-permute-start(f32[248,128]{1,0:T(8,128)S(1)} %add_add_fusion.1), channel_id=1, source_target_pairs={{0,5},{1,16},{2,19},{3,6},{4,21},{5,0},{6,3},{7,22},{8,25},{9,12},... | collective-permute-start | bytes 380936 | tf_op jit(solution)/shard_map/total/ppermute | solution.py:405
  31.3 0.8 %total.2 = bf16[256,64]{1,0:T(8,128)(2,1)} custom-call(bf16[64,256]{1,0:T(8,128)(2,1)S(1)} %get-tuple-element.50.feat_ref), custom_call_target="tpu_custom_call" | custom-call | flops 10000000 | bytes 1000000 | tf_op jit(solution)/shard_map/total/pallas_call | solution.py:408
  32.1 1.9 %collective-permute-done.8 = f32[248,128]{1,0:T(8,128)S(1)} collective-permute-done((f32[248,128]{1,0:T(8,128)S(1)}, f32[248,128]{1,0:T(8,128)S(1)}, u32[]{:S(2)}, u32[]{:S(2)}) %collective-permute-start.8) | collective-permute-done | bytes 127008 | tf_op jit(solution)/shard_map/total/ppermute | solution.py:405
  34.0 2.7 %collective-permute-done.10 = f32[248,128]{1,0:T(8,128)S(1)} collective-permute-done((f32[248,128]{1,0:T(8,128)S(1)}, f32[248,128]{1,0:T(8,128)S(1)}, u32[]{:S(2)}, u32[]{:S(2)}) %collective-permute-start.10) | collective-permute-done | bytes 127008 | tf_op jit(solution)/shard_map/total/ppermute | solution.py:405
  36.6 0.0 collective-permute-done.9
  36.7 0.2 collective-permute-start.11
  36.9 1.2 %collective-permute-done.11.other_ref = f32[248,128]{1,0:T(8,128)S(1)} collective-permute-done((f32[248,128]{1,0:T(8,128)S(1)}, f32[248,128]{1,0:T(8,128)S(1)}, u32[]{:S(2)}, u32[]{:S(2)}) %collective-permute-start.11) | collective-permute-done | bytes 127008 | tf_op jit(solution)/shard_map/total/ppermute | solution.py:415
  38.1 0.9 %total.3 = (f32[27,4,32]{2,1,0:T(4,128)}, f32[864,64]{1,0:T(8,128)}) custom-call(f32[248,128]{1,0:T(8,128)S(1)} %add_add_fusion.mine_ref, f32[248,128]{1,0:T(8,128)S(1)} %collective-permute-done.11.other_ref), custom_call_target="tpu_custom_call" | custom-call | tf_op jit(solution)/shard_map/total/pallas_call | solution.py:492
  (7 shorter events, 0.1 us)
Async XLA Ops:
  0.6 1.0 %copy-start = (bf16[1,4,4,64,64]{4,3,2,1,0:T(8,128)(2,1)S(1)}, bf16[1,4,4,64,64]{4,3,2,1,0:T(8,128)(2,1)}, u32[]{:S(2)}) copy-start(bf16[1,4,4,64,64]{4,3,2,1,0:T(8,128)(2,1)} %crop_ref.1) | copy-start | bytes 393220
  2.5 1.6 %collective-permute-start.1 = (bf16[64,256]{1,0:T(8,128)(2,1)S(1)}, bf16[64,256]{1,0:T(8,128)(2,1)S(1)}, u32[]{:S(2)}, u32[]{:S(2)}) collective-permute-start(bf16[64,256]{1,0:T(8,128)(2,1)S(1)} %get-tuple-element.32), channel_id=1, source_target_pairs={{0,1},{1,0},{2,3},{3,2},{4,5},{5,4},{6,7},{7,6},{8,9},{9,8},{10,11... | collective-permute-start | bytes 98312 | tf_op jit(solution)/shard_map/halo/ppermute | solution.py:433
  4.0 3.9 %collective-permute-start = (bf16[320,256]{1,0:T(8,128)(2,1)S(1)}, bf16[320,256]{1,0:T(8,128)(2,1)S(1)}, u32[]{:S(2)}, u32[]{:S(2)}) collective-permute-start(bf16[320,256]{1,0:T(8,128)(2,1)S(1)} %pad_maximum_fusion.1.own_ref), channel_id=1, source_target_pairs={{0,1},{1,0},{2,3},{3,2},{4,5},{5,4},{6,7},{7,6},{8,9},{9,8},{10,11... | collective-permute-start | bytes 491528 | tf_op jit(solution)/shard_map/halo/ppermute | solution.py:435
  4.1 6.7 %collective-permute-start.2 = (bf16[384,256]{1,0:T(8,128)(2,1)S(1)}, bf16[384,256]{1,0:T(8,128)(2,1)S(1)}, u32[]{:S(2)}, u32[]{:S(2)}) collective-permute-start(bf16[384,256]{1,0:T(8,128)(2,1)S(1)} %pad_maximum_fusion), channel_id=1, source_target_pairs={{1,2},{3,4},{5,6},{7,8},{9,10},{11,12},{13,14},{17,18},{19,20},{21... | collective-permute-start | bytes 589832 | tf_op jit(solution)/shard_map/halo/ppermute | solution.py:433
  7.9 0.9 %copy-start.1 = (bf16[3,3,3,32,64]{4,3,2,1,0:T(8,128)(2,1)S(1)}, bf16[3,3,3,32,64]{4,3,2,1,0:T(8,128)(2,1)}, u32[]{:S(2)}) copy-start(bf16[3,3,3,32,64]{4,3,2,1,0:T(8,128)(2,1)} %param.6) | copy-start | bytes 331780
  10.8 2.3 %collective-permute-start.3 = (bf16[256,256]{1,0:T(8,128)(2,1)S(1)}, bf16[256,256]{1,0:T(8,128)(2,1)S(1)}, u32[]{:S(2)}, u32[]{:S(2)}) collective-permute-start(bf16[256,256]{1,0:T(8,128)(2,1)S(1)} %slice.3), channel_id=1, source_target_pairs={{0,1},{1,0},{2,3},{3,2},{4,5},{5,4},{6,7},{7,6},{8,9},{9,8},{10,11... | collective-permute-start | bytes 393224 | tf_op jit(solution)/shard_map/far/ppermute | solution.py:454
  16.2 2.5 %collective-permute-start.4 = (f32[216,128]{1,0:T(8,128)S(1)}, f32[216,128]{1,0:T(8,128)S(1)}, u32[]{:S(2)}, u32[]{:S(2)}) collective-permute-start(f32[216,128]{1,0:T(8,128)S(1)} %get-tuple-element.41), channel_id=1, source_target_pairs={{0,1},{1,0},{2,3},{3,2},{4,5},{5,4},{6,7},{7,6},{8,9},{9,8},{10,11... | collective-permute-start | bytes 331784 | tf_op jit(solution)/shard_map/second/ppermute | solution.py:480
  18.7 6.3 %collective-permute-start.6 = (f32[248,128]{1,0:T(8,128)S(1)}, f32[248,128]{1,0:T(8,128)S(1)}, u32[]{:S(2)}, u32[]{:S(2)}) collective-permute-start(f32[248,128]{1,0:T(8,128)S(1)} %pad_maximum_fusion.2), channel_id=1, source_target_pairs={{0,3},{1,8},{2,11},{3,0},{4,13},{5,6},{6,5},{7,14},{8,1},{9,10},{1... | collective-permute-start | bytes 380936 | tf_op jit(solution)/shard_map/total/ppermute | solution.py:405
  21.3 5.8 %collective-permute-start.7 = (f32[248,128]{1,0:T(8,128)S(1)}, f32[248,128]{1,0:T(8,128)S(1)}, u32[]{:S(2)}, u32[]{:S(2)}) collective-permute-start(f32[248,128]{1,0:T(8,128)S(1)} %pad_maximum_fusion.2), channel_id=1, source_target_pairs={{0,18},{1,13},{2,14},{3,17},{4,8},{5,23},{6,20},{7,11},{8,4},{9,27... | collective-permute-start | bytes 380936 | tf_op jit(solution)/shard_map/total/ppermute | solution.py:405
  22.3 4.8 %collective-permute-start.5 = (f32[248,128]{1,0:T(8,128)S(1)}, f32[248,128]{1,0:T(8,128)S(1)}, u32[]{:S(2)}, u32[]{:S(2)}) collective-permute-start(f32[248,128]{1,0:T(8,128)S(1)} %pad_maximum_fusion.2), channel_id=1, source_target_pairs={{0,17},{1,4},{2,7},{3,18},{4,1},{5,20},{6,23},{7,2},{8,13},{9,24},... | collective-permute-start | bytes 380936 | tf_op jit(solution)/shard_map/total/ppermute | solution.py:405
  27.1 6.8 %collective-permute-start.8 = (f32[248,128]{1,0:T(8,128)S(1)}, f32[248,128]{1,0:T(8,128)S(1)}, u32[]{:S(2)}, u32[]{:S(2)}) collective-permute-start(f32[248,128]{1,0:T(8,128)S(1)} %add_add_fusion.1), channel_id=1, source_target_pairs={{0,12},{1,19},{2,16},{3,15},{4,22},{5,9},{6,10},{7,21},{8,26},{9,5... | collective-permute-start | bytes 380936 | tf_op jit(solution)/shard_map/total/ppermute | solution.py:405
  30.4 6.2 %collective-permute-start.10 = (f32[248,128]{1,0:T(8,128)S(1)}, f32[248,128]{1,0:T(8,128)S(1)}, u32[]{:S(2)}, u32[]{:S(2)}) collective-permute-start(f32[248,128]{1,0:T(8,128)S(1)} %add_add_fusion.1), channel_id=1, source_target_pairs={{0,9},{1,2},{2,1},{3,10},{4,7},{5,12},{6,15},{7,4},{8,11},{9,0},{1... | collective-permute-start | bytes 380936 | tf_op jit(solution)/shard_map/total/ppermute | solution.py:405
  30.4 6.2 %collective-permute-start.9 = (f32[248,128]{1,0:T(8,128)S(1)}, f32[248,128]{1,0:T(8,128)S(1)}, u32[]{:S(2)}, u32[]{:S(2)}) collective-permute-start(f32[248,128]{1,0:T(8,128)S(1)} %add_add_fusion.1), channel_id=1, source_target_pairs={{0,5},{1,16},{2,19},{3,6},{4,21},{5,0},{6,3},{7,22},{8,25},{9,12},... | collective-permute-start | bytes 380936 | tf_op jit(solution)/shard_map/total/ppermute | solution.py:405
  36.7 1.4 %collective-permute-start.11 = (f32[248,128]{1,0:T(8,128)S(1)}, f32[248,128]{1,0:T(8,128)S(1)}, u32[]{:S(2)}, u32[]{:S(2)}) collective-permute-start(f32[248,128]{1,0:T(8,128)S(1)} %add_add_fusion.mine_ref), channel_id=1, source_target_pairs={{0,1},{1,0},{2,3},{3,2},{4,5},{5,4},{6,7},{7,6},{8,9},{9,8},{10,11... | collective-permute-start | bytes 380936 | tf_op jit(solution)/shard_map/total/ppermute | solution.py:415

commit v3 on v2

--- a/solution.py
+++ b/solution.py
@@ -10,6 +10,7 @@
 F32 = jnp.float32
 BF16 = jnp.bfloat16
 LANES = 256
+ORDERS = (((0, 1, 2), (0, 1, 2)), ((1, 0, 2), (1, 0, 2)))
 VMEM = pl.BlockSpec(memory_space=pltpu.VMEM)
 
 
@@ -84,10 +85,11 @@
 
     row, col = iota((96, 256), 0), iota((96, 256), 1)
     place = one_hot((lax.rem(row, 32) == lax.rem(col, 32)) & (lax.rem(col // 32, 4) == row // 32 + col // 128))
+    odd = 1 - near_half()
     for a in range(3):
         for b in range(3):
-            at = (a * 9 + b * 3) * 32
-            both = mm_tn(f2_ref[at : at + 96, :], place).astype(BF16)
+            at = pl.multiple_of(((a + odd * (2 - 2 * a)) * 9 + b * 3) * 32, 32)
+            both = mm_tn(f2_ref[pl.ds(at, 96), :], place).astype(BF16)
             for fq in range(2):
                 lane = a * 512 + (b + fq) * 128
                 w2_ref[fq * 128 : fq * 128 + 64, lane : lane + 128] = both[:, 0:128]
@@ -99,21 +101,17 @@
     none = jnp.zeros((32, 64), BF16)
     for a in range(3):
         for b in range(3):
-            at = ((2 - a) * 9 + (2 - b) * 3) * 32
-            taps = [f2_ref[at + 32 * k : at + 32 * k + 32, :] for k in (2, 1, 0)]
+            at = ((2 - a + odd * (2 * a - 2)) * 9 + (2 - b) * 3) * 32
+            taps = [f2_ref[pl.ds(pl.multiple_of(at + 32 * k, 32), 32), :] for k in (2, 1, 0)]
             for er in range(2):
                 block = jnp.concatenate([none] + taps if er else taps + [none], axis=1)
-                for s in range(2):
-                    for eq in range(2):
-                        lane = (a + s) * 1024 + (b + eq) * 256
-                        row = (s * 4 + eq * 2 + er) * 32
-                        wb_ref[row : row + 32, lane : lane + 256] = block
-        for s in range(2):
-            for eq in range(2):
-                lane = (a + s) * 1024 + (0 if eq else 3) * 256
-                wb_ref[s * 128 + eq * 64 : s * 128 + eq * 64 + 64, lane : lane + 256] = jnp.zeros((64, 256), BF16)
-    wb_ref[0:128, 3072:4096] = jnp.zeros((128, 1024), BF16)
-    wb_ref[128:256, 0:1024] = jnp.zeros((128, 1024), BF16)
+                for eq in range(2):
+                    lane = a * 1024 + (b + eq) * 256
+                    row = (eq * 2 + er) * 32
+                    wb_ref[row : row + 32, lane : lane + 256] = block
+        for eq in range(2):
+            lane = a * 1024 + (0 if eq else 3) * 256
+            wb_ref[eq * 64 : eq * 64 + 64, lane : lane + 256] = jnp.zeros((64, 256), BF16)
 
     k, lane = iota((LANES, LANES), 0), iota((LANES, LANES), 1)
     sh_ref[0] = one_hot(k == lane - 16)
@@ -234,10 +232,11 @@
 def extend(ref, planes, size, sh_ref):
     for source, target, matrix in ((2, 0, 0), (1, 3, 1)):
         at, to = (source * 4 + 1) * size, (target * 4 + 1) * size
-        block = ref[:, at : at + 2 * size, :].reshape(planes * 2 * size, LANES)
+        block = jnp.concatenate([ref[k, at : at + 2 * size, :] for k in planes], axis=0)
         moved = mm(block, sh_ref[matrix]).astype(BF16)
-        ref[:, to : to + 2 * size, :] = moved.reshape(planes, 2 * size, LANES)
-    cells = [(k, q) for k in range(planes) for q in range(4)]
+        for n, k in enumerate(planes):
+            ref[k, to : to + 2 * size, :] = moved[n * 2 * size : (n + 1) * 2 * size]
+    cells = [(k, q) for k in planes for q in range(4)]
     for source, target, matrix in ((2, 0, 2), (1, 3, 3)):
         block = jnp.concatenate(
             [ref[k, (q * 4 + source) * size : (q * 4 + source + 1) * size, :] for k, q in cells], axis=0
@@ -249,14 +248,11 @@
 
 def second_kernel(own_ref, near_ref, far_ref, fwd_ref, w1_ref, w2_ref, sh_ref, maps_near, maps_far,
                   feat_ref, keep_ref, send_ref, g_ext,
-                  mg, xt, a_ext, pack):
+                  mg, xt, a_ext, acc, pack):
     half = near_half()
     index, last = lax.axis_index("space"), lax.axis_size("space") - 1
     has_far = jnp.where((index == 0) | (index == last), 0.0, 1.0)
     near_has_far = jnp.where((index == 1) | (index == last - 1), 0.0, 1.0)
-
-    mg[0] = merge(near_ref[0:256, :], fwd_ref[...] * near_has_far.astype(BF16), plane_rows(half))
-    spread(1, mg, xt, sh_ref)
 
     def place(k):
         def store(at, rows):
@@ -264,41 +260,53 @@
             a_ext[k, to : to + rows.shape[0], :] = rows
         return store
 
-    def order(k):
-        return jnp.where(half == 1, k, 5 - k)
-
-    first_maps(xt, 0, half, w1_ref, place(order(5)))
-    for k, plane in ((3, maps_near[0]), (4, maps_near[1]), (2, maps_far[0]), (1, maps_far[1]), (0, maps_far[2])):
+    mg[0] = merge(near_ref[0:256, :], fwd_ref[...] * near_has_far.astype(BF16), plane_rows(half))
+    spread(1, mg, xt, sh_ref)
+    first_maps(xt, 0, half, w1_ref, place(5))
+
+    known = (maps_far[2], maps_far[1], maps_far[0], maps_near[0], maps_near[1])
+    for k, plane in enumerate(known):
         for eq in range(2):
-            place(order(k))(eq * 64, plane[eq * 64 : eq * 64 + 64])
-    extend(a_ext, 6, 32, sh_ref)
-
-    feats = jnp.zeros((64, LANES), F32)
+            place(k)(eq * 64, plane[eq * 64 : eq * 64 + 64])
+    extend(a_ext, range(6), 32, sh_ref)
+
     near_cot, far_cot = near_ref[256:320, :].astype(F32), far_ref[256:320, :].astype(F32) * has_far
     own_cot = own_ref[256:320, :].astype(F32)
-    pick = jnp.where(half == 1, 1.0, 0.0)
-    left_cot = far_cot * pick + near_cot * (1.0 - pick)
-    right_cot = near_cot * pick + far_cot * (1.0 - pick)
-    for t, cot in enumerate((left_cot, own_cot, own_cot, right_cot)):
-        z = mm(w2_ref[...], a_ext[t : t + 3].reshape(1536, LANES))
+    def second_maps(t, cot, feats=None):
         full, low = cot * 0.125, 0.3 * cot * 0.125
+        zs = []
+        for fq in range(2):
+            weights = [w2_ref[fq * 128 : fq * 128 + 128, a * 512 + fq * 128 : a * 512 + fq * 128 + 384] for a in range(3)]
+            rows = [a_ext[t + a, fq * 128 : fq * 128 + 384, :] for a in range(3)]
+            zs.append(mm(jnp.concatenate(weights, axis=1), jnp.concatenate(rows, axis=0)))
+        z = jnp.concatenate(zs, axis=0)
         for f in range(4):
             zf = z[f * 64 : f * 64 + 64]
-            if t in (1, 2):
+            if feats is not None:
                 feats = feats + jnp.where(zf > 0, zf, 0.3 * zf)
             at = ((f // 2 + 1) * 4 + f % 2 + 1) * 64
             g_ext[t, at : at + 64, :] = jnp.where(zf > 0, full, low).astype(BF16)
+        return feats
+
+    second_maps(0, far_cot)
+    feats = second_maps(2, own_cot, second_maps(1, own_cot, jnp.zeros((64, LANES), F32)))
     feat_ref[...] = (feats * 0.125).astype(BF16)
 
+    second_maps(3, near_cot)
+
+    grads = [
+        jnp.concatenate([g_ext[t + 1, (fq * 4 + 5) * 64 : (fq * 4 + 7) * 64, :] for fq in range(2)], axis=0)
+        for t in range(2)
+    ]
     for a in range(3):
-        acc = jnp.zeros((384, 128), F32)
-        for t in range(2):
-            for fq in range(2):
-                maps = a_ext[t + 1 + a, fq * 128 : fq * 128 + 384, :]
-                at = ((fq + 1) * 4 + 1) * 64
-                acc = acc + mm_nt(maps, g_ext[t + 1, at : at + 128, :])
+        both = mm_nt(a_ext[1 + a], grads[0]) + mm_nt(a_ext[2 + a], grads[1])
         for b in range(3):
-            block = acc[b * 128 : b * 128 + 128]
+            block = both[b * 128 : b * 128 + 128, 0:128] + both[b * 128 + 128 : b * 128 + 256, 128:256]
+            acc[a, b * 128 : b * 128 + 128, :] = block
+    for a in range(3):
+        tap = jnp.where(half == 1, a, 2 - a)
+        for b in range(3):
+            block = acc[tap, b * 128 : b * 128 + 128, :]
             swapped = pltpu.roll(block, 64, 1)
             for h in range(2):
                 chunk = (a * 3 + b) * 2 + h
@@ -313,14 +321,14 @@
     which = share()
     keep_ref[...] = pack[pl.ds(pl.multiple_of(which * 216, 8), 216), :]
     send_ref[...] = pack[pl.ds(pl.multiple_of(216 - which * 216, 8), 216), :]
-    extend(g_ext, 4, 64, sh_ref)
+    extend(g_ext, range(4), 64, sh_ref)
 
 
 def first_kernel(g_ext, wb_ref, xt_near, z_near, xt_far, z_far, one_ref, both, cells, taps):
-    half = near_half()
-    both[...] = mm(wb_ref[...], g_ext[...].reshape(4096, LANES))
-    for which, x_ref, z_ref in ((half, xt_near, z_near), (1 - half, xt_far, z_far)):
-        back = both[pl.ds(pl.multiple_of(which * 128, 128), 128), :]
+    for m in range(2):
+        both[m] = mm(wb_ref[...], g_ext[m : m + 3].reshape(3072, LANES))
+    for m, x_ref, z_ref in ((0, xt_far, z_far), (1, xt_near, z_near)):
+        back = both[m]
         acc = jnp.zeros((256, 256), F32)
         for eq in range(2):
             for er in range(2):
@@ -333,8 +341,9 @@
                     axis=0,
                 )
                 acc = acc + mm_nt(crop, grad)
-        cells[which] = acc
-    first, second = cells[0].reshape(16, 16, 256), cells[1].reshape(16, 16, 256)
+        cells[m] = acc
+    half = near_half()
+    first, second = cells[1 - half].reshape(16, 16, 256), cells[half].reshape(16, 16, 256)
     first = first + jnp.concatenate([second[:, 8:], second[:, :8]], axis=1)
     taps[0:256, :] = jnp.concatenate([first[:, 12:], first[:, :12]], axis=1).reshape(256, 256)
     taps[256:288, :] = jnp.zeros((32, 256), F32)
@@ -400,6 +409,8 @@
         turned = groups
     for step, (even, odd) in enumerate(zip(groups, turned)):
         masks = [[b | 1 for b in group] + [group[0] ^ group[-1]] for group in (even, odd)]
+        if len(even) == 2:
+            masks = [[masks[k][n] for n in ORDERS[step % 2][k]] for k in range(2)]
         count = 3 if len(even) == 2 else 1
         parts = [
             lax.ppermute(mine, axes, [(i, i ^ masks[shares[i]][k]) for i in range(size)]) for k in range(count)
@@ -439,7 +450,7 @@
             (
                 shape((512, 256), BF16),
                 shape((256, 1536), BF16),
-                shape((256, 4096), BF16),
+                shape((128, 3072), BF16),
                 shape((4, LANES, LANES), BF16),
                 shape((576, LANES), BF16),
                 shape((4, 256, LANES), F32),
@@ -472,6 +483,7 @@
                 pltpu.VMEM((1, 256, LANES), BF16),
                 pltpu.VMEM((1, 576, LANES), BF16),
                 pltpu.VMEM((6, 512, LANES), BF16),
+                pltpu.VMEM((3, 384, 128), F32),
                 pltpu.VMEM((432, 128), F32),
             ],
             flops=4_000_000_000,
@@ -482,7 +494,7 @@
         one = call(
             first_kernel,
             shape((32, 128), F32),
-            [pltpu.VMEM((256, LANES), F32), pltpu.VMEM((2, 256, 256), F32), pltpu.VMEM((288, 256), F32)],
+            [pltpu.VMEM((2, 128, LANES), F32), pltpu.VMEM((2, 256, 256), F32), pltpu.VMEM((288, 256), F32)],
             flops=4_000_000_000,
             size=6_000_000,
         )(g_ext, wb, xt_near, z_near, xt_far, z_far)

time: 39.3 us -> 38.2 us (0.972)
  Pallas kernels: 10.1 us -> 8.92 us
    pallas_call x1, Pallas kernels: 2.03 us -> 1.4 us  [local(): call(first_kernel, shape((32, 128), F32), [pltpu.VMEM((2, 128, LANES), F3...]
    pallas_call x1, Pallas kernels: 3.14 us -> 2.67 us  [local(): call(second_kernel, (shape((64, LANES), BF16), shape((216, 128), F32), sh...]
  transfers between devices with their start and end apart: 12 -> 12, of which waited for: 7 -> 7; matrix products, arithmetic and copies ran while one was open for 4% -> 5% of each run, Pallas kernels for 13% -> 12%
where the time goes in v3:
time: 38.2 us; the launch traced here: 37.9 us
  starting transfers between devices  13.7 us (36%)
  waiting for transfers between devices  10.8 us (28%)
  Pallas kernels  8.92 us (23%)
  local copies, waits for them, and re-layouts  3.57 us (9%)
  between operations  0.74 us (2%)
    ppermute x6, waiting for transfers between devices, total_over_mesh(): lax.ppermute(mine, axes, [(i, i ^ masks[shares[i]][k]) for i in range(siz...  9.1 us
    ppermute x6, starting transfers between devices, total_over_mesh(): lax.ppermute(mine, axes, [(i, i ^ masks[shares[i]][k]) for i in range(siz...  7.98 us
    ppermute x1, starting transfers between devices, local(): lax.ppermute(jnp.concatenate([own, cot, lax.ppermute(edge, 'space', near)...  3 us
    pallas_call x1, Pallas kernels, local(): call(second_kernel, (shape((64, LANES), BF16), shape((216, 128), F32), sh...  2.67 us
    unnamed x4, local copies, waits for them, and re-layouts  1.87 us
    pallas_call x1, Pallas kernels, local(): call(first_kernel, shape((32, 128), F32), [pltpu.VMEM((2, 128, LANES), F3...  1.4 us
    ppermute x1, starting transfers between devices, local(): forward = lax.ppermute(beyond[:256], 'space', near)  1.28 us
    pallas_call x1, Pallas kernels, local(): call(near_kernel, (shape((512, 256), BF16), shape((256, 1536), BF16), sha...  1.27 us
  transfers between devices with their start and end apart: 12, of which 7 were waited for; matrix products, arithmetic and copies ran while one was open for 5% of the time, Pallas kernels for 12%

profile of v3, /device:TPU:0, one launch (start us, length us, event | category | flops | bytes accessed | tf_op | source)
XLA Modules:
  0.0 37.9 jit_solution(3392953809176773566)
XLA Ops:
  0.6 0.0 copy-start
  0.6 0.9 %copy-done = bf16[1,4,4,64,64]{4,3,2,1,0:T(8,128)(2,1)S(1)} copy-done((bf16[1,4,4,64,64]{4,3,2,1,0:T(8,128)(2,1)S(1)}, bf16[1,4,4,64,64]{4,3,2,1,0:T(8,128)(2,1)}, u32[]{:S(2)}) %copy-start) | copy-done | bytes 131096
  1.6 0.9 %blocks.1 = (bf16[256,256]{1,0:T(8,128)(2,1)S(1)}, bf16[64,256]{1,0:T(8,128)(2,1)S(1)}) custom-call(bf16[1,4,4,64,64]{4,3,2,1,0:T(8,128)(2,1)S(1)} %copy-done), custom_call_target="tpu_custom_call" | custom-call | tf_op jit(solution)/shard_map/blocks/pallas_call | solution.py:436
  2.5 0.5 %collective-permute-start.1 = (bf16[64,256]{1,0:T(8,128)(2,1)S(1)}, bf16[64,256]{1,0:T(8,128)(2,1)S(1)}, u32[]{:S(2)}, u32[]{:S(2)}) collective-permute-start(bf16[64,256]{1,0:T(8,128)(2,1)S(1)} %get-tuple-element.32), channel_id=1, source_target_pairs={{0,1},{1,0},{2,3},{3,2},{4,5},{5,4},{6,7},{7,6},{8,9},{9,8},{10,11... | collective-permute-start | bytes 98312 | tf_op jit(solution)/shard_map/halo/ppermute | solution.py:444
  3.0 0.9 %copy.8 = bf16[256,64]{0,1:T(8,128)(2,1)S(1)} copy(bf16[256,64]{1,0:T(8,128)(2,1)} %bitcast.13) | data formatting | bytes 65536 | tf_op jit(solution)/shard_map/blocks/optimization_barrier | solution.py:441
  4.0 0.1 collective-permute-start
  4.1 0.0 collective-permute-done.1
  4.1 3.0 %collective-permute-start.2 = (bf16[384,256]{1,0:T(8,128)(2,1)S(1)}, bf16[384,256]{1,0:T(8,128)(2,1)S(1)}, u32[]{:S(2)}, u32[]{:S(2)}) collective-permute-start(bf16[384,256]{1,0:T(8,128)(2,1)S(1)} %pad_maximum_fusion), channel_id=1, source_target_pairs={{1,2},{3,4},{5,6},{7,8},{9,10},{11,12},{13,14},{17,18},{19,20},{21... | collective-permute-start | bytes 589832 | tf_op jit(solution)/shard_map/halo/ppermute | solution.py:444
  7.1 0.8 %reshape.25.f1_ref = bf16[108,32]{1,0:T(8,128)(2,1)S(1)} reshape(bf16[3,3,3,4,32]{4,3,2,1,0:T(4,128)(2,1)} %param.5) | data formatting | bytes 13824 | tf_op jit(solution)/shard_map/near/reshape | solution.py:462
  7.9 0.0 collective-permute-done.near_ref
  7.9 0.0 copy-start.1
  7.9 0.9 %copy-done.1 = bf16[3,3,3,32,64]{4,3,2,1,0:T(8,128)(2,1)S(1)} copy-done((bf16[3,3,3,32,64]{4,3,2,1,0:T(8,128)(2,1)S(1)}, bf16[3,3,3,32,64]{4,3,2,1,0:T(8,128)(2,1)}, u32[]{:S(2)}) %copy-start.1) | copy-done | bytes 110616
  8.9 1.3 %near.1 = (bf16[512,256]{1,0:T(8,128)(2,1)S(1)}, bf16[256,1536]{1,0:T(8,128)(2,1)S(1)}, bf16[128,3072]{1,0:T(8,128)(2,1)S(1)}, bf16[4,256,256]{2,1,0:T(8,128)(2,...) custom-call(bf16[320,256]{1,0:T(8,128)(2,1)S(1)} %pad_maximum_fusion.1.own_ref, ...), custom_call_target="tpu_custom_call" | custom-call | flops 1000000000 | bytes 4000000 | tf_op jit(solution)/shard_map/near/pallas_call | solution.py:448
  10.1 0.6 %collective-permute-done.2.far_ref = bf16[384,256]{1,0:T(8,128)(2,1)S(1)} collective-permute-done((bf16[384,256]{1,0:T(8,128)(2,1)S(1)}, bf16[384,256]{1,0:T(8,128)(2,1)S(1)}, u32[]{:S(2)}, u32[]{:S(2)}) %collective-permute-start.2) | collective-permute-done | bytes 196640 | tf_op jit(solution)/shard_map/halo/ppermute | solution.py:444
  10.8 1.3 %collective-permute-start.3 = (bf16[256,256]{1,0:T(8,128)(2,1)S(1)}, bf16[256,256]{1,0:T(8,128)(2,1)S(1)}, u32[]{:S(2)}, u32[]{:S(2)}) collective-permute-start(bf16[256,256]{1,0:T(8,128)(2,1)S(1)} %slice.3), channel_id=1, source_target_pairs={{0,1},{1,0},{2,3},{3,2},{4,5},{5,4},{6,7},{7,6},{8,9},{9,8},{10,11... | collective-permute-start | bytes 393224 | tf_op jit(solution)/shard_map/far/ppermute | solution.py:465
  12.1 0.9 %far.1 = (bf16[576,256]{1,0:T(8,128)(2,1)S(1)}, f32[4,256,256]{2,1,0:T(8,128)S(1)}, bf16[3,128,256]{2,1,0:T(8,128)(2,1)S(1)}) custom-call(bf16[320,256]{1,0:T(8,128)(2,1)S(1)} %pad_maximum_fusion.1.own_ref, bf16[384,256]{1,0:T(8,128)(2,1)S(1)} %collective-permute-done.2.far_ref, bf16[512,256]{1,0:T(8,128)(2,1)S(1)} %get-tuple-element.35.w1_ref, ...), custom_call_target="tpu_custom_call" | custom-call | flops 1000000000 | bytes 3000000 | tf_op jit(solution)/shard_map/far/pallas_call | solution.py:466
  13.0 0.1 collective-permute-done.3.fwd_ref
  13.1 2.7 %second.1 = (bf16[64,256]{1,0:T(8,128)(2,1)S(1)}, f32[216,128]{1,0:T(8,128)S(1)}, f32[216,128]{1,0:T(8,128)S(1)}, bf16[4,1024,256]{2,1,0:T(8,128)(2,1)S(1)}) custom-call(bf16[320,256]{1,0:T(8,128)(2,1)S(1)} %pad_maximum_fusion.1.own_ref, bf16[320,256]{1,0:T(8,128)(2,1)S(1)} %collective-permute-done.near_ref, ...), custom_call_target="tpu_custom_call" | custom-call | flops 4000000000 | bytes 6000000 | tf_op jit(solution)/shard_map/second/pallas_call | solution.py:474
  15.7 0.4 %collective-permute-start.4 = (f32[216,128]{1,0:T(8,128)S(1)}, f32[216,128]{1,0:T(8,128)S(1)}, u32[]{:S(2)}, u32[]{:S(2)}) collective-permute-start(f32[216,128]{1,0:T(8,128)S(1)} %get-tuple-element.41), channel_id=1, source_target_pairs={{0,1},{1,0},{2,3},{3,2},{4,5},{5,4},{6,7},{7,6},{8,9},{9,8},{10,11... | collective-permute-start | bytes 331784 | tf_op jit(solution)/shard_map/second/ppermute | solution.py:492
  16.2 1.4 %first.1 = f32[32,128]{1,0:T(8,128)S(1)} custom-call(bf16[4,1024,256]{2,1,0:T(8,128)(2,1)S(1)} %get-tuple-element.42.g_ext, bf16[128,3072]{1,0:T(8,128)(2,1)S(1)} %get-tuple-element.43.wb_ref, bf16[576,256]{1,0:T(8,128)(2,1)S(1)} %get-tuple-element.44.xt_near, f32[4,256,256]{2,1,0:T(8,128)S(1)} %get-tuple-element.45.z_near, ...), custom_call_target="tpu_custom_call" | custom-call | flops 4000000000 | bytes 6000000 | tf_op jit(solution)/shard_map/first/pallas_call | solution.py:494
  17.6 0.0 collective-permute-done.4
  17.6 2.5 %collective-permute-start.6 = (f32[248,128]{1,0:T(8,128)S(1)}, f32[248,128]{1,0:T(8,128)S(1)}, u32[]{:S(2)}, u32[]{:S(2)}) collective-permute-start(f32[248,128]{1,0:T(8,128)S(1)} %pad_maximum_fusion.2), channel_id=1, source_target_pairs={{0,3},{1,8},{2,11},{3,0},{4,13},{5,6},{6,5},{7,14},{8,1},{9,10},{1... | collective-permute-start | bytes 380936 | tf_op jit(solution)/shard_map/total/ppermute | solution.py:416
  20.2 1.0 %collective-permute-start.7 = (f32[248,128]{1,0:T(8,128)S(1)}, f32[248,128]{1,0:T(8,128)S(1)}, u32[]{:S(2)}, u32[]{:S(2)}) collective-permute-start(f32[248,128]{1,0:T(8,128)S(1)} %pad_maximum_fusion.2), channel_id=1, source_target_pairs={{0,18},{1,13},{2,14},{3,17},{4,8},{5,23},{6,20},{7,11},{8,4},{9,27... | collective-permute-start | bytes 380936 | tf_op jit(solution)/shard_map/total/ppermute | solution.py:416
  21.2 0.2 collective-permute-start.5
  21.4 2.5 %collective-permute-done.6 = f32[248,128]{1,0:T(8,128)S(1)} collective-permute-done((f32[248,128]{1,0:T(8,128)S(1)}, f32[248,128]{1,0:T(8,128)S(1)}, u32[]{:S(2)}, u32[]{:S(2)}) %collective-permute-start.6) | collective-permute-done | bytes 127008 | tf_op jit(solution)/shard_map/total/ppermute | solution.py:416
  24.0 2.0 %collective-permute-done.7 = f32[248,128]{1,0:T(8,128)S(1)} collective-permute-done((f32[248,128]{1,0:T(8,128)S(1)}, f32[248,128]{1,0:T(8,128)S(1)}, u32[]{:S(2)}, u32[]{:S(2)}) %collective-permute-start.7) | collective-permute-done | bytes 127008 | tf_op jit(solution)/shard_map/total/ppermute | solution.py:416
  26.0 0.0 collective-permute-done.5
  26.0 3.3 %collective-permute-start.8 = (f32[248,128]{1,0:T(8,128)S(1)}, f32[248,128]{1,0:T(8,128)S(1)}, u32[]{:S(2)}, u32[]{:S(2)}) collective-permute-start(f32[248,128]{1,0:T(8,128)S(1)} %add_add_fusion.1), channel_id=1, source_target_pairs={{0,12},{1,19},{2,16},{3,15},{4,22},{5,9},{6,10},{7,21},{8,26},{9,5... | collective-permute-start | bytes 380936 | tf_op jit(solution)/shard_map/total/ppermute | solution.py:416
  29.3 0.0 collective-permute-start.10
  29.3 0.9 %collective-permute-start.9 = (f32[248,128]{1,0:T(8,128)S(1)}, f32[248,128]{1,0:T(8,128)S(1)}, u32[]{:S(2)}, u32[]{:S(2)}) collective-permute-start(f32[248,128]{1,0:T(8,128)S(1)} %add_add_fusion.1), channel_id=1, source_target_pairs={{0,9},{1,2},{2,1},{3,10},{4,7},{5,12},{6,15},{7,4},{8,11},{9,0},{1... | collective-permute-start | bytes 380936 | tf_op jit(solution)/shard_map/total/ppermute | solution.py:416
  30.2 0.8 %total.2 = bf16[256,64]{1,0:T(8,128)(2,1)} custom-call(bf16[64,256]{1,0:T(8,128)(2,1)S(1)} %get-tuple-element.50.feat_ref), custom_call_target="tpu_custom_call" | custom-call | flops 10000000 | bytes 1000000 | tf_op jit(solution)/shard_map/total/pallas_call | solution.py:419
  31.0 1.9 %collective-permute-done.8 = f32[248,128]{1,0:T(8,128)S(1)} collective-permute-done((f32[248,128]{1,0:T(8,128)S(1)}, f32[248,128]{1,0:T(8,128)S(1)}, u32[]{:S(2)}, u32[]{:S(2)}) %collective-permute-start.8) | collective-permute-done | bytes 127008 | tf_op jit(solution)/shard_map/total/ppermute | solution.py:416
  32.9 2.7 %collective-permute-done.10 = f32[248,128]{1,0:T(8,128)S(1)} collective-permute-done((f32[248,128]{1,0:T(8,128)S(1)}, f32[248,128]{1,0:T(8,128)S(1)}, u32[]{:S(2)}, u32[]{:S(2)}) %collective-permute-start.10) | collective-permute-done | bytes 127008 | tf_op jit(solution)/shard_map/total/ppermute | solution.py:416
  35.5 0.0 collective-permute-done.9
  35.6 0.4 %collective-permute-start.11 = (f32[248,128]{1,0:T(8,128)S(1)}, f32[248,128]{1,0:T(8,128)S(1)}, u32[]{:S(2)}, u32[]{:S(2)}) collective-permute-start(f32[248,128]{1,0:T(8,128)S(1)} %add_add_fusion.mine_ref), channel_id=1, source_target_pairs={{0,1},{1,0},{2,3},{3,2},{4,5},{5,4},{6,7},{7,6},{8,9},{9,8},{10,11... | collective-permute-start | bytes 380936 | tf_op jit(solution)/shard_map/total/ppermute | solution.py:426
  36.0 1.0 %collective-permute-done.11.other_ref = f32[248,128]{1,0:T(8,128)S(1)} collective-permute-done((f32[248,128]{1,0:T(8,128)S(1)}, f32[248,128]{1,0:T(8,128)S(1)}, u32[]{:S(2)}, u32[]{:S(2)}) %collective-permute-start.11) | collective-permute-done | bytes 127008 | tf_op jit(solution)/shard_map/total/ppermute | solution.py:426
  37.0 0.9 %total.3 = (f32[27,4,32]{2,1,0:T(4,128)}, f32[864,64]{1,0:T(8,128)}) custom-call(f32[248,128]{1,0:T(8,128)S(1)} %add_add_fusion.mine_ref, f32[248,128]{1,0:T(8,128)S(1)} %collective-permute-done.11.other_ref), custom_call_target="tpu_custom_call" | custom-call | tf_op jit(solution)/shard_map/total/pallas_call | solution.py:504
  (7 shorter events, 0.1 us)
Async XLA Ops:
  0.6 1.0 %copy-start = (bf16[1,4,4,64,64]{4,3,2,1,0:T(8,128)(2,1)S(1)}, bf16[1,4,4,64,64]{4,3,2,1,0:T(8,128)(2,1)}, u32[]{:S(2)}) copy-start(bf16[1,4,4,64,64]{4,3,2,1,0:T(8,128)(2,1)} %crop_ref.1) | copy-start | bytes 393220
  2.5 1.6 %collective-permute-start.1 = (bf16[64,256]{1,0:T(8,128)(2,1)S(1)}, bf16[64,256]{1,0:T(8,128)(2,1)S(1)}, u32[]{:S(2)}, u32[]{:S(2)}) collective-permute-start(bf16[64,256]{1,0:T(8,128)(2,1)S(1)} %get-tuple-element.32), channel_id=1, source_target_pairs={{0,1},{1,0},{2,3},{3,2},{4,5},{5,4},{6,7},{7,6},{8,9},{9,8},{10,11... | collective-permute-start | bytes 98312 | tf_op jit(solution)/shard_map/halo/ppermute | solution.py:444
  4.0 3.9 %collective-permute-start = (bf16[320,256]{1,0:T(8,128)(2,1)S(1)}, bf16[320,256]{1,0:T(8,128)(2,1)S(1)}, u32[]{:S(2)}, u32[]{:S(2)}) collective-permute-start(bf16[320,256]{1,0:T(8,128)(2,1)S(1)} %pad_maximum_fusion.1.own_ref), channel_id=1, source_target_pairs={{0,1},{1,0},{2,3},{3,2},{4,5},{5,4},{6,7},{7,6},{8,9},{9,8},{10,11... | collective-permute-start | bytes 491528 | tf_op jit(solution)/shard_map/halo/ppermute | solution.py:446
  4.1 6.7 %collective-permute-start.2 = (bf16[384,256]{1,0:T(8,128)(2,1)S(1)}, bf16[384,256]{1,0:T(8,128)(2,1)S(1)}, u32[]{:S(2)}, u32[]{:S(2)}) collective-permute-start(bf16[384,256]{1,0:T(8,128)(2,1)S(1)} %pad_maximum_fusion), channel_id=1, source_target_pairs={{1,2},{3,4},{5,6},{7,8},{9,10},{11,12},{13,14},{17,18},{19,20},{21... | collective-permute-start | bytes 589832 | tf_op jit(solution)/shard_map/halo/ppermute | solution.py:444
  7.9 0.9 %copy-start.1 = (bf16[3,3,3,32,64]{4,3,2,1,0:T(8,128)(2,1)S(1)}, bf16[3,3,3,32,64]{4,3,2,1,0:T(8,128)(2,1)}, u32[]{:S(2)}) copy-start(bf16[3,3,3,32,64]{4,3,2,1,0:T(8,128)(2,1)} %param.6) | copy-start | bytes 331780
  10.8 2.3 %collective-permute-start.3 = (bf16[256,256]{1,0:T(8,128)(2,1)S(1)}, bf16[256,256]{1,0:T(8,128)(2,1)S(1)}, u32[]{:S(2)}, u32[]{:S(2)}) collective-permute-start(bf16[256,256]{1,0:T(8,128)(2,1)S(1)} %slice.3), channel_id=1, source_target_pairs={{0,1},{1,0},{2,3},{3,2},{4,5},{5,4},{6,7},{7,6},{8,9},{9,8},{10,11... | collective-permute-start | bytes 393224 | tf_op jit(solution)/shard_map/far/ppermute | solution.py:465
  15.7 1.8 %collective-permute-start.4 = (f32[216,128]{1,0:T(8,128)S(1)}, f32[216,128]{1,0:T(8,128)S(1)}, u32[]{:S(2)}, u32[]{:S(2)}) collective-permute-start(f32[216,128]{1,0:T(8,128)S(1)} %get-tuple-element.41), channel_id=1, source_target_pairs={{0,1},{1,0},{2,3},{3,2},{4,5},{5,4},{6,7},{7,6},{8,9},{9,8},{10,11... | collective-permute-start | bytes 331784 | tf_op jit(solution)/shard_map/second/ppermute | solution.py:492
  17.6 6.3 %collective-permute-start.6 = (f32[248,128]{1,0:T(8,128)S(1)}, f32[248,128]{1,0:T(8,128)S(1)}, u32[]{:S(2)}, u32[]{:S(2)}) collective-permute-start(f32[248,128]{1,0:T(8,128)S(1)} %pad_maximum_fusion.2), channel_id=1, source_target_pairs={{0,3},{1,8},{2,11},{3,0},{4,13},{5,6},{6,5},{7,14},{8,1},{9,10},{1... | collective-permute-start | bytes 380936 | tf_op jit(solution)/shard_map/total/ppermute | solution.py:416
  20.2 5.8 %collective-permute-start.7 = (f32[248,128]{1,0:T(8,128)S(1)}, f32[248,128]{1,0:T(8,128)S(1)}, u32[]{:S(2)}, u32[]{:S(2)}) collective-permute-start(f32[248,128]{1,0:T(8,128)S(1)} %pad_maximum_fusion.2), channel_id=1, source_target_pairs={{0,18},{1,13},{2,14},{3,17},{4,8},{5,23},{6,20},{7,11},{8,4},{9,27... | collective-permute-start | bytes 380936 | tf_op jit(solution)/shard_map/total/ppermute | solution.py:416
  21.2 4.8 %collective-permute-start.5 = (f32[248,128]{1,0:T(8,128)S(1)}, f32[248,128]{1,0:T(8,128)S(1)}, u32[]{:S(2)}, u32[]{:S(2)}) collective-permute-start(f32[248,128]{1,0:T(8,128)S(1)} %pad_maximum_fusion.2), channel_id=1, source_target_pairs={{0,17},{1,4},{2,7},{3,18},{4,1},{5,20},{6,23},{7,2},{8,13},{9,24},... | collective-permute-start | bytes 380936 | tf_op jit(solution)/shard_map/total/ppermute | solution.py:416
  26.0 6.8 %collective-permute-start.8 = (f32[248,128]{1,0:T(8,128)S(1)}, f32[248,128]{1,0:T(8,128)S(1)}, u32[]{:S(2)}, u32[]{:S(2)}) collective-permute-start(f32[248,128]{1,0:T(8,128)S(1)} %add_add_fusion.1), channel_id=1, source_target_pairs={{0,12},{1,19},{2,16},{3,15},{4,22},{5,9},{6,10},{7,21},{8,26},{9,5... | collective-permute-start | bytes 380936 | tf_op jit(solution)/shard_map/total/ppermute | solution.py:416
  29.3 6.2 %collective-permute-start.10 = (f32[248,128]{1,0:T(8,128)S(1)}, f32[248,128]{1,0:T(8,128)S(1)}, u32[]{:S(2)}, u32[]{:S(2)}) collective-permute-start(f32[248,128]{1,0:T(8,128)S(1)} %add_add_fusion.1), channel_id=1, source_target_pairs={{0,5},{1,16},{2,19},{3,6},{4,21},{5,0},{6,3},{7,22},{8,25},{9,12},... | collective-permute-start | bytes 380936 | tf_op jit(solution)/shard_map/total/ppermute | solution.py:416
  29.3 6.2 %collective-permute-start.9 = (f32[248,128]{1,0:T(8,128)S(1)}, f32[248,128]{1,0:T(8,128)S(1)}, u32[]{:S(2)}, u32[]{:S(2)}) collective-permute-start(f32[248,128]{1,0:T(8,128)S(1)} %add_add_fusion.1), channel_id=1, source_target_pairs={{0,9},{1,2},{2,1},{3,10},{4,7},{5,12},{6,15},{7,4},{8,11},{9,0},{1... | collective-permute-start | bytes 380936 | tf_op jit(solution)/shard_map/total/ppermute | solution.py:416
  35.6 1.4 %collective-permute-start.11 = (f32[248,128]{1,0:T(8,128)S(1)}, f32[248,128]{1,0:T(8,128)S(1)}, u32[]{:S(2)}, u32[]{:S(2)}) collective-permute-start(f32[248,128]{1,0:T(8,128)S(1)} %add_add_fusion.mine_ref), channel_id=1, source_target_pairs={{0,1},{1,0},{2,3},{3,2},{4,5},{5,4},{6,7},{7,6},{8,9},{9,8},{10,11... | collective-permute-start | bytes 380936 | tf_op jit(solution)/shard_map/total/ppermute | solution.py:426

commit v4 on v3

--- a/solution.py
+++ b/solution.py
@@ -34,7 +34,7 @@
     return jnp.where(mask, 1.0, 0.0).astype(BF16)
 
 
-def blocks_kernel(crop_ref, own_ref, edge_ref, rows_ref):
+def blocks_kernel(crop_ref, own_ref, rows_ref):
     parity = lax.rem(lax.axis_index("space"), 2)
     row, col = iota((64, 1024), 0), iota((64, 1024), 1)
     spread = one_hot(row == 4 * lax.rem(col, 16) + col // LANES)
@@ -66,11 +66,10 @@
         & (lax.rem(e, 4) == m_i)
     )
     packed = mm(one_hot(body | edge), rows_ref[...].astype(BF16)).astype(BF16)
-    own_ref[...] = packed[0:256]
-    edge_ref[...] = packed[256:320]
-
-
-def matrices(f1_ref, f2_ref, w1_ref, w2_ref, wb_ref, sh_ref):
+    own_ref[...] = packed
+
+
+def matrices(f1_ref, f2_ref, w1_ref, w2_ref, wb_ref, sh_ref, f1):
     col = iota((1, 4096), 1)
     half, dp, dq, dr = col // 2048, lax.rem(col // 1024, 2), lax.rem(col // 512, 2), lax.rem(col // 256, 2)
     b = lax.rem(col // 64, 4) - dq
@@ -79,7 +78,9 @@
     inside = (a >= 0) & (a < 3) & (b >= 0) & (b < 3) & (c >= 0) & (c < 3)
     wanted = jnp.where(inside, (a * 9 + b * 3 + c) * 4 + lax.rem(col, 4), -1)
     place = one_hot(iota((108, 4096), 0) == wanted)
-    w1 = mm_tn(f1_ref[...], place).astype(BF16)
+    for tap in range(27):
+        f1[tap * 4 : tap * 4 + 4, :] = f1_ref[tap].astype(F32)
+    w1 = mm_tn(f1[...].astype(BF16), place).astype(BF16)
     for k in range(16):
         w1_ref[k * 32 : (k + 1) * 32, :] = w1[:, k * LANES : (k + 1) * LANES]
 
@@ -184,8 +185,8 @@
 
 
 def near_kernel(own_ref, near_ref, f1_ref, f2_ref,
-                w1_ref, w2_ref, wb_ref, sh_ref, xt_ref, z_ref, maps_ref, mg, xt):
-    matrices(f1_ref, f2_ref, w1_ref, w2_ref, wb_ref, sh_ref)
+                w1_ref, w2_ref, wb_ref, sh_ref, xt_ref, z_ref, maps_ref, mg, xt, f1):
+    matrices(f1_ref, f2_ref, w1_ref, w2_ref, wb_ref, sh_ref, f1)
     half = near_half()
     own, near = own_ref[0:256, :], near_ref[0:256, :]
     mg[0] = merge(own, near, plane_rows(half))
@@ -202,22 +203,21 @@
     first_maps(xt, 1, 1 - half, w1_ref, put(1))
 
 
-def far_kernel(own_ref, far_ref, w1_ref, sh_ref, xt_ref, z_ref, maps_ref, mg, xt):
+def far_kernel(own_ref, far_ref, tail_ref, w1_ref, sh_ref, xt_ref, z_ref, maps_ref, mg, xt):
     index = lax.axis_index("space")
     half = 1 - near_half()
     end = jnp.where(half == 0, index == 0, index == lax.axis_size("space") - 1)
     inside = jnp.where(end, 0.0, 1.0)
-    own, far = own_ref[0:256, :], far_ref[0:256, :] * inside.astype(BF16)
+    own, far = own_ref[0:256, :], far_ref[...] * inside.astype(BF16)
     rows = plane_rows(half)
     n, m = iota((256, 64), 0), iota((256, 64), 1)
     same = (n // 16 == m // 4) & (lax.rem(n, 4) == lax.rem(m, 4)) & (lax.rem(n // 4, 4) == 3 - 3 * half)
-    beyond = (mm(one_hot(same), far_ref[320:384, :]) * inside).astype(BF16)
+    beyond = (mm(one_hot(same), tail_ref[0:64, :]) * inside).astype(BF16)
     mg[0] = merge(own, far, rows)
     mg[1] = merge(far, own, plane_rows(1 - half))
     mg[2] = merge(far, beyond, rows)
     spread(3, mg, xt, sh_ref)
     xt_ref[...] = xt[0]
-    scale = inside * 0.125
 
     def put(k):
         def store(at, rows):
@@ -225,8 +225,8 @@
         return store
 
     first_maps(xt, 0, half, w1_ref, put(0), z_ref)
-    first_maps(xt, 1, 1 - half, w1_ref, put(1), scale=scale)
-    first_maps(xt, 2, half, w1_ref, put(2), scale=scale)
+    first_maps(xt, 1, 1 - half, w1_ref, put(1), scale=inside * 0.125)
+    first_maps(xt, 2, half, w1_ref, put(2), scale=inside * 0.125)
 
 
 def extend(ref, planes, size, sh_ref):
@@ -246,7 +246,7 @@
             ref[k, (q * 4 + target) * size : (q * 4 + target + 1) * size, :] = moved[n * size : (n + 1) * size]
 
 
-def second_kernel(own_ref, near_ref, far_ref, fwd_ref, w1_ref, w2_ref, sh_ref, maps_near, maps_far,
+def second_kernel(near_ref, tail_ref, fwd_ref, cot_ref, w1_ref, w2_ref, sh_ref, maps_near, maps_far,
                   feat_ref, keep_ref, send_ref, g_ext,
                   mg, xt, a_ext, acc, pack):
     half = near_half()
@@ -260,7 +260,7 @@
             a_ext[k, to : to + rows.shape[0], :] = rows
         return store
 
-    mg[0] = merge(near_ref[0:256, :], fwd_ref[...] * near_has_far.astype(BF16), plane_rows(half))
+    mg[0] = merge(near_ref[0:256, :], fwd_ref[0:256, :] * near_has_far.astype(BF16), plane_rows(half))
     spread(1, mg, xt, sh_ref)
     first_maps(xt, 0, half, w1_ref, place(5))
 
@@ -270,8 +270,8 @@
             place(k)(eq * 64, plane[eq * 64 : eq * 64 + 64])
     extend(a_ext, range(6), 32, sh_ref)
 
-    near_cot, far_cot = near_ref[256:320, :].astype(F32), far_ref[256:320, :].astype(F32) * has_far
-    own_cot = own_ref[256:320, :].astype(F32)
+    near_cot, far_cot = fwd_ref[256:320, :].astype(F32), tail_ref[64:128, :].astype(F32) * has_far
+    own_cot = cot_ref[...].astype(F32)
     def second_maps(t, cot, feats=None):
         full, low = cot * 0.125, 0.3 * cot * 0.125
         zs = []
@@ -433,17 +433,13 @@
         pairs += [(k * n_space + i, (k + 1) * n_space + i) for k in range(0, n_dp, 2) for i in (0, n_space - 1)]
     across = both_ways(pairs)
     with jax.named_scope("blocks"):
-        own, edge = call(
-            blocks_kernel,
-            (shape((256, LANES), BF16), shape((64, LANES), BF16)),
-            [pltpu.VMEM((512, LANES), F32)],
-        )(crop)
+        own = call(blocks_kernel, shape((320, LANES), BF16), [pltpu.VMEM((512, LANES), F32)])(crop)
         own, cot = lax.optimization_barrier((own, cotangent.transpose(0, 2, 3, 4, 1).reshape(LANES, 64)))
         cot = cot.T
     with jax.named_scope("halo"):
-        beyond = lax.ppermute(jnp.concatenate([own, cot, lax.ppermute(edge, "space", near)], axis=0), ("dp", "space"), across)
-        own = jnp.concatenate([own, cot], axis=0)
         beside = lax.ppermute(own, "space", near)
+        beyond = lax.ppermute(own[:256], ("dp", "space"), across)
+        tail = lax.ppermute(jnp.concatenate([beside[256:], cot], axis=0), ("dp", "space"), across)
     with jax.named_scope("near"):
         w1, w2, wb, shifts, xt_near, z_near, maps_near = call(
             near_kernel,
@@ -456,20 +452,20 @@
                 shape((4, 256, LANES), F32),
                 shape((2, 128, LANES), BF16),
             ),
-            [pltpu.VMEM((2, 256, LANES), BF16), pltpu.VMEM((2, 576, LANES), BF16)],
+            [pltpu.VMEM((2, 256, LANES), BF16), pltpu.VMEM((2, 576, LANES), BF16), pltpu.VMEM((108, 32), F32)],
             flops=1_000_000_000,
             size=4_000_000,
-        )(own, beside, filter_one.reshape(108, 32), filter_two.reshape(864, 64))
-    beyond, xt_near = lax.optimization_barrier((beyond, xt_near))
+        )(own, beside, filter_one.reshape(27, 4, 32), filter_two.reshape(864, 64))
+    beyond, tail, xt_near = lax.optimization_barrier((beyond, tail, xt_near))
     with jax.named_scope("far"):
-        forward = lax.ppermute(beyond[:256], "space", near)
+        forward = lax.ppermute(jnp.concatenate([beyond, cot], axis=0), "space", near)
         xt_far, z_far, maps_far = call(
             far_kernel,
             (shape((576, LANES), BF16), shape((4, 256, LANES), F32), shape((3, 128, LANES), BF16)),
             [pltpu.VMEM((3, 256, LANES), BF16), pltpu.VMEM((3, 576, LANES), BF16)],
             flops=1_000_000_000,
             size=3_000_000,
-        )(own, beyond, w1, shifts)
+        )(own, beyond, tail, w1, shifts)
     with jax.named_scope("second"):
         feats, keep, send, g_ext = call(
             second_kernel,
@@ -488,7 +484,7 @@
             ],
             flops=4_000_000_000,
             size=6_000_000,
-        )(own, beside, beyond, forward, w1, w2, shifts, maps_near, maps_far)
+        )(beside, tail, forward, cot, w1, w2, shifts, maps_near, maps_far)
         received = lax.ppermute(send, "space", near)
     with jax.named_scope("first"):
         one = call(

time: 38.2 us -> 36.7 us (0.961)
  starting transfers between devices: 13.7 us -> 11.5 us
  waiting for transfers between devices: 10.8 us -> 11.6 us
    ppermute x3, starting transfers between devices: 4.8 us -> 3.05 us  [the longest x1 2.57 us: local(): beyond = lax.ppermute(own[:256], ('dp', 'space'), across)]
    reshape x1 -> x0, local copies, waits for them, and re-layouts: 0.77 us -> none  [local(): filter_one.reshape(108, 32)]
    unnamed x4 -> x6, local copies, waits for them, and re-layouts: 1.87 us -> 2.62 us
    ppermute x3, waiting for transfers between devices: 0.74 us -> 1.42 us  [the longest x1 0.93 us: local(): lax.ppermute(jnp.concatenate([beside[256:], cot], axis=0), ('dp', 'space'...]
    ppermute x6, starting transfers between devices: 7.98 us -> 7.55 us  [total_over_mesh(): lax.ppermute(mine, axes, [(i, i ^ masks[shares[i]][k]) for i in range(siz...]
    ppermute x1, starting transfers between devices: 0.12 us -> 0.52 us  [local(): beside = lax.ppermute(own, 'space', near)]
  transfers between devices with their start and end apart: 12 -> 12, of which waited for: 7 -> 7; matrix products, arithmetic and copies ran while one was open for 5% -> 3% of each run, Pallas kernels for 12% -> 12%
where the time goes in v4:
time: 36.7 us; the launch traced here: 36.4 us
  waiting for transfers between devices  11.6 us (32%)
  starting transfers between devices  11.5 us (31%)
  Pallas kernels  8.9 us (24%)
  local copies, waits for them, and re-layouts  3.56 us (10%)
  between operations  0.75 us (2%)
    ppermute x6, waiting for transfers between devices, total_over_mesh(): lax.ppermute(mine, axes, [(i, i ^ masks[shares[i]][k]) for i in range(siz...  8.93 us
    ppermute x6, starting transfers between devices, total_over_mesh(): lax.ppermute(mine, axes, [(i, i ^ masks[shares[i]][k]) for i in range(siz...  7.55 us
    pallas_call x1, Pallas kernels, local(): call(second_kernel, (shape((64, LANES), BF16), shape((216, 128), F32), sh...  2.66 us
    unnamed x6, local copies, waits for them, and re-layouts  2.62 us
    ppermute x1, starting transfers between devices, local(): beyond = lax.ppermute(own[:256], ('dp', 'space'), across)  2.57 us
    pallas_call x1, Pallas kernels, local(): call(first_kernel, shape((32, 128), F32), [pltpu.VMEM((2, 128, LANES), F3...  1.39 us
    pallas_call x1, Pallas kernels, local(): call(near_kernel, (shape((512, 256), BF16), shape((256, 1536), BF16), sha...  1.28 us
    ppermute x1, waiting for transfers between devices, total_over_mesh(): lax.ppermute(mine, axes, [(i, i ^ 1) for i in range(size)])  1.23 us
  transfers between devices with their start and end apart: 12, of which 7 were waited for; matrix products, arithmetic and copies ran while one was open for 3% of the time, Pallas kernels for 12%

profile of v4, /device:TPU:0, one launch (start us, length us, event | category | flops | bytes accessed | tf_op | source)
XLA Modules:
  0.0 36.4 jit_solution(15146975882107588120)
XLA Ops:
  0.6 0.0 copy-start
  0.6 0.9 %copy-done = bf16[1,4,4,64,64]{4,3,2,1,0:T(8,128)(2,1)S(1)} copy-done((bf16[1,4,4,64,64]{4,3,2,1,0:T(8,128)(2,1)S(1)}, bf16[1,4,4,64,64]{4,3,2,1,0:T(8,128)(2,1)}, u32[]{:S(2)}) %copy-start) | copy-done | bytes 131096
  1.6 0.9 %blocks.1.own_ref = bf16[320,256]{1,0:T(8,128)(2,1)S(1)} custom-call(bf16[1,4,4,64,64]{4,3,2,1,0:T(8,128)(2,1)S(1)} %copy-done), custom_call_target="tpu_custom_call" | custom-call | tf_op jit(solution)/shard_map/blocks/pallas_call | solution.py:436
  2.5 0.5 %collective-permute-start = (bf16[320,256]{1,0:T(8,128)(2,1)S(1)}, bf16[320,256]{1,0:T(8,128)(2,1)S(1)}, u32[]{:S(2)}, u32[]{:S(2)}) collective-permute-start(bf16[320,256]{1,0:T(8,128)(2,1)S(1)} %blocks.1.own_ref), channel_id=1, source_target_pairs={{0,1},{1,0},{2,3},{3,2},{4,5},{5,4},{6,7},{7,6},{8,9},{9,8},{10,11... | collective-permute-start | bytes 491528 | tf_op jit(solution)/shard_map/halo/ppermute | solution.py:440
  3.1 2.6 %collective-permute-start.1 = (bf16[256,256]{1,0:T(8,128)(2,1)S(1)}, bf16[256,256]{1,0:T(8,128)(2,1)S(1)}, u32[]{:S(2)}, u32[]{:S(2)}) collective-permute-start(bf16[256,256]{1,0:T(8,128)(2,1)S(1)} %slice.6), channel_id=1, source_target_pairs={{1,2},{3,4},{5,6},{7,8},{9,10},{11,12},{13,14},{17,18},{19,20},{21... | collective-permute-start | bytes 393224 | tf_op jit(solution)/shard_map/halo/ppermute | solution.py:441
  5.6 0.9 %copy.8 = bf16[256,64]{0,1:T(8,128)(2,1)S(1)} copy(bf16[256,64]{1,0:T(8,128)(2,1)} %bitcast.16) | data formatting | bytes 65536 | tf_op jit(solution)/shard_map/blocks/optimization_barrier | solution.py:437
  6.5 0.0 collective-permute-done.near_ref
  6.6 0.4 %collective-permute-start.2 = (bf16[128,256]{1,0:T(8,128)(2,1)S(1)}, bf16[128,256]{1,0:T(8,128)(2,1)S(1)}, u32[]{:S(2)}, u32[]{:S(2)}) collective-permute-start(bf16[128,256]{1,0:T(8,128)(2,1)S(1)} %pad_maximum_fusion.2), channel_id=1, source_target_pairs={{1,2},{3,4},{5,6},{7,8},{9,10},{11,12},{13,14},{17,18},{19,20},{21... | collective-permute-start | bytes 196616 | tf_op jit(solution)/shard_map/halo/ppermute | solution.py:442
  7.0 0.0 copy-start.1
  7.0 0.9 %copy-done.1 = bf16[3,3,3,32,64]{4,3,2,1,0:T(8,128)(2,1)S(1)} copy-done((bf16[3,3,3,32,64]{4,3,2,1,0:T(8,128)(2,1)S(1)}, bf16[3,3,3,32,64]{4,3,2,1,0:T(8,128)(2,1)}, u32[]{:S(2)}) %copy-start.1) | copy-done | bytes 110616
  7.9 0.0 copy-start.2
  7.9 0.7 %copy-done.2 = bf16[3,3,3,4,32]{4,3,2,1,0:T(4,128)(2,1)S(1)} copy-done((bf16[3,3,3,4,32]{4,3,2,1,0:T(4,128)(2,1)S(1)}, bf16[3,3,3,4,32]{4,3,2,1,0:T(4,128)(2,1)}, u32[]{:S(2)}) %copy-start.2) | copy-done | bytes 6936
  8.7 1.3 %near.1 = (bf16[512,256]{1,0:T(8,128)(2,1)S(1)}, bf16[256,1536]{1,0:T(8,128)(2,1)S(1)}, bf16[128,3072]{1,0:T(8,128)(2,1)S(1)}, bf16[4,256,256]{2,1,0:T(8,128)(2,...) custom-call(bf16[320,256]{1,0:T(8,128)(2,1)S(1)} %blocks.1.own_ref, ...), custom_call_target="tpu_custom_call" | custom-call | flops 1000000000 | bytes 4000000 | tf_op jit(solution)/shard_map/near/pallas_call | solution.py:444
  10.0 0.0 collective-permute-done.1.far_ref
  10.0 0.9 %collective-permute-done.2.tail_ref = bf16[128,256]{1,0:T(8,128)(2,1)S(1)} collective-permute-done((bf16[128,256]{1,0:T(8,128)(2,1)S(1)}, bf16[128,256]{1,0:T(8,128)(2,1)S(1)}, u32[]{:S(2)}, u32[]{:S(2)}) %collective-permute-start.2) | collective-permute-done | bytes 65568 | tf_op jit(solution)/shard_map/halo/ppermute | solution.py:442
  10.9 0.1 collective-permute-start.3
  11.0 0.9 %far.1 = (bf16[576,256]{1,0:T(8,128)(2,1)S(1)}, f32[4,256,256]{2,1,0:T(8,128)S(1)}, bf16[3,128,256]{2,1,0:T(8,128)(2,1)S(1)}) custom-call(bf16[320,256]{1,0:T(8,128)(2,1)S(1)} %blocks.1.own_ref, bf16[256,256]{1,0:T(8,128)(2,1)S(1)} %collective-permute-done.1.far_ref, bf16[128,256]{1,0:T(8,128)(2,1)S(1)} %collective-permute-done.2.tail_ref, ...), custom_call_target="tpu_custom_call" | custom-call | flops 1000000000 | bytes 3000000 | tf_op jit(solution)/shard_map/far/pallas_call | solution.py:462
  11.9 0.5 %collective-permute-done.3.fwd_ref = bf16[320,256]{1,0:T(8,128)(2,1)S(1)} collective-permute-done((bf16[320,256]{1,0:T(8,128)(2,1)S(1)}, bf16[320,256]{1,0:T(8,128)(2,1)S(1)}, u32[]{:S(2)}, u32[]{:S(2)}) %collective-permute-start.3) | collective-permute-done | bytes 163872 | tf_op jit(solution)/shard_map/far/ppermute | solution.py:461
  12.4 2.7 %second.1 = (bf16[64,256]{1,0:T(8,128)(2,1)S(1)}, f32[216,128]{1,0:T(8,128)S(1)}, f32[216,128]{1,0:T(8,128)S(1)}, bf16[4,1024,256]{2,1,0:T(8,128)(2,1)S(1)}) custom-call(bf16[320,256]{1,0:T(8,128)(2,1)S(1)} %collective-permute-done.near_ref, bf16[128,256]{1,0:T(8,128)(2,1)S(1)} %collective-permute-done.2.tail_ref, ...), custom_call_target="tpu_custom_call" | custom-call | flops 4000000000 | bytes 6000000 | tf_op jit(solution)/shard_map/second/pallas_call | solution.py:470
  15.1 0.2 collective-permute-start.4
  15.3 1.4 %first.1 = f32[32,128]{1,0:T(8,128)S(1)} custom-call(bf16[4,1024,256]{2,1,0:T(8,128)(2,1)S(1)} %get-tuple-element.40.g_ext, bf16[128,3072]{1,0:T(8,128)(2,1)S(1)} %get-tuple-element.41.wb_ref, bf16[576,256]{1,0:T(8,128)(2,1)S(1)} %get-tuple-element.42.xt_near, f32[4,256,256]{2,1,0:T(8,128)S(1)} %get-tuple-element.43.z_near, ...), custom_call_target="tpu_custom_call" | custom-call | flops 4000000000 | bytes 6000000 | tf_op jit(solution)/shard_map/first/pallas_call | solution.py:490
  16.7 0.0 collective-permute-done.4
  16.7 1.7 %collective-permute-start.6 = (f32[248,128]{1,0:T(8,128)S(1)}, f32[248,128]{1,0:T(8,128)S(1)}, u32[]{:S(2)}, u32[]{:S(2)}) collective-permute-start(f32[248,128]{1,0:T(8,128)S(1)} %pad_maximum_fusion.1), channel_id=1, source_target_pairs={{0,3},{1,8},{2,11},{3,0},{4,13},{5,6},{6,5},{7,14},{8,1},{9,10},{1... | collective-permute-start | bytes 380936 | tf_op jit(solution)/shard_map/total/ppermute | solution.py:416
  18.4 1.2 %collective-permute-start.7 = (f32[248,128]{1,0:T(8,128)S(1)}, f32[248,128]{1,0:T(8,128)S(1)}, u32[]{:S(2)}, u32[]{:S(2)}) collective-permute-start(f32[248,128]{1,0:T(8,128)S(1)} %pad_maximum_fusion.1), channel_id=1, source_target_pairs={{0,18},{1,13},{2,14},{3,17},{4,8},{5,23},{6,20},{7,11},{8,4},{9,27... | collective-permute-start | bytes 380936 | tf_op jit(solution)/shard_map/total/ppermute | solution.py:416
  19.6 0.2 collective-permute-start.5
  19.8 2.3 %collective-permute-done.6 = f32[248,128]{1,0:T(8,128)S(1)} collective-permute-done((f32[248,128]{1,0:T(8,128)S(1)}, f32[248,128]{1,0:T(8,128)S(1)}, u32[]{:S(2)}, u32[]{:S(2)}) %collective-permute-start.6) | collective-permute-done | bytes 127008 | tf_op jit(solution)/shard_map/total/ppermute | solution.py:416
  22.2 2.0 %collective-permute-done.7 = f32[248,128]{1,0:T(8,128)S(1)} collective-permute-done((f32[248,128]{1,0:T(8,128)S(1)}, f32[248,128]{1,0:T(8,128)S(1)}, u32[]{:S(2)}, u32[]{:S(2)}) %collective-permute-start.7) | collective-permute-done | bytes 127008 | tf_op jit(solution)/shard_map/total/ppermute | solution.py:416
  24.2 0.0 collective-permute-done.5
  24.2 4.1 %collective-permute-start.8 = (f32[248,128]{1,0:T(8,128)S(1)}, f32[248,128]{1,0:T(8,128)S(1)}, u32[]{:S(2)}, u32[]{:S(2)}) collective-permute-start(f32[248,128]{1,0:T(8,128)S(1)} %add_add_fusion.1), channel_id=1, source_target_pairs={{0,12},{1,19},{2,16},{3,15},{4,22},{5,9},{6,10},{7,21},{8,26},{9,5... | collective-permute-start | bytes 380936 | tf_op jit(solution)/shard_map/total/ppermute | solution.py:416
  28.3 0.0 collective-permute-start.10
  28.3 0.4 collective-permute-start.9
  28.7 0.8 %total.2 = bf16[256,64]{1,0:T(8,128)(2,1)} custom-call(bf16[64,256]{1,0:T(8,128)(2,1)S(1)} %get-tuple-element.48.feat_ref), custom_call_target="tpu_custom_call" | custom-call | flops 10000000 | bytes 1000000 | tf_op jit(solution)/shard_map/total/pallas_call | solution.py:419
  29.5 1.8 %collective-permute-done.8 = f32[248,128]{1,0:T(8,128)S(1)} collective-permute-done((f32[248,128]{1,0:T(8,128)S(1)}, f32[248,128]{1,0:T(8,128)S(1)}, u32[]{:S(2)}, u32[]{:S(2)}) %collective-permute-start.8) | collective-permute-done | bytes 127008 | tf_op jit(solution)/shard_map/total/ppermute | solution.py:416
  31.3 2.7 %collective-permute-done.10 = f32[248,128]{1,0:T(8,128)S(1)} collective-permute-done((f32[248,128]{1,0:T(8,128)S(1)}, f32[248,128]{1,0:T(8,128)S(1)}, u32[]{:S(2)}, u32[]{:S(2)}) %collective-permute-start.10) | collective-permute-done | bytes 127008 | tf_op jit(solution)/shard_map/total/ppermute | solution.py:416
  34.0 0.0 collective-permute-done.9
  34.1 0.2 collective-permute-start.11
  34.2 1.2 %collective-permute-done.11.other_ref = f32[248,128]{1,0:T(8,128)S(1)} collective-permute-done((f32[248,128]{1,0:T(8,128)S(1)}, f32[248,128]{1,0:T(8,128)S(1)}, u32[]{:S(2)}, u32[]{:S(2)}) %collective-permute-start.11) | collective-permute-done | bytes 127008 | tf_op jit(solution)/shard_map/total/ppermute | solution.py:426
  35.5 0.9 %total.3 = (f32[27,4,32]{2,1,0:T(4,128)}, f32[864,64]{1,0:T(8,128)}) custom-call(f32[248,128]{1,0:T(8,128)S(1)} %add_add_fusion.mine_ref, f32[248,128]{1,0:T(8,128)S(1)} %collective-permute-done.11.other_ref), custom_call_target="tpu_custom_call" | custom-call | tf_op jit(solution)/shard_map/total/pallas_call | solution.py:500
  (8 shorter events, 0.1 us)
Async XLA Ops:
  0.6 1.0 %copy-start = (bf16[1,4,4,64,64]{4,3,2,1,0:T(8,128)(2,1)S(1)}, bf16[1,4,4,64,64]{4,3,2,1,0:T(8,128)(2,1)}, u32[]{:S(2)}) copy-start(bf16[1,4,4,64,64]{4,3,2,1,0:T(8,128)(2,1)} %crop_ref.1) | copy-start | bytes 393220
  2.5 4.0 %collective-permute-start = (bf16[320,256]{1,0:T(8,128)(2,1)S(1)}, bf16[320,256]{1,0:T(8,128)(2,1)S(1)}, u32[]{:S(2)}, u32[]{:S(2)}) collective-permute-start(bf16[320,256]{1,0:T(8,128)(2,1)S(1)} %blocks.1.own_ref), channel_id=1, source_target_pairs={{0,1},{1,0},{2,3},{3,2},{4,5},{5,4},{6,7},{7,6},{8,9},{9,8},{10,11... | collective-permute-start | bytes 491528 | tf_op jit(solution)/shard_map/halo/ppermute | solution.py:440
  3.1 6.9 %collective-permute-start.1 = (bf16[256,256]{1,0:T(8,128)(2,1)S(1)}, bf16[256,256]{1,0:T(8,128)(2,1)S(1)}, u32[]{:S(2)}, u32[]{:S(2)}) collective-permute-start(bf16[256,256]{1,0:T(8,128)(2,1)S(1)} %slice.6), channel_id=1, source_target_pairs={{1,2},{3,4},{5,6},{7,8},{9,10},{11,12},{13,14},{17,18},{19,20},{21... | collective-permute-start | bytes 393224 | tf_op jit(solution)/shard_map/halo/ppermute | solution.py:441
  6.6 4.3 %collective-permute-start.2 = (bf16[128,256]{1,0:T(8,128)(2,1)S(1)}, bf16[128,256]{1,0:T(8,128)(2,1)S(1)}, u32[]{:S(2)}, u32[]{:S(2)}) collective-permute-start(bf16[128,256]{1,0:T(8,128)(2,1)S(1)} %pad_maximum_fusion.2), channel_id=1, source_target_pairs={{1,2},{3,4},{5,6},{7,8},{9,10},{11,12},{13,14},{17,18},{19,20},{21... | collective-permute-start | bytes 196616 | tf_op jit(solution)/shard_map/halo/ppermute | solution.py:442
  7.0 0.9 %copy-start.1 = (bf16[3,3,3,32,64]{4,3,2,1,0:T(8,128)(2,1)S(1)}, bf16[3,3,3,32,64]{4,3,2,1,0:T(8,128)(2,1)}, u32[]{:S(2)}) copy-start(bf16[3,3,3,32,64]{4,3,2,1,0:T(8,128)(2,1)} %param.6) | copy-start | bytes 331780
  7.9 0.7 %copy-start.2 = (bf16[3,3,3,4,32]{4,3,2,1,0:T(4,128)(2,1)S(1)}, bf16[3,3,3,4,32]{4,3,2,1,0:T(4,128)(2,1)}, u32[]{:S(2)}) copy-start(bf16[3,3,3,4,32]{4,3,2,1,0:T(4,128)(2,1)} %param.5) | copy-start | bytes 20740
  10.9 1.5 %collective-permute-start.3 = (bf16[320,256]{1,0:T(8,128)(2,1)S(1)}, bf16[320,256]{1,0:T(8,128)(2,1)S(1)}, u32[]{:S(2)}, u32[]{:S(2)}) collective-permute-start(bf16[320,256]{1,0:T(8,128)(2,1)S(1)} %pad_maximum_fusion), channel_id=1, source_target_pairs={{0,1},{1,0},{2,3},{3,2},{4,5},{5,4},{6,7},{7,6},{8,9},{9,8},{10,11... | collective-permute-start | bytes 491528 | tf_op jit(solution)/shard_map/far/ppermute | solution.py:461
  15.1 1.6 %collective-permute-start.4 = (f32[216,128]{1,0:T(8,128)S(1)}, f32[216,128]{1,0:T(8,128)S(1)}, u32[]{:S(2)}, u32[]{:S(2)}) collective-permute-start(f32[216,128]{1,0:T(8,128)S(1)} %get-tuple-element.39), channel_id=1, source_target_pairs={{0,1},{1,0},{2,3},{3,2},{4,5},{5,4},{6,7},{7,6},{8,9},{9,8},{10,11... | collective-permute-start | bytes 331784 | tf_op jit(solution)/shard_map/second/ppermute | solution.py:488
  16.7 5.5 %collective-permute-start.6 = (f32[248,128]{1,0:T(8,128)S(1)}, f32[248,128]{1,0:T(8,128)S(1)}, u32[]{:S(2)}, u32[]{:S(2)}) collective-permute-start(f32[248,128]{1,0:T(8,128)S(1)} %pad_maximum_fusion.1), channel_id=1, source_target_pairs={{0,3},{1,8},{2,11},{3,0},{4,13},{5,6},{6,5},{7,14},{8,1},{9,10},{1... | collective-permute-start | bytes 380936 | tf_op jit(solution)/shard_map/total/ppermute | solution.py:416
  18.4 5.8 %collective-permute-start.7 = (f32[248,128]{1,0:T(8,128)S(1)}, f32[248,128]{1,0:T(8,128)S(1)}, u32[]{:S(2)}, u32[]{:S(2)}) collective-permute-start(f32[248,128]{1,0:T(8,128)S(1)} %pad_maximum_fusion.1), channel_id=1, source_target_pairs={{0,18},{1,13},{2,14},{3,17},{4,8},{5,23},{6,20},{7,11},{8,4},{9,27... | collective-permute-start | bytes 380936 | tf_op jit(solution)/shard_map/total/ppermute | solution.py:416
  19.6 4.6 %collective-permute-start.5 = (f32[248,128]{1,0:T(8,128)S(1)}, f32[248,128]{1,0:T(8,128)S(1)}, u32[]{:S(2)}, u32[]{:S(2)}) collective-permute-start(f32[248,128]{1,0:T(8,128)S(1)} %pad_maximum_fusion.1), channel_id=1, source_target_pairs={{0,17},{1,4},{2,7},{3,18},{4,1},{5,20},{6,23},{7,2},{8,13},{9,24},... | collective-permute-start | bytes 380936 | tf_op jit(solution)/shard_map/total/ppermute | solution.py:416
  24.2 7.1 %collective-permute-start.8 = (f32[248,128]{1,0:T(8,128)S(1)}, f32[248,128]{1,0:T(8,128)S(1)}, u32[]{:S(2)}, u32[]{:S(2)}) collective-permute-start(f32[248,128]{1,0:T(8,128)S(1)} %add_add_fusion.1), channel_id=1, source_target_pairs={{0,12},{1,19},{2,16},{3,15},{4,22},{5,9},{6,10},{7,21},{8,26},{9,5... | collective-permute-start | bytes 380936 | tf_op jit(solution)/shard_map/total/ppermute | solution.py:416
  28.3 5.7 %collective-permute-start.10 = (f32[248,128]{1,0:T(8,128)S(1)}, f32[248,128]{1,0:T(8,128)S(1)}, u32[]{:S(2)}, u32[]{:S(2)}) collective-permute-start(f32[248,128]{1,0:T(8,128)S(1)} %add_add_fusion.1), channel_id=1, source_target_pairs={{0,5},{1,16},{2,19},{3,6},{4,21},{5,0},{6,3},{7,22},{8,25},{9,12},... | collective-permute-start | bytes 380936 | tf_op jit(solution)/shard_map/total/ppermute | solution.py:416
  28.3 5.7 %collective-permute-start.9 = (f32[248,128]{1,0:T(8,128)S(1)}, f32[248,128]{1,0:T(8,128)S(1)}, u32[]{:S(2)}, u32[]{:S(2)}) collective-permute-start(f32[248,128]{1,0:T(8,128)S(1)} %add_add_fusion.1), channel_id=1, source_target_pairs={{0,9},{1,2},{2,1},{3,10},{4,7},{5,12},{6,15},{7,4},{8,11},{9,0},{1... | collective-permute-start | bytes 380936 | tf_op jit(solution)/shard_map/total/ppermute | solution.py:416
  34.1 1.4 %collective-permute-start.11 = (f32[248,128]{1,0:T(8,128)S(1)}, f32[248,128]{1,0:T(8,128)S(1)}, u32[]{:S(2)}, u32[]{:S(2)}) collective-permute-start(f32[248,128]{1,0:T(8,128)S(1)} %add_add_fusion.mine_ref), channel_id=1, source_target_pairs={{0,1},{1,0},{2,3},{3,2},{4,5},{5,4},{6,7},{7,6},{8,9},{9,8},{10,11... | collective-permute-start | bytes 380936 | tf_op jit(solution)/shard_map/total/ppermute | solution.py:426

commit v5 on v4

--- a/solution.py
+++ b/solution.py
@@ -10,7 +10,7 @@
 F32 = jnp.float32
 BF16 = jnp.bfloat16
 LANES = 256
-ORDERS = (((0, 1, 2), (0, 1, 2)), ((1, 0, 2), (1, 0, 2)))
+ORDERS = (((0, 2, 1), (0, 2, 1)), ((1, 0, 2), (1, 0, 2)))
 VMEM = pl.BlockSpec(memory_space=pltpu.VMEM)
 
 
@@ -36,7 +36,7 @@
 
 def blocks_kernel(crop_ref, own_ref, rows_ref):
     parity = lax.rem(lax.axis_index("space"), 2)
-    row, col = iota((64, 1024), 0), iota((64, 1024), 1)
+    row, col = iota((64, 1), 0), iota((1, 1024), 1)
     spread = one_hot(row == 4 * lax.rem(col, 16) + col // LANES)
     own = (row // 4) == lax.rem(col, LANES) // 16
     for i in range(4):
@@ -48,24 +48,12 @@
             for rr in range(4):
                 at = rr * 128 + (i * 4 + p) * 8
                 rows_ref[at : at + 8, :] = part[:, rr * LANES : (rr + 1) * LANES]
-    n, m = iota((320, 512), 0), iota((320, 512), 1)
-    m_rr, m_i, m_p, m_qq = m // 128, lax.rem(m, 128) // 32, lax.rem(m // 8, 4), lax.rem(m, 4)
-    body = (
-        (n < 256)
-        & (n // 64 == m_qq)
-        & (lax.rem(n // 16, 4) == m_rr)
-        & (lax.rem(n // 4, 4) == m_p)
-        & (lax.rem(n, 4) == m_i)
-    )
+    n, m = iota((320, 1), 0), iota((1, 512), 1)
     e = n - 256
-    edge = (
-        (n >= 256)
-        & (e // 16 == m_qq)
-        & (lax.rem(e // 4, 4) == m_rr)
-        & (3 - 3 * parity == m_p)
-        & (lax.rem(e, 4) == m_i)
-    )
-    packed = mm(one_hot(body | edge), rows_ref[...].astype(BF16)).astype(BF16)
+    body = lax.rem(n // 16, 4) * 64 + lax.rem(n, 4) * 16 + lax.rem(n // 4, 4) * 4 + n // 64
+    edge = lax.rem(e // 4, 4) * 64 + lax.rem(e, 4) * 16 + (3 - 3 * parity) * 4 + e // 16
+    held = m // 128 * 64 + lax.rem(m, 128) // 32 * 16 + lax.rem(m // 8, 4) * 4 + lax.rem(m, 4)
+    packed = mm(one_hot(jnp.where(n < 256, body, edge) == held), rows_ref[...].astype(BF16)).astype(BF16)
     own_ref[...] = packed
 
 
@@ -135,7 +123,7 @@
 
 def plane_rows(half):
     plane = 3 - 3 * half
-    return one_hot(lax.rem(iota((256, LANES), 0) // 4, 4) == plane)
+    return one_hot(jnp.broadcast_to(lax.rem(iota((256, 1), 0) // 4, 4), (256, LANES)) == plane)
 
 
 def merge(block, other, rows):
@@ -210,8 +198,8 @@
     inside = jnp.where(end, 0.0, 1.0)
     own, far = own_ref[0:256, :], far_ref[...] * inside.astype(BF16)
     rows = plane_rows(half)
-    n, m = iota((256, 64), 0), iota((256, 64), 1)
-    same = (n // 16 == m // 4) & (lax.rem(n, 4) == lax.rem(m, 4)) & (lax.rem(n // 4, 4) == 3 - 3 * half)
+    n, m = iota((256, 1), 0), iota((1, 64), 1)
+    same = jnp.where(lax.rem(n // 4, 4) == 3 - 3 * half, n // 16 * 4 + lax.rem(n, 4), -1) == m
     beyond = (mm(one_hot(same), tail_ref[0:64, :]) * inside).astype(BF16)
     mg[0] = merge(own, far, rows)
     mg[1] = merge(far, own, plane_rows(1 - half))

time: 36.7 us -> 36.4 us (level)
  waiting for transfers between devices: 11.6 us -> 11 us
  starting transfers between devices: 11.5 us -> 11.9 us
    ppermute x6, waiting for transfers between devices: 8.93 us -> 8.54 us  [total_over_mesh(): lax.ppermute(mine, axes, [(i, i ^ masks[shares[i]][k]) for i in range(siz...]
where the time goes in v5:
time: 36.4 us; the launch traced here: 36.1 us
  starting transfers between devices  11.9 us (33%)
  waiting for transfers between devices  11 us (30%)
  Pallas kernels  8.9 us (24%)
  local copies, waits for them, and re-layouts  3.56 us (10%)
  between operations  0.75 us (2%)
    ppermute x6, waiting for transfers between devices, total_over_mesh(): lax.ppermute(mine, axes, [(i, i ^ masks[shares[i]][k]) for i in range(siz...  8.54 us
    ppermute x6, starting transfers between devices, total_over_mesh(): lax.ppermute(mine, axes, [(i, i ^ masks[shares[i]][k]) for i in range(siz...  7.66 us
    pallas_call x1, Pallas kernels, local(): call(second_kernel, (shape((64, LANES), BF16), shape((216, 128), F32), sh...  2.66 us
    unnamed x6, local copies, waits for them, and re-layouts  2.62 us
    ppermute x1, starting transfers between devices, local(): beyond = lax.ppermute(own[:256], ('dp', 'space'), across)  2.57 us
    pallas_call x1, Pallas kernels, local(): call(first_kernel, shape((32, 128), F32), [pltpu.VMEM((2, 128, LANES), F3...  1.38 us
    pallas_call x1, Pallas kernels, local(): call(near_kernel, (shape((512, 256), BF16), shape((256, 1536), BF16), sha...  1.28 us
    ppermute x1, waiting for transfers between devices, total_over_mesh(): lax.ppermute(mine, axes, [(i, i ^ 1) for i in range(size)])  0.99 us
  transfers between devices with their start and end apart: 12, of which 7 were waited for; matrix products, arithmetic and copies ran while one was open for 3% of the time, Pallas kernels for 12%

profile of v5, /device:TPU:0, one launch (start us, length us, event | category | flops | bytes accessed | tf_op | source)
XLA Modules:
  0.0 36.1 jit_solution(17961942026923463761)
XLA Ops:
  0.6 0.0 copy-start
  0.6 0.9 %copy-done = bf16[1,4,4,64,64]{4,3,2,1,0:T(8,128)(2,1)S(1)} copy-done((bf16[1,4,4,64,64]{4,3,2,1,0:T(8,128)(2,1)S(1)}, bf16[1,4,4,64,64]{4,3,2,1,0:T(8,128)(2,1)}, u32[]{:S(2)}) %copy-start) | copy-done | bytes 131096
  1.6 0.9 %blocks.1.own_ref = bf16[320,256]{1,0:T(8,128)(2,1)S(1)} custom-call(bf16[1,4,4,64,64]{4,3,2,1,0:T(8,128)(2,1)S(1)} %copy-done), custom_call_target="tpu_custom_call" | custom-call | tf_op jit(solution)/shard_map/blocks/pallas_call | solution.py:424
  2.5 0.5 %collective-permute-start = (bf16[320,256]{1,0:T(8,128)(2,1)S(1)}, bf16[320,256]{1,0:T(8,128)(2,1)S(1)}, u32[]{:S(2)}, u32[]{:S(2)}) collective-permute-start(bf16[320,256]{1,0:T(8,128)(2,1)S(1)} %blocks.1.own_ref), channel_id=1, source_target_pairs={{0,1},{1,0},{2,3},{3,2},{4,5},{5,4},{6,7},{7,6},{8,9},{9,8},{10,11... | collective-permute-start | bytes 491528 | tf_op jit(solution)/shard_map/halo/ppermute | solution.py:428
  3.1 2.6 %collective-permute-start.1 = (bf16[256,256]{1,0:T(8,128)(2,1)S(1)}, bf16[256,256]{1,0:T(8,128)(2,1)S(1)}, u32[]{:S(2)}, u32[]{:S(2)}) collective-permute-start(bf16[256,256]{1,0:T(8,128)(2,1)S(1)} %slice.6), channel_id=1, source_target_pairs={{1,2},{3,4},{5,6},{7,8},{9,10},{11,12},{13,14},{17,18},{19,20},{21... | collective-permute-start | bytes 393224 | tf_op jit(solution)/shard_map/halo/ppermute | solution.py:429
  5.6 0.9 %copy.8 = bf16[256,64]{0,1:T(8,128)(2,1)S(1)} copy(bf16[256,64]{1,0:T(8,128)(2,1)} %bitcast.16) | data formatting | bytes 65536 | tf_op jit(solution)/shard_map/blocks/optimization_barrier | solution.py:425
  6.5 0.0 collective-permute-done.near_ref
  6.6 0.4 %collective-permute-start.2 = (bf16[128,256]{1,0:T(8,128)(2,1)S(1)}, bf16[128,256]{1,0:T(8,128)(2,1)S(1)}, u32[]{:S(2)}, u32[]{:S(2)}) collective-permute-start(bf16[128,256]{1,0:T(8,128)(2,1)S(1)} %pad_maximum_fusion.2), channel_id=1, source_target_pairs={{1,2},{3,4},{5,6},{7,8},{9,10},{11,12},{13,14},{17,18},{19,20},{21... | collective-permute-start | bytes 196616 | tf_op jit(solution)/shard_map/halo/ppermute | solution.py:430
  7.0 0.0 copy-start.1
  7.0 0.9 %copy-done.1 = bf16[3,3,3,32,64]{4,3,2,1,0:T(8,128)(2,1)S(1)} copy-done((bf16[3,3,3,32,64]{4,3,2,1,0:T(8,128)(2,1)S(1)}, bf16[3,3,3,32,64]{4,3,2,1,0:T(8,128)(2,1)}, u32[]{:S(2)}) %copy-start.1) | copy-done | bytes 110616
  7.9 0.0 copy-start.2
  7.9 0.7 %copy-done.2 = bf16[3,3,3,4,32]{4,3,2,1,0:T(4,128)(2,1)S(1)} copy-done((bf16[3,3,3,4,32]{4,3,2,1,0:T(4,128)(2,1)S(1)}, bf16[3,3,3,4,32]{4,3,2,1,0:T(4,128)(2,1)}, u32[]{:S(2)}) %copy-start.2) | copy-done | bytes 6936
  8.7 1.3 %near.1 = (bf16[512,256]{1,0:T(8,128)(2,1)S(1)}, bf16[256,1536]{1,0:T(8,128)(2,1)S(1)}, bf16[128,3072]{1,0:T(8,128)(2,1)S(1)}, bf16[4,256,256]{2,1,0:T(8,128)(2,...) custom-call(bf16[320,256]{1,0:T(8,128)(2,1)S(1)} %blocks.1.own_ref, ...), custom_call_target="tpu_custom_call" | custom-call | flops 1000000000 | bytes 4000000 | tf_op jit(solution)/shard_map/near/pallas_call | solution.py:432
  10.0 0.0 collective-permute-done.1.far_ref
  10.0 0.9 %collective-permute-done.2.tail_ref = bf16[128,256]{1,0:T(8,128)(2,1)S(1)} collective-permute-done((bf16[128,256]{1,0:T(8,128)(2,1)S(1)}, bf16[128,256]{1,0:T(8,128)(2,1)S(1)}, u32[]{:S(2)}, u32[]{:S(2)}) %collective-permute-start.2) | collective-permute-done | bytes 65568 | tf_op jit(solution)/shard_map/halo/ppermute | solution.py:430
  10.9 0.1 collective-permute-start.3
  11.0 0.9 %far.1 = (bf16[576,256]{1,0:T(8,128)(2,1)S(1)}, f32[4,256,256]{2,1,0:T(8,128)S(1)}, bf16[3,128,256]{2,1,0:T(8,128)(2,1)S(1)}) custom-call(bf16[320,256]{1,0:T(8,128)(2,1)S(1)} %blocks.1.own_ref, bf16[256,256]{1,0:T(8,128)(2,1)S(1)} %collective-permute-done.1.far_ref, bf16[128,256]{1,0:T(8,128)(2,1)S(1)} %collective-permute-done.2.tail_ref, ...), custom_call_target="tpu_custom_call" | custom-call | flops 1000000000 | bytes 3000000 | tf_op jit(solution)/shard_map/far/pallas_call | solution.py:450
  11.9 0.5 %collective-permute-done.3.fwd_ref = bf16[320,256]{1,0:T(8,128)(2,1)S(1)} collective-permute-done((bf16[320,256]{1,0:T(8,128)(2,1)S(1)}, bf16[320,256]{1,0:T(8,128)(2,1)S(1)}, u32[]{:S(2)}, u32[]{:S(2)}) %collective-permute-start.3) | collective-permute-done | bytes 163872 | tf_op jit(solution)/shard_map/far/ppermute | solution.py:449
  12.4 2.7 %second.1 = (bf16[64,256]{1,0:T(8,128)(2,1)S(1)}, f32[216,128]{1,0:T(8,128)S(1)}, f32[216,128]{1,0:T(8,128)S(1)}, bf16[4,1024,256]{2,1,0:T(8,128)(2,1)S(1)}) custom-call(bf16[320,256]{1,0:T(8,128)(2,1)S(1)} %collective-permute-done.near_ref, bf16[128,256]{1,0:T(8,128)(2,1)S(1)} %collective-permute-done.2.tail_ref, ...), custom_call_target="tpu_custom_call" | custom-call | flops 4000000000 | bytes 6000000 | tf_op jit(solution)/shard_map/second/pallas_call | solution.py:458
  15.1 0.2 collective-permute-start.4
  15.3 1.4 %first.1 = f32[32,128]{1,0:T(8,128)S(1)} custom-call(bf16[4,1024,256]{2,1,0:T(8,128)(2,1)S(1)} %get-tuple-element.40.g_ext, bf16[128,3072]{1,0:T(8,128)(2,1)S(1)} %get-tuple-element.41.wb_ref, bf16[576,256]{1,0:T(8,128)(2,1)S(1)} %get-tuple-element.42.xt_near, f32[4,256,256]{2,1,0:T(8,128)S(1)} %get-tuple-element.43.z_near, ...), custom_call_target="tpu_custom_call" | custom-call | flops 4000000000 | bytes 6000000 | tf_op jit(solution)/shard_map/first/pallas_call | solution.py:478
  16.7 0.0 collective-permute-done.4
  16.7 2.9 %collective-permute-start.6 = (f32[248,128]{1,0:T(8,128)S(1)}, f32[248,128]{1,0:T(8,128)S(1)}, u32[]{:S(2)}, u32[]{:S(2)}) collective-permute-start(f32[248,128]{1,0:T(8,128)S(1)} %pad_maximum_fusion.1), channel_id=1, source_target_pairs={{0,18},{1,13},{2,14},{3,17},{4,8},{5,23},{6,20},{7,11},{8,4},{9,27... | collective-permute-start | bytes 380936 | tf_op jit(solution)/shard_map/total/ppermute | solution.py:404
  19.6 0.0 collective-permute-start.7
  19.6 0.4 %collective-permute-start.5 = (f32[248,128]{1,0:T(8,128)S(1)}, f32[248,128]{1,0:T(8,128)S(1)}, u32[]{:S(2)}, u32[]{:S(2)}) collective-permute-start(f32[248,128]{1,0:T(8,128)S(1)} %pad_maximum_fusion.1), channel_id=1, source_target_pairs={{0,17},{1,4},{2,7},{3,18},{4,1},{5,20},{6,23},{7,2},{8,13},{9,24},... | collective-permute-start | bytes 380936 | tf_op jit(solution)/shard_map/total/ppermute | solution.py:404
  20.0 2.6 %collective-permute-done.6 = f32[248,128]{1,0:T(8,128)S(1)} collective-permute-done((f32[248,128]{1,0:T(8,128)S(1)}, f32[248,128]{1,0:T(8,128)S(1)}, u32[]{:S(2)}, u32[]{:S(2)}) %collective-permute-start.6) | collective-permute-done | bytes 127008 | tf_op jit(solution)/shard_map/total/ppermute | solution.py:404
  22.6 1.4 %collective-permute-done.7 = f32[248,128]{1,0:T(8,128)S(1)} collective-permute-done((f32[248,128]{1,0:T(8,128)S(1)}, f32[248,128]{1,0:T(8,128)S(1)}, u32[]{:S(2)}, u32[]{:S(2)}) %collective-permute-start.7) | collective-permute-done | bytes 127008 | tf_op jit(solution)/shard_map/total/ppermute | solution.py:404
  23.9 0.0 collective-permute-done.5
  24.0 4.0 %collective-permute-start.8 = (f32[248,128]{1,0:T(8,128)S(1)}, f32[248,128]{1,0:T(8,128)S(1)}, u32[]{:S(2)}, u32[]{:S(2)}) collective-permute-start(f32[248,128]{1,0:T(8,128)S(1)} %add_add_fusion.1), channel_id=1, source_target_pairs={{0,12},{1,19},{2,16},{3,15},{4,22},{5,9},{6,10},{7,21},{8,26},{9,5... | collective-permute-start | bytes 380936 | tf_op jit(solution)/shard_map/total/ppermute | solution.py:404
  28.0 0.0 collective-permute-start.10
  28.0 0.4 collective-permute-start.9
  28.4 0.8 %total.2 = bf16[256,64]{1,0:T(8,128)(2,1)} custom-call(bf16[64,256]{1,0:T(8,128)(2,1)S(1)} %get-tuple-element.48.feat_ref), custom_call_target="tpu_custom_call" | custom-call | flops 10000000 | bytes 1000000 | tf_op jit(solution)/shard_map/total/pallas_call | solution.py:407
  29.2 1.8 %collective-permute-done.8 = f32[248,128]{1,0:T(8,128)S(1)} collective-permute-done((f32[248,128]{1,0:T(8,128)S(1)}, f32[248,128]{1,0:T(8,128)S(1)}, u32[]{:S(2)}, u32[]{:S(2)}) %collective-permute-start.8) | collective-permute-done | bytes 127008 | tf_op jit(solution)/shard_map/total/ppermute | solution.py:404
  31.0 2.7 %collective-permute-done.10 = f32[248,128]{1,0:T(8,128)S(1)} collective-permute-done((f32[248,128]{1,0:T(8,128)S(1)}, f32[248,128]{1,0:T(8,128)S(1)}, u32[]{:S(2)}, u32[]{:S(2)}) %collective-permute-start.10) | collective-permute-done | bytes 127008 | tf_op jit(solution)/shard_map/total/ppermute | solution.py:404
  33.7 0.0 collective-permute-done.9
  33.8 0.4 %collective-permute-start.11 = (f32[248,128]{1,0:T(8,128)S(1)}, f32[248,128]{1,0:T(8,128)S(1)}, u32[]{:S(2)}, u32[]{:S(2)}) collective-permute-start(f32[248,128]{1,0:T(8,128)S(1)} %add_add_fusion.mine_ref), channel_id=1, source_target_pairs={{0,1},{1,0},{2,3},{3,2},{4,5},{5,4},{6,7},{7,6},{8,9},{9,8},{10,11... | collective-permute-start | bytes 380936 | tf_op jit(solution)/shard_map/total/ppermute | solution.py:414
  34.2 1.0 %collective-permute-done.11.other_ref = f32[248,128]{1,0:T(8,128)S(1)} collective-permute-done((f32[248,128]{1,0:T(8,128)S(1)}, f32[248,128]{1,0:T(8,128)S(1)}, u32[]{:S(2)}, u32[]{:S(2)}) %collective-permute-start.11) | collective-permute-done | bytes 127008 | tf_op jit(solution)/shard_map/total/ppermute | solution.py:414
  35.2 0.9 %total.3 = (f32[27,4,32]{2,1,0:T(4,128)}, f32[864,64]{1,0:T(8,128)}) custom-call(f32[248,128]{1,0:T(8,128)S(1)} %add_add_fusion.mine_ref, f32[248,128]{1,0:T(8,128)S(1)} %collective-permute-done.11.other_ref), custom_call_target="tpu_custom_call" | custom-call | tf_op jit(solution)/shard_map/total/pallas_call | solution.py:488
  (8 shorter events, 0.1 us)
Async XLA Ops:
  0.6 1.0 %copy-start = (bf16[1,4,4,64,64]{4,3,2,1,0:T(8,128)(2,1)S(1)}, bf16[1,4,4,64,64]{4,3,2,1,0:T(8,128)(2,1)}, u32[]{:S(2)}) copy-start(bf16[1,4,4,64,64]{4,3,2,1,0:T(8,128)(2,1)} %crop_ref.1) | copy-start | bytes 393220
  2.5 4.0 %collective-permute-start = (bf16[320,256]{1,0:T(8,128)(2,1)S(1)}, bf16[320,256]{1,0:T(8,128)(2,1)S(1)}, u32[]{:S(2)}, u32[]{:S(2)}) collective-permute-start(bf16[320,256]{1,0:T(8,128)(2,1)S(1)} %blocks.1.own_ref), channel_id=1, source_target_pairs={{0,1},{1,0},{2,3},{3,2},{4,5},{5,4},{6,7},{7,6},{8,9},{9,8},{10,11... | collective-permute-start | bytes 491528 | tf_op jit(solution)/shard_map/halo/ppermute | solution.py:428
  3.1 6.9 %collective-permute-start.1 = (bf16[256,256]{1,0:T(8,128)(2,1)S(1)}, bf16[256,256]{1,0:T(8,128)(2,1)S(1)}, u32[]{:S(2)}, u32[]{:S(2)}) collective-permute-start(bf16[256,256]{1,0:T(8,128)(2,1)S(1)} %slice.6), channel_id=1, source_target_pairs={{1,2},{3,4},{5,6},{7,8},{9,10},{11,12},{13,14},{17,18},{19,20},{21... | collective-permute-start | bytes 393224 | tf_op jit(solution)/shard_map/halo/ppermute | solution.py:429
  6.6 4.3 %collective-permute-start.2 = (bf16[128,256]{1,0:T(8,128)(2,1)S(1)}, bf16[128,256]{1,0:T(8,128)(2,1)S(1)}, u32[]{:S(2)}, u32[]{:S(2)}) collective-permute-start(bf16[128,256]{1,0:T(8,128)(2,1)S(1)} %pad_maximum_fusion.2), channel_id=1, source_target_pairs={{1,2},{3,4},{5,6},{7,8},{9,10},{11,12},{13,14},{17,18},{19,20},{21... | collective-permute-start | bytes 196616 | tf_op jit(solution)/shard_map/halo/ppermute | solution.py:430
  7.0 0.9 %copy-start.1 = (bf16[3,3,3,32,64]{4,3,2,1,0:T(8,128)(2,1)S(1)}, bf16[3,3,3,32,64]{4,3,2,1,0:T(8,128)(2,1)}, u32[]{:S(2)}) copy-start(bf16[3,3,3,32,64]{4,3,2,1,0:T(8,128)(2,1)} %param.6) | copy-start | bytes 331780
  7.9 0.7 %copy-start.2 = (bf16[3,3,3,4,32]{4,3,2,1,0:T(4,128)(2,1)S(1)}, bf16[3,3,3,4,32]{4,3,2,1,0:T(4,128)(2,1)}, u32[]{:S(2)}) copy-start(bf16[3,3,3,4,32]{4,3,2,1,0:T(4,128)(2,1)} %param.5) | copy-start | bytes 20740
  10.9 1.5 %collective-permute-start.3 = (bf16[320,256]{1,0:T(8,128)(2,1)S(1)}, bf16[320,256]{1,0:T(8,128)(2,1)S(1)}, u32[]{:S(2)}, u32[]{:S(2)}) collective-permute-start(bf16[320,256]{1,0:T(8,128)(2,1)S(1)} %pad_maximum_fusion), channel_id=1, source_target_pairs={{0,1},{1,0},{2,3},{3,2},{4,5},{5,4},{6,7},{7,6},{8,9},{9,8},{10,11... | collective-permute-start | bytes 491528 | tf_op jit(solution)/shard_map/far/ppermute | solution.py:449
  15.1 1.6 %collective-permute-start.4 = (f32[216,128]{1,0:T(8,128)S(1)}, f32[216,128]{1,0:T(8,128)S(1)}, u32[]{:S(2)}, u32[]{:S(2)}) collective-permute-start(f32[216,128]{1,0:T(8,128)S(1)} %get-tuple-element.39), channel_id=1, source_target_pairs={{0,1},{1,0},{2,3},{3,2},{4,5},{5,4},{6,7},{7,6},{8,9},{9,8},{10,11... | collective-permute-start | bytes 331784 | tf_op jit(solution)/shard_map/second/ppermute | solution.py:476
  16.7 5.9 %collective-permute-start.6 = (f32[248,128]{1,0:T(8,128)S(1)}, f32[248,128]{1,0:T(8,128)S(1)}, u32[]{:S(2)}, u32[]{:S(2)}) collective-permute-start(f32[248,128]{1,0:T(8,128)S(1)} %pad_maximum_fusion.1), channel_id=1, source_target_pairs={{0,18},{1,13},{2,14},{3,17},{4,8},{5,23},{6,20},{7,11},{8,4},{9,27... | collective-permute-start | bytes 380936 | tf_op jit(solution)/shard_map/total/ppermute | solution.py:404
  19.6 4.4 %collective-permute-start.7 = (f32[248,128]{1,0:T(8,128)S(1)}, f32[248,128]{1,0:T(8,128)S(1)}, u32[]{:S(2)}, u32[]{:S(2)}) collective-permute-start(f32[248,128]{1,0:T(8,128)S(1)} %pad_maximum_fusion.1), channel_id=1, source_target_pairs={{0,3},{1,8},{2,11},{3,0},{4,13},{5,6},{6,5},{7,14},{8,1},{9,10},{1... | collective-permute-start | bytes 380936 | tf_op jit(solution)/shard_map/total/ppermute | solution.py:404
  19.6 4.4 %collective-permute-start.5 = (f32[248,128]{1,0:T(8,128)S(1)}, f32[248,128]{1,0:T(8,128)S(1)}, u32[]{:S(2)}, u32[]{:S(2)}) collective-permute-start(f32[248,128]{1,0:T(8,128)S(1)} %pad_maximum_fusion.1), channel_id=1, source_target_pairs={{0,17},{1,4},{2,7},{3,18},{4,1},{5,20},{6,23},{7,2},{8,13},{9,24},... | collective-permute-start | bytes 380936 | tf_op jit(solution)/shard_map/total/ppermute | solution.py:404
  24.0 7.0 %collective-permute-start.8 = (f32[248,128]{1,0:T(8,128)S(1)}, f32[248,128]{1,0:T(8,128)S(1)}, u32[]{:S(2)}, u32[]{:S(2)}) collective-permute-start(f32[248,128]{1,0:T(8,128)S(1)} %add_add_fusion.1), channel_id=1, source_target_pairs={{0,12},{1,19},{2,16},{3,15},{4,22},{5,9},{6,10},{7,21},{8,26},{9,5... | collective-permute-start | bytes 380936 | tf_op jit(solution)/shard_map/total/ppermute | solution.py:404
  28.0 5.7 %collective-permute-start.10 = (f32[248,128]{1,0:T(8,128)S(1)}, f32[248,128]{1,0:T(8,128)S(1)}, u32[]{:S(2)}, u32[]{:S(2)}) collective-permute-start(f32[248,128]{1,0:T(8,128)S(1)} %add_add_fusion.1), channel_id=1, source_target_pairs={{0,5},{1,16},{2,19},{3,6},{4,21},{5,0},{6,3},{7,22},{8,25},{9,12},... | collective-permute-start | bytes 380936 | tf_op jit(solution)/shard_map/total/ppermute | solution.py:404
  28.0 5.7 %collective-permute-start.9 = (f32[248,128]{1,0:T(8,128)S(1)}, f32[248,128]{1,0:T(8,128)S(1)}, u32[]{:S(2)}, u32[]{:S(2)}) collective-permute-start(f32[248,128]{1,0:T(8,128)S(1)} %add_add_fusion.1), channel_id=1, source_target_pairs={{0,9},{1,2},{2,1},{3,10},{4,7},{5,12},{6,15},{7,4},{8,11},{9,0},{1... | collective-permute-start | bytes 380936 | tf_op jit(solution)/shard_map/total/ppermute | solution.py:404
  33.8 1.4 %collective-permute-start.11 = (f32[248,128]{1,0:T(8,128)S(1)}, f32[248,128]{1,0:T(8,128)S(1)}, u32[]{:S(2)}, u32[]{:S(2)}) collective-permute-start(f32[248,128]{1,0:T(8,128)S(1)} %add_add_fusion.mine_ref), channel_id=1, source_target_pairs={{0,1},{1,0},{2,3},{3,2},{4,5},{5,4},{6,7},{7,6},{8,9},{9,8},{10,11... | collective-permute-start | bytes 380936 | tf_op jit(solution)/shard_map/total/ppermute | solution.py:414

commit v6 on v5

--- a/solution.py
+++ b/solution.py
@@ -57,7 +57,7 @@
     own_ref[...] = packed
 
 
-def matrices(f1_ref, f2_ref, w1_ref, w2_ref, wb_ref, sh_ref, f1):
+def matrices(f1_ref, f2_ref, w1_ref, w2_ref, wb_ref, sh_ref):
     col = iota((1, 4096), 1)
     half, dp, dq, dr = col // 2048, lax.rem(col // 1024, 2), lax.rem(col // 512, 2), lax.rem(col // 256, 2)
     b = lax.rem(col // 64, 4) - dq
@@ -66,9 +66,7 @@
     inside = (a >= 0) & (a < 3) & (b >= 0) & (b < 3) & (c >= 0) & (c < 3)
     wanted = jnp.where(inside, (a * 9 + b * 3 + c) * 4 + lax.rem(col, 4), -1)
     place = one_hot(iota((108, 4096), 0) == wanted)
-    for tap in range(27):
-        f1[tap * 4 : tap * 4 + 4, :] = f1_ref[tap].astype(F32)
-    w1 = mm_tn(f1[...].astype(BF16), place).astype(BF16)
+    w1 = mm_tn(f1_ref[...], place).astype(BF16)
     for k in range(16):
         w1_ref[k * 32 : (k + 1) * 32, :] = w1[:, k * LANES : (k + 1) * LANES]
 
@@ -173,8 +171,8 @@
 
 
 def near_kernel(own_ref, near_ref, f1_ref, f2_ref,
-                w1_ref, w2_ref, wb_ref, sh_ref, xt_ref, z_ref, maps_ref, mg, xt, f1):
-    matrices(f1_ref, f2_ref, w1_ref, w2_ref, wb_ref, sh_ref, f1)
+                w1_ref, w2_ref, wb_ref, sh_ref, xt_ref, z_ref, maps_ref, mg, xt):
+    matrices(f1_ref, f2_ref, w1_ref, w2_ref, wb_ref, sh_ref)
     half = near_half()
     own, near = own_ref[0:256, :], near_ref[0:256, :]
     mg[0] = merge(own, near, plane_rows(half))
@@ -421,7 +419,9 @@
         pairs += [(k * n_space + i, (k + 1) * n_space + i) for k in range(0, n_dp, 2) for i in (0, n_space - 1)]
     across = both_ways(pairs)
     with jax.named_scope("blocks"):
-        own = call(blocks_kernel, shape((320, LANES), BF16), [pltpu.VMEM((512, LANES), F32)])(crop)
+        own = call(
+            blocks_kernel, shape((320, LANES), BF16), [pltpu.VMEM((512, LANES), F32)], flops=1_000_000_000, size=3_000_000
+        )(crop)
         own, cot = lax.optimization_barrier((own, cotangent.transpose(0, 2, 3, 4, 1).reshape(LANES, 64)))
         cot = cot.T
     with jax.named_scope("halo"):
@@ -440,10 +440,10 @@
                 shape((4, 256, LANES), F32),
                 shape((2, 128, LANES), BF16),
             ),
-            [pltpu.VMEM((2, 256, LANES), BF16), pltpu.VMEM((2, 576, LANES), BF16), pltpu.VMEM((108, 32), F32)],
+            [pltpu.VMEM((2, 256, LANES), BF16), pltpu.VMEM((2, 576, LANES), BF16)],
             flops=1_000_000_000,
             size=4_000_000,
-        )(own, beside, filter_one.reshape(27, 4, 32), filter_two.reshape(864, 64))
+        )(own, beside, filter_one.reshape(108, 32), filter_two.reshape(864, 64))
     beyond, tail, xt_near = lax.optimization_barrier((beyond, tail, xt_near))
     with jax.named_scope("far"):
         forward = lax.ppermute(jnp.concatenate([beyond, cot], axis=0), "space", near)

time: 36.4 us -> 36.4 us (level)
  local copies, waits for them, and re-layouts: 3.56 us -> 1.08 us
  starting transfers between devices: 11.9 us -> 13.9 us
  waiting for transfers between devices: 11 us -> 11.5 us
    unnamed x6 -> x8, local copies, waits for them, and re-layouts: 2.62 us -> 0.95 us
    optimization_barrier x1, local copies, waits for them, and re-layouts: 0.92 us -> 0.09 us  [local(): lax.optimization_barrier((own, cotangent.transpose(0, 2, 3, 4, 1).reshape...]
    ppermute x1, starting transfers between devices: 0.41 us -> 1.2 us  [local(): lax.ppermute(jnp.concatenate([beside[256:], cot], axis=0), ('dp', 'space'...]
    ppermute x1, waiting for transfers between devices: 0.94 us -> 1.56 us  [local(): lax.ppermute(jnp.concatenate([beside[256:], cot], axis=0), ('dp', 'space'...]
    ppermute x6, starting transfers between devices: 7.66 us -> 8.21 us  [total_over_mesh(): lax.ppermute(mine, axes, [(i, i ^ masks[shares[i]][k]) for i in range(siz...]
  transfers between devices with their start and end apart: 12 -> 12, of which waited for: 7 -> 8; matrix products, arithmetic and copies ran while one was open for 3% -> 0% of each run, Pallas kernels for 12% -> 12%
where the time goes in v6:
time: 36.4 us; the launch traced here: 36.2 us
  starting transfers between devices  13.9 us (38%)
  waiting for transfers between devices  11.5 us (32%)
  Pallas kernels  8.89 us (24%)
  local copies, waits for them, and re-layouts  1.08 us (3%)
  between operations  0.75 us (2%)
    ppermute x6, waiting for transfers between devices, total_over_mesh(): lax.ppermute(mine, axes, [(i, i ^ masks[shares[i]][k]) for i in range(siz...  8.55 us
    ppermute x6, starting transfers between devices, total_over_mesh(): lax.ppermute(mine, axes, [(i, i ^ masks[shares[i]][k]) for i in range(siz...  8.21 us
    pallas_call x1, Pallas kernels, local(): call(second_kernel, (shape((64, LANES), BF16), shape((216, 128), F32), sh...  2.66 us
    ppermute x1, starting transfers between devices, local(): beyond = lax.ppermute(own[:256], ('dp', 'space'), across)  2.57 us
    ppermute x1, waiting for transfers between devices, local(): lax.ppermute(jnp.concatenate([beside[256:], cot], axis=0), ('dp', 'space'...  1.56 us
    pallas_call x1, Pallas kernels, local(): call(first_kernel, shape((32, 128), F32), [pltpu.VMEM((2, 128, LANES), F3...  1.39 us
    pallas_call x1, Pallas kernels, local(): call(near_kernel, (shape((512, 256), BF16), shape((256, 1536), BF16), sha...  1.28 us
    ppermute x1, starting transfers between devices, local(): lax.ppermute(jnp.concatenate([beside[256:], cot], axis=0), ('dp', 'space'...  1.2 us
  transfers between devices with their start and end apart: 12, of which 8 were waited for; matrix products, arithmetic and copies ran while one was open for 0% of the time, Pallas kernels for 12%

profile of v6, /device:TPU:0, one launch (start us, length us, event | category | flops | bytes accessed | tf_op | source)
XLA Modules:
  0.0 36.2 jit_solution(16664976028272826041)
XLA Ops:
  0.6 0.0 copy-start
  0.6 0.9 %copy-done = bf16[1,4,4,64,64]{4,3,2,1,0:T(8,128)(2,1)S(1)} copy-done((bf16[1,4,4,64,64]{4,3,2,1,0:T(8,128)(2,1)S(1)}, bf16[1,4,4,64,64]{4,3,2,1,0:T(8,128)(2,1)}, u32[]{:S(2)}) %copy-start) | copy-done | bytes 131096
  1.6 0.0 copy-start.3
  1.6 0.0 copy-start.2
  1.6 0.0 copy-start.1
  1.6 0.9 %blocks.1.own_ref = bf16[320,256]{1,0:T(8,128)(2,1)S(1)} custom-call(bf16[1,4,4,64,64]{4,3,2,1,0:T(8,128)(2,1)S(1)} %copy-done), custom_call_target="tpu_custom_call" | custom-call | flops 1000000000 | bytes 3000000 | tf_op jit(solution)/shard_map/blocks/pallas_call | solution.py:422
  2.5 0.5 %collective-permute-start = (bf16[320,256]{1,0:T(8,128)(2,1)S(1)}, bf16[320,256]{1,0:T(8,128)(2,1)S(1)}, u32[]{:S(2)}, u32[]{:S(2)}) collective-permute-start(bf16[320,256]{1,0:T(8,128)(2,1)S(1)} %blocks.1.own_ref), channel_id=1, source_target_pairs={{0,1},{1,0},{2,3},{3,2},{4,5},{5,4},{6,7},{7,6},{8,9},{9,8},{10,11... | collective-permute-start | bytes 491528 | tf_op jit(solution)/shard_map/halo/ppermute | solution.py:428
  3.1 2.6 %collective-permute-start.1 = (bf16[256,256]{1,0:T(8,128)(2,1)S(1)}, bf16[256,256]{1,0:T(8,128)(2,1)S(1)}, u32[]{:S(2)}, u32[]{:S(2)}) collective-permute-start(bf16[256,256]{1,0:T(8,128)(2,1)S(1)} %slice.6), channel_id=1, source_target_pairs={{1,2},{3,4},{5,6},{7,8},{9,10},{11,12},{13,14},{17,18},{19,20},{21... | collective-permute-start | bytes 393224 | tf_op jit(solution)/shard_map/halo/ppermute | solution.py:429
  5.6 0.0 copy-done.3
  5.7 0.0 copy-done.2
  5.7 0.1 copy.8
  5.8 0.0 collective-permute-done.near_ref
  5.8 1.2 %collective-permute-start.2 = (bf16[128,256]{1,0:T(8,128)(2,1)S(1)}, bf16[128,256]{1,0:T(8,128)(2,1)S(1)}, u32[]{:S(2)}, u32[]{:S(2)}) collective-permute-start(bf16[128,256]{1,0:T(8,128)(2,1)S(1)} %pad_maximum_fusion.2), channel_id=1, source_target_pairs={{1,2},{3,4},{5,6},{7,8},{9,10},{11,12},{13,14},{17,18},{19,20},{21... | collective-permute-start | bytes 196616 | tf_op jit(solution)/shard_map/halo/ppermute | solution.py:430
  7.0 0.0 copy-done.1
  7.0 1.3 %near.1 = (bf16[512,256]{1,0:T(8,128)(2,1)S(1)}, bf16[256,1536]{1,0:T(8,128)(2,1)S(1)}, bf16[128,3072]{1,0:T(8,128)(2,1)S(1)}, bf16[4,256,256]{2,1,0:T(8,128)(2,...) custom-call(bf16[320,256]{1,0:T(8,128)(2,1)S(1)} %blocks.1.own_ref, ...), custom_call_target="tpu_custom_call" | custom-call | flops 1000000000 | bytes 4000000 | tf_op jit(solution)/shard_map/near/pallas_call | solution.py:432
  8.3 0.3 collective-permute-done.1.far_ref
  8.6 1.6 %collective-permute-done.2.tail_ref = bf16[128,256]{1,0:T(8,128)(2,1)S(1)} collective-permute-done((bf16[128,256]{1,0:T(8,128)(2,1)S(1)}, bf16[128,256]{1,0:T(8,128)(2,1)S(1)}, u32[]{:S(2)}, u32[]{:S(2)}) %collective-permute-start.2) | collective-permute-done | bytes 65568 | tf_op jit(solution)/shard_map/halo/ppermute | solution.py:430
  10.2 0.4 %collective-permute-start.3 = (bf16[320,256]{1,0:T(8,128)(2,1)S(1)}, bf16[320,256]{1,0:T(8,128)(2,1)S(1)}, u32[]{:S(2)}, u32[]{:S(2)}) collective-permute-start(bf16[320,256]{1,0:T(8,128)(2,1)S(1)} %pad_maximum_fusion), channel_id=1, source_target_pairs={{0,1},{1,0},{2,3},{3,2},{4,5},{5,4},{6,7},{7,6},{8,9},{9,8},{10,11... | collective-permute-start | bytes 491528 | tf_op jit(solution)/shard_map/far/ppermute | solution.py:449
  10.6 0.9 %far.1 = (bf16[576,256]{1,0:T(8,128)(2,1)S(1)}, f32[4,256,256]{2,1,0:T(8,128)S(1)}, bf16[3,128,256]{2,1,0:T(8,128)(2,1)S(1)}) custom-call(bf16[320,256]{1,0:T(8,128)(2,1)S(1)} %blocks.1.own_ref, bf16[256,256]{1,0:T(8,128)(2,1)S(1)} %collective-permute-done.1.far_ref, bf16[128,256]{1,0:T(8,128)(2,1)S(1)} %collective-permute-done.2.tail_ref, ...), custom_call_target="tpu_custom_call" | custom-call | flops 1000000000 | bytes 3000000 | tf_op jit(solution)/shard_map/far/pallas_call | solution.py:450
  11.5 0.1 collective-permute-done.3.fwd_ref
  11.6 2.7 %second.1 = (bf16[64,256]{1,0:T(8,128)(2,1)S(1)}, f32[216,128]{1,0:T(8,128)S(1)}, f32[216,128]{1,0:T(8,128)S(1)}, bf16[4,1024,256]{2,1,0:T(8,128)(2,1)S(1)}) custom-call(bf16[320,256]{1,0:T(8,128)(2,1)S(1)} %collective-permute-done.near_ref, bf16[128,256]{1,0:T(8,128)(2,1)S(1)} %collective-permute-done.2.tail_ref, ...), custom_call_target="tpu_custom_call" | custom-call | flops 4000000000 | bytes 6000000 | tf_op jit(solution)/shard_map/second/pallas_call | solution.py:458
  14.3 0.4 %collective-permute-start.4 = (f32[216,128]{1,0:T(8,128)S(1)}, f32[216,128]{1,0:T(8,128)S(1)}, u32[]{:S(2)}, u32[]{:S(2)}) collective-permute-start(f32[216,128]{1,0:T(8,128)S(1)} %get-tuple-element.39), channel_id=1, source_target_pairs={{0,1},{1,0},{2,3},{3,2},{4,5},{5,4},{6,7},{7,6},{8,9},{9,8},{10,11... | collective-permute-start | bytes 331784 | tf_op jit(solution)/shard_map/second/ppermute | solution.py:476
  14.7 1.4 %first.1 = f32[32,128]{1,0:T(8,128)S(1)} custom-call(bf16[4,1024,256]{2,1,0:T(8,128)(2,1)S(1)} %get-tuple-element.40.g_ext, bf16[128,3072]{1,0:T(8,128)(2,1)S(1)} %get-tuple-element.41.wb_ref, bf16[576,256]{1,0:T(8,128)(2,1)S(1)} %get-tuple-element.42.xt_near, f32[4,256,256]{2,1,0:T(8,128)S(1)} %get-tuple-element.43.z_near, ...), custom_call_target="tpu_custom_call" | custom-call | flops 4000000000 | bytes 6000000 | tf_op jit(solution)/shard_map/first/pallas_call | solution.py:478
  16.1 0.0 collective-permute-done.4
  16.1 3.5 %collective-permute-start.6 = (f32[248,128]{1,0:T(8,128)S(1)}, f32[248,128]{1,0:T(8,128)S(1)}, u32[]{:S(2)}, u32[]{:S(2)}) collective-permute-start(f32[248,128]{1,0:T(8,128)S(1)} %pad_maximum_fusion.1), channel_id=1, source_target_pairs={{0,18},{1,13},{2,14},{3,17},{4,8},{5,23},{6,20},{7,11},{8,4},{9,27... | collective-permute-start | bytes 380936 | tf_op jit(solution)/shard_map/total/ppermute | solution.py:402
  19.6 0.0 collective-permute-start.7
  19.7 0.4 collective-permute-start.5
  20.0 2.5 %collective-permute-done.6 = f32[248,128]{1,0:T(8,128)S(1)} collective-permute-done((f32[248,128]{1,0:T(8,128)S(1)}, f32[248,128]{1,0:T(8,128)S(1)}, u32[]{:S(2)}, u32[]{:S(2)}) %collective-permute-start.6) | collective-permute-done | bytes 127008 | tf_op jit(solution)/shard_map/total/ppermute | solution.py:402
  22.6 1.4 %collective-permute-done.7 = f32[248,128]{1,0:T(8,128)S(1)} collective-permute-done((f32[248,128]{1,0:T(8,128)S(1)}, f32[248,128]{1,0:T(8,128)S(1)}, u32[]{:S(2)}, u32[]{:S(2)}) %collective-permute-start.7) | collective-permute-done | bytes 127008 | tf_op jit(solution)/shard_map/total/ppermute | solution.py:402
  24.0 0.0 collective-permute-done.5
  24.0 4.0 %collective-permute-start.8 = (f32[248,128]{1,0:T(8,128)S(1)}, f32[248,128]{1,0:T(8,128)S(1)}, u32[]{:S(2)}, u32[]{:S(2)}) collective-permute-start(f32[248,128]{1,0:T(8,128)S(1)} %add_add_fusion.1), channel_id=1, source_target_pairs={{0,12},{1,19},{2,16},{3,15},{4,22},{5,9},{6,10},{7,21},{8,26},{9,5... | collective-permute-start | bytes 380936 | tf_op jit(solution)/shard_map/total/ppermute | solution.py:402
  28.0 0.0 collective-permute-start.10
  28.0 0.4 collective-permute-start.9
  28.4 0.8 %total.2 = bf16[256,64]{1,0:T(8,128)(2,1)} custom-call(bf16[64,256]{1,0:T(8,128)(2,1)S(1)} %get-tuple-element.48.feat_ref), custom_call_target="tpu_custom_call" | custom-call | flops 10000000 | bytes 1000000 | tf_op jit(solution)/shard_map/total/pallas_call | solution.py:405
  29.2 1.8 %collective-permute-done.8 = f32[248,128]{1,0:T(8,128)S(1)} collective-permute-done((f32[248,128]{1,0:T(8,128)S(1)}, f32[248,128]{1,0:T(8,128)S(1)}, u32[]{:S(2)}, u32[]{:S(2)}) %collective-permute-start.8) | collective-permute-done | bytes 127008 | tf_op jit(solution)/shard_map/total/ppermute | solution.py:402
  31.0 2.7 %collective-permute-done.10 = f32[248,128]{1,0:T(8,128)S(1)} collective-permute-done((f32[248,128]{1,0:T(8,128)S(1)}, f32[248,128]{1,0:T(8,128)S(1)}, u32[]{:S(2)}, u32[]{:S(2)}) %collective-permute-start.10) | collective-permute-done | bytes 127008 | tf_op jit(solution)/shard_map/total/ppermute | solution.py:402
  33.8 0.0 collective-permute-done.9
  33.8 0.5 %collective-permute-start.11 = (f32[248,128]{1,0:T(8,128)S(1)}, f32[248,128]{1,0:T(8,128)S(1)}, u32[]{:S(2)}, u32[]{:S(2)}) collective-permute-start(f32[248,128]{1,0:T(8,128)S(1)} %add_add_fusion.mine_ref), channel_id=1, source_target_pairs={{0,1},{1,0},{2,3},{3,2},{4,5},{5,4},{6,7},{7,6},{8,9},{9,8},{10,11... | collective-permute-start | bytes 380936 | tf_op jit(solution)/shard_map/total/ppermute | solution.py:412
  34.3 1.0 %collective-permute-done.11.other_ref = f32[248,128]{1,0:T(8,128)S(1)} collective-permute-done((f32[248,128]{1,0:T(8,128)S(1)}, f32[248,128]{1,0:T(8,128)S(1)}, u32[]{:S(2)}, u32[]{:S(2)}) %collective-permute-start.11) | collective-permute-done | bytes 127008 | tf_op jit(solution)/shard_map/total/ppermute | solution.py:412
  35.3 0.9 %total.3 = (f32[27,4,32]{2,1,0:T(4,128)}, f32[864,64]{1,0:T(8,128)}) custom-call(f32[248,128]{1,0:T(8,128)S(1)} %add_add_fusion.mine_ref, f32[248,128]{1,0:T(8,128)S(1)} %collective-permute-done.11.other_ref), custom_call_target="tpu_custom_call" | custom-call | tf_op jit(solution)/shard_map/total/pallas_call | solution.py:488
  (9 shorter events, 0.2 us)
Async XLA Ops:
  0.6 1.0 %copy-start = (bf16[1,4,4,64,64]{4,3,2,1,0:T(8,128)(2,1)S(1)}, bf16[1,4,4,64,64]{4,3,2,1,0:T(8,128)(2,1)}, u32[]{:S(2)}) copy-start(bf16[1,4,4,64,64]{4,3,2,1,0:T(8,128)(2,1)} %crop_ref.1) | copy-start | bytes 393220
  1.6 4.1 %copy-start.3 = (bf16[3,3,3,4,32]{4,3,2,1,0:T(4,128)(2,1)S(1)}, bf16[3,3,3,4,32]{4,3,2,1,0:T(4,128)(2,1)}, u32[]{:S(2)}) copy-start(bf16[3,3,3,4,32]{4,3,2,1,0:T(4,128)(2,1)} %param.5) | copy-start | bytes 20740
  1.6 4.1 %copy-start.2 = (bf16[1,64,1,16,16]{1,4,3,2,0:T(8,128)(2,1)S(1)}, bf16[1,64,1,16,16]{1,4,3,2,0:T(8,128)(2,1)}, u32[]{:S(2)}) copy-start(bf16[1,64,1,16,16]{1,4,3,2,0:T(8,128)(2,1)} %param.7) | copy-start | bytes 98308
  1.6 5.4 %copy-start.1 = (bf16[3,3,3,32,64]{4,3,2,1,0:T(8,128)(2,1)S(1)}, bf16[3,3,3,32,64]{4,3,2,1,0:T(8,128)(2,1)}, u32[]{:S(2)}) copy-start(bf16[3,3,3,32,64]{4,3,2,1,0:T(8,128)(2,1)} %param.6) | copy-start | bytes 331780
  2.5 3.2 %collective-permute-start = (bf16[320,256]{1,0:T(8,128)(2,1)S(1)}, bf16[320,256]{1,0:T(8,128)(2,1)S(1)}, u32[]{:S(2)}, u32[]{:S(2)}) collective-permute-start(bf16[320,256]{1,0:T(8,128)(2,1)S(1)} %blocks.1.own_ref), channel_id=1, source_target_pairs={{0,1},{1,0},{2,3},{3,2},{4,5},{5,4},{6,7},{7,6},{8,9},{9,8},{10,11... | collective-permute-start | bytes 491528 | tf_op jit(solution)/shard_map/halo/ppermute | solution.py:428
  3.1 5.5 %collective-permute-start.1 = (bf16[256,256]{1,0:T(8,128)(2,1)S(1)}, bf16[256,256]{1,0:T(8,128)(2,1)S(1)}, u32[]{:S(2)}, u32[]{:S(2)}) collective-permute-start(bf16[256,256]{1,0:T(8,128)(2,1)S(1)} %slice.6), channel_id=1, source_target_pairs={{1,2},{3,4},{5,6},{7,8},{9,10},{11,12},{13,14},{17,18},{19,20},{21... | collective-permute-start | bytes 393224 | tf_op jit(solution)/shard_map/halo/ppermute | solution.py:429
  5.8 4.3 %collective-permute-start.2 = (bf16[128,256]{1,0:T(8,128)(2,1)S(1)}, bf16[128,256]{1,0:T(8,128)(2,1)S(1)}, u32[]{:S(2)}, u32[]{:S(2)}) collective-permute-start(bf16[128,256]{1,0:T(8,128)(2,1)S(1)} %pad_maximum_fusion.2), channel_id=1, source_target_pairs={{1,2},{3,4},{5,6},{7,8},{9,10},{11,12},{13,14},{17,18},{19,20},{21... | collective-permute-start | bytes 196616 | tf_op jit(solution)/shard_map/halo/ppermute | solution.py:430
  10.2 1.5 %collective-permute-start.3 = (bf16[320,256]{1,0:T(8,128)(2,1)S(1)}, bf16[320,256]{1,0:T(8,128)(2,1)S(1)}, u32[]{:S(2)}, u32[]{:S(2)}) collective-permute-start(bf16[320,256]{1,0:T(8,128)(2,1)S(1)} %pad_maximum_fusion), channel_id=1, source_target_pairs={{0,1},{1,0},{2,3},{3,2},{4,5},{5,4},{6,7},{7,6},{8,9},{9,8},{10,11... | collective-permute-start | bytes 491528 | tf_op jit(solution)/shard_map/far/ppermute | solution.py:449
  14.3 1.8 %collective-permute-start.4 = (f32[216,128]{1,0:T(8,128)S(1)}, f32[216,128]{1,0:T(8,128)S(1)}, u32[]{:S(2)}, u32[]{:S(2)}) collective-permute-start(f32[216,128]{1,0:T(8,128)S(1)} %get-tuple-element.39), channel_id=1, source_target_pairs={{0,1},{1,0},{2,3},{3,2},{4,5},{5,4},{6,7},{7,6},{8,9},{9,8},{10,11... | collective-permute-start | bytes 331784 | tf_op jit(solution)/shard_map/second/ppermute | solution.py:476
  16.1 6.4 %collective-permute-start.6 = (f32[248,128]{1,0:T(8,128)S(1)}, f32[248,128]{1,0:T(8,128)S(1)}, u32[]{:S(2)}, u32[]{:S(2)}) collective-permute-start(f32[248,128]{1,0:T(8,128)S(1)} %pad_maximum_fusion.1), channel_id=1, source_target_pairs={{0,18},{1,13},{2,14},{3,17},{4,8},{5,23},{6,20},{7,11},{8,4},{9,27... | collective-permute-start | bytes 380936 | tf_op jit(solution)/shard_map/total/ppermute | solution.py:402
  19.6 4.3 %collective-permute-start.7 = (f32[248,128]{1,0:T(8,128)S(1)}, f32[248,128]{1,0:T(8,128)S(1)}, u32[]{:S(2)}, u32[]{:S(2)}) collective-permute-start(f32[248,128]{1,0:T(8,128)S(1)} %pad_maximum_fusion.1), channel_id=1, source_target_pairs={{0,3},{1,8},{2,11},{3,0},{4,13},{5,6},{6,5},{7,14},{8,1},{9,10},{1... | collective-permute-start | bytes 380936 | tf_op jit(solution)/shard_map/total/ppermute | solution.py:402
  19.7 4.3 %collective-permute-start.5 = (f32[248,128]{1,0:T(8,128)S(1)}, f32[248,128]{1,0:T(8,128)S(1)}, u32[]{:S(2)}, u32[]{:S(2)}) collective-permute-start(f32[248,128]{1,0:T(8,128)S(1)} %pad_maximum_fusion.1), channel_id=1, source_target_pairs={{0,17},{1,4},{2,7},{3,18},{4,1},{5,20},{6,23},{7,2},{8,13},{9,24},... | collective-permute-start | bytes 380936 | tf_op jit(solution)/shard_map/total/ppermute | solution.py:402
  24.0 7.0 %collective-permute-start.8 = (f32[248,128]{1,0:T(8,128)S(1)}, f32[248,128]{1,0:T(8,128)S(1)}, u32[]{:S(2)}, u32[]{:S(2)}) collective-permute-start(f32[248,128]{1,0:T(8,128)S(1)} %add_add_fusion.1), channel_id=1, source_target_pairs={{0,12},{1,19},{2,16},{3,15},{4,22},{5,9},{6,10},{7,21},{8,26},{9,5... | collective-permute-start | bytes 380936 | tf_op jit(solution)/shard_map/total/ppermute | solution.py:402
  28.0 5.7 %collective-permute-start.10 = (f32[248,128]{1,0:T(8,128)S(1)}, f32[248,128]{1,0:T(8,128)S(1)}, u32[]{:S(2)}, u32[]{:S(2)}) collective-permute-start(f32[248,128]{1,0:T(8,128)S(1)} %add_add_fusion.1), channel_id=1, source_target_pairs={{0,5},{1,16},{2,19},{3,6},{4,21},{5,0},{6,3},{7,22},{8,25},{9,12},... | collective-permute-start | bytes 380936 | tf_op jit(solution)/shard_map/total/ppermute | solution.py:402
  28.0 5.7 %collective-permute-start.9 = (f32[248,128]{1,0:T(8,128)S(1)}, f32[248,128]{1,0:T(8,128)S(1)}, u32[]{:S(2)}, u32[]{:S(2)}) collective-permute-start(f32[248,128]{1,0:T(8,128)S(1)} %add_add_fusion.1), channel_id=1, source_target_pairs={{0,9},{1,2},{2,1},{3,10},{4,7},{5,12},{6,15},{7,4},{8,11},{9,0},{1... | collective-permute-start | bytes 380936 | tf_op jit(solution)/shard_map/total/ppermute | solution.py:402
  33.8 1.5 %collective-permute-start.11 = (f32[248,128]{1,0:T(8,128)S(1)}, f32[248,128]{1,0:T(8,128)S(1)}, u32[]{:S(2)}, u32[]{:S(2)}) collective-permute-start(f32[248,128]{1,0:T(8,128)S(1)} %add_add_fusion.mine_ref), channel_id=1, source_target_pairs={{0,1},{1,0},{2,3},{3,2},{4,5},{5,4},{6,7},{7,6},{8,9},{9,8},{10,11... | collective-permute-start | bytes 380936 | tf_op jit(solution)/shard_map/total/ppermute | solution.py:412

commit v7 on v6

--- a/solution.py
+++ b/solution.py
@@ -11,6 +11,7 @@
 BF16 = jnp.bfloat16
 LANES = 256
 ORDERS = (((0, 2, 1), (0, 2, 1)), ((1, 0, 2), (1, 0, 2)))
+SHIFTS = [(1, 0), (-1, 0), (0, 1), (0, -1), (1, 1), (1, -1), (-1, 1), (-1, -1)]
 VMEM = pl.BlockSpec(memory_space=pltpu.VMEM)
 
 
@@ -101,10 +102,9 @@
             wb_ref[eq * 64 : eq * 64 + 64, lane : lane + 256] = jnp.zeros((64, 256), BF16)
 
     k, lane = iota((LANES, LANES), 0), iota((LANES, LANES), 1)
-    sh_ref[0] = one_hot(k == lane - 16)
-    sh_ref[1] = one_hot(k == lane + 16)
-    sh_ref[2] = one_hot((k == lane - 1) & (lax.rem(lane, 16) != 0))
-    sh_ref[3] = one_hot((k == lane + 1) & (lax.rem(lane, 16) != 15))
+    for n, (q, r) in enumerate(SHIFTS):
+        kept = lax.rem(lane, 16) != (0 if r == 1 else 15 if r == -1 else 16)
+        sh_ref[n] = one_hot((k == lane - 16 * q - r) & kept)
 
 
 def near_half():
@@ -133,19 +133,16 @@
         for qq in range(4):
             at = ((qq + 1) * 6 + 1) * 16
             xt[k, at : at + 64, :] = mg[k, qq * 64 : qq * 64 + 64, :]
-    up = mm(mg[:, 192:256, :].reshape(count * 64, LANES), sh_ref[0]).astype(BF16)
-    down = mm(mg[:, 0:64, :].reshape(count * 64, LANES), sh_ref[1]).astype(BF16)
-    for k in range(count):
-        xt[k, 16:80, :] = up[k * 64 : k * 64 + 64]
-        xt[k, 496:560, :] = down[k * 64 : k * 64 + 64]
-    cells = [(k, q) for k in range(count) for q in range(6)]
-    last = jnp.concatenate([xt[k, (q * 6 + 4) * 16 : (q * 6 + 5) * 16, :] for k, q in cells], axis=0)
-    first = jnp.concatenate([xt[k, (q * 6 + 1) * 16 : (q * 6 + 2) * 16, :] for k, q in cells], axis=0)
-    up = mm(last, sh_ref[2]).astype(BF16)
-    down = mm(first, sh_ref[3]).astype(BF16)
-    for n, (k, q) in enumerate(cells):
-        xt[k, q * 96 : q * 96 + 16, :] = up[n * 16 : n * 16 + 16]
-        xt[k, q * 96 + 80 : q * 96 + 96, :] = down[n * 16 : n * 16 + 16]
+    for n, (q, r) in enumerate(SHIFTS):
+        q_from, q_to = {1: ([3], [0]), -1: ([0], [5]), 0: (range(4), range(1, 5))}[q]
+        r_from, r_to = {1: ([3], [0]), -1: ([0], [5]), 0: (range(4), range(1, 5))}[r]
+        size = 16 * len(r_from)
+        starts = [(k, (i * 4 + r_from[0]) * 16) for k in range(count) for i in q_from]
+        rows = [mg[k, at : at + size, :] for k, at in starts]
+        moved = mm(jnp.concatenate(rows, axis=0), sh_ref[n]).astype(BF16)
+        targets = [(k, (i * 6 + r_to[0]) * 16) for k in range(count) for i in q_to]
+        for m, (k, at) in enumerate(targets):
+            xt[k, at : at + size, :] = moved[m * size : (m + 1) * size]
 
 
 def patch(xt, k, eq, er):
@@ -216,20 +213,16 @@
 
 
 def extend(ref, planes, size, sh_ref):
-    for source, target, matrix in ((2, 0, 0), (1, 3, 1)):
-        at, to = (source * 4 + 1) * size, (target * 4 + 1) * size
-        block = jnp.concatenate([ref[k, at : at + 2 * size, :] for k in planes], axis=0)
-        moved = mm(block, sh_ref[matrix]).astype(BF16)
-        for n, k in enumerate(planes):
-            ref[k, to : to + 2 * size, :] = moved[n * 2 * size : (n + 1) * 2 * size]
-    cells = [(k, q) for k in planes for q in range(4)]
-    for source, target, matrix in ((2, 0, 2), (1, 3, 3)):
-        block = jnp.concatenate(
-            [ref[k, (q * 4 + source) * size : (q * 4 + source + 1) * size, :] for k, q in cells], axis=0
-        )
-        moved = mm(block, sh_ref[matrix]).astype(BF16)
-        for n, (k, q) in enumerate(cells):
-            ref[k, (q * 4 + target) * size : (q * 4 + target + 1) * size, :] = moved[n * size : (n + 1) * size]
+    for n, (q, r) in enumerate(SHIFTS):
+        q_from, q_to = {1: ([2], [0]), -1: ([1], [3]), 0: ([1, 2], [1, 2])}[q]
+        r_from, r_to = {1: ([2], [0]), -1: ([1], [3]), 0: ([1, 2], [1, 2])}[r]
+        wide = size * len(r_from)
+        starts = [(k, (i * 4 + r_from[0]) * size) for k in planes for i in q_from]
+        rows = [ref[k, at : at + wide, :] for k, at in starts]
+        moved = mm(jnp.concatenate(rows, axis=0), sh_ref[n]).astype(BF16)
+        targets = [(k, (i * 4 + r_to[0]) * size) for k in planes for i in q_to]
+        for m, (k, at) in enumerate(targets):
+            ref[k, at : at + wide, :] = moved[m * wide : (m + 1) * wide]
 
 
 def second_kernel(near_ref, tail_ref, fwd_ref, cot_ref, w1_ref, w2_ref, sh_ref, maps_near, maps_far,
@@ -435,7 +428,7 @@
                 shape((512, 256), BF16),
                 shape((256, 1536), BF16),
                 shape((128, 3072), BF16),
-                shape((4, LANES, LANES), BF16),
+                shape((8, LANES, LANES), BF16),
                 shape((576, LANES), BF16),
                 shape((4, 256, LANES), F32),
                 shape((2, 128, LANES), BF16),

time: 36.4 us -> 36.4 us (level)
  transfers between devices with their start and end apart: 12 -> 12, of which waited for: 8 -> 7; matrix products, arithmetic and copies ran while one was open for 0% -> 0% of each run, Pallas kernels for 12% -> 12%
where the time goes in v7:
time: 36.4 us; the launch traced here: 36.2 us
  starting transfers between devices  13.9 us (38%)
  waiting for transfers between devices  11.4 us (31%)
  Pallas kernels  9.05 us (25%)
  local copies, waits for them, and re-layouts  1.08 us (3%)
  between operations  0.75 us (2%)
    ppermute x6, waiting for transfers between devices, total_over_mesh(): lax.ppermute(mine, axes, [(i, i ^ masks[shares[i]][k]) for i in range(siz...  8.55 us
    ppermute x6, starting transfers between devices, total_over_mesh(): lax.ppermute(mine, axes, [(i, i ^ masks[shares[i]][k]) for i in range(siz...  8.2 us
    pallas_call x1, Pallas kernels, local(): call(second_kernel, (shape((64, LANES), BF16), shape((216, 128), F32), sh...  2.68 us
    ppermute x1, starting transfers between devices, local(): beyond = lax.ppermute(own[:256], ('dp', 'space'), across)  2.57 us
    ppermute x1, waiting for transfers between devices, local(): lax.ppermute(jnp.concatenate([beside[256:], cot], axis=0), ('dp', 'space'...  1.56 us
    pallas_call x1, Pallas kernels, local(): call(first_kernel, shape((32, 128), F32), [pltpu.VMEM((2, 128, LANES), F3...  1.39 us
    pallas_call x1, Pallas kernels, local(): call(near_kernel, (shape((512, 256), BF16), shape((256, 1536), BF16), sha...  1.32 us
    ppermute x1, starting transfers between devices, local(): lax.ppermute(jnp.concatenate([beside[256:], cot], axis=0), ('dp', 'space'...  1.2 us
  transfers between devices with their start and end apart: 12, of which 7 were waited for; matrix products, arithmetic and copies ran while one was open for 0% of the time, Pallas kernels for 12%

profile of v7, /device:TPU:0, one launch (start us, length us, event | category | flops | bytes accessed | tf_op | source)
XLA Modules:
  0.0 36.2 jit_solution(9732383328566915420)
XLA Ops:
  0.6 0.0 copy-start
  0.6 0.9 %copy-done = bf16[1,4,4,64,64]{4,3,2,1,0:T(8,128)(2,1)S(1)} copy-done((bf16[1,4,4,64,64]{4,3,2,1,0:T(8,128)(2,1)S(1)}, bf16[1,4,4,64,64]{4,3,2,1,0:T(8,128)(2,1)}, u32[]{:S(2)}) %copy-start) | copy-done | bytes 131096
  1.6 0.0 copy-start.3
  1.6 0.0 copy-start.2
  1.6 0.0 copy-start.1
  1.6 0.9 %blocks.1.own_ref = bf16[320,256]{1,0:T(8,128)(2,1)S(1)} custom-call(bf16[1,4,4,64,64]{4,3,2,1,0:T(8,128)(2,1)S(1)} %copy-done), custom_call_target="tpu_custom_call" | custom-call | flops 1000000000 | bytes 3000000 | tf_op jit(solution)/shard_map/blocks/pallas_call | solution.py:415
  2.5 0.5 %collective-permute-start = (bf16[320,256]{1,0:T(8,128)(2,1)S(1)}, bf16[320,256]{1,0:T(8,128)(2,1)S(1)}, u32[]{:S(2)}, u32[]{:S(2)}) collective-permute-start(bf16[320,256]{1,0:T(8,128)(2,1)S(1)} %blocks.1.own_ref), channel_id=1, source_target_pairs={{0,1},{1,0},{2,3},{3,2},{4,5},{5,4},{6,7},{7,6},{8,9},{9,8},{10,11... | collective-permute-start | bytes 491528 | tf_op jit(solution)/shard_map/halo/ppermute | solution.py:421
  3.1 2.6 %collective-permute-start.1 = (bf16[256,256]{1,0:T(8,128)(2,1)S(1)}, bf16[256,256]{1,0:T(8,128)(2,1)S(1)}, u32[]{:S(2)}, u32[]{:S(2)}) collective-permute-start(bf16[256,256]{1,0:T(8,128)(2,1)S(1)} %slice.6), channel_id=1, source_target_pairs={{1,2},{3,4},{5,6},{7,8},{9,10},{11,12},{13,14},{17,18},{19,20},{21... | collective-permute-start | bytes 393224 | tf_op jit(solution)/shard_map/halo/ppermute | solution.py:422
  5.6 0.0 copy-done.3
  5.7 0.0 copy-done.2
  5.7 0.1 copy.8
  5.8 0.0 collective-permute-done.near_ref
  5.8 1.2 %collective-permute-start.2 = (bf16[128,256]{1,0:T(8,128)(2,1)S(1)}, bf16[128,256]{1,0:T(8,128)(2,1)S(1)}, u32[]{:S(2)}, u32[]{:S(2)}) collective-permute-start(bf16[128,256]{1,0:T(8,128)(2,1)S(1)} %pad_maximum_fusion.2), channel_id=1, source_target_pairs={{1,2},{3,4},{5,6},{7,8},{9,10},{11,12},{13,14},{17,18},{19,20},{21... | collective-permute-start | bytes 196616 | tf_op jit(solution)/shard_map/halo/ppermute | solution.py:423
  7.0 0.0 copy-done.1
  7.0 1.3 %near.1 = (bf16[512,256]{1,0:T(8,128)(2,1)S(1)}, bf16[256,1536]{1,0:T(8,128)(2,1)S(1)}, bf16[128,3072]{1,0:T(8,128)(2,1)S(1)}, bf16[8,256,256]{2,1,0:T(8,128)(2,...) custom-call(bf16[320,256]{1,0:T(8,128)(2,1)S(1)} %blocks.1.own_ref, ...), custom_call_target="tpu_custom_call" | custom-call | flops 1000000000 | bytes 4000000 | tf_op jit(solution)/shard_map/near/pallas_call | solution.py:425
  8.3 0.2 collective-permute-done.1.far_ref
  8.6 1.6 %collective-permute-done.2.tail_ref = bf16[128,256]{1,0:T(8,128)(2,1)S(1)} collective-permute-done((bf16[128,256]{1,0:T(8,128)(2,1)S(1)}, bf16[128,256]{1,0:T(8,128)(2,1)S(1)}, u32[]{:S(2)}, u32[]{:S(2)}) %collective-permute-start.2) | collective-permute-done | bytes 65568 | tf_op jit(solution)/shard_map/halo/ppermute | solution.py:423
  10.2 0.4 %collective-permute-start.3 = (bf16[320,256]{1,0:T(8,128)(2,1)S(1)}, bf16[320,256]{1,0:T(8,128)(2,1)S(1)}, u32[]{:S(2)}, u32[]{:S(2)}) collective-permute-start(bf16[320,256]{1,0:T(8,128)(2,1)S(1)} %pad_maximum_fusion), channel_id=1, source_target_pairs={{0,1},{1,0},{2,3},{3,2},{4,5},{5,4},{6,7},{7,6},{8,9},{9,8},{10,11... | collective-permute-start | bytes 491528 | tf_op jit(solution)/shard_map/far/ppermute | solution.py:442
  10.6 1.0 %far.1 = (bf16[576,256]{1,0:T(8,128)(2,1)S(1)}, f32[4,256,256]{2,1,0:T(8,128)S(1)}, bf16[3,128,256]{2,1,0:T(8,128)(2,1)S(1)}) custom-call(bf16[320,256]{1,0:T(8,128)(2,1)S(1)} %blocks.1.own_ref, bf16[256,256]{1,0:T(8,128)(2,1)S(1)} %collective-permute-done.1.far_ref, bf16[128,256]{1,0:T(8,128)(2,1)S(1)} %collective-permute-done.2.tail_ref, ...), custom_call_target="tpu_custom_call" | custom-call | flops 1000000000 | bytes 3000000 | tf_op jit(solution)/shard_map/far/pallas_call | solution.py:443
  11.6 0.0 collective-permute-done.3.fwd_ref
  11.6 2.7 %second.1 = (bf16[64,256]{1,0:T(8,128)(2,1)S(1)}, f32[216,128]{1,0:T(8,128)S(1)}, f32[216,128]{1,0:T(8,128)S(1)}, bf16[4,1024,256]{2,1,0:T(8,128)(2,1)S(1)}) custom-call(bf16[320,256]{1,0:T(8,128)(2,1)S(1)} %collective-permute-done.near_ref, bf16[128,256]{1,0:T(8,128)(2,1)S(1)} %collective-permute-done.2.tail_ref, ...), custom_call_target="tpu_custom_call" | custom-call | flops 4000000000 | bytes 6000000 | tf_op jit(solution)/shard_map/second/pallas_call | solution.py:451
  14.3 0.4 %collective-permute-start.4 = (f32[216,128]{1,0:T(8,128)S(1)}, f32[216,128]{1,0:T(8,128)S(1)}, u32[]{:S(2)}, u32[]{:S(2)}) collective-permute-start(f32[216,128]{1,0:T(8,128)S(1)} %get-tuple-element.39), channel_id=1, source_target_pairs={{0,1},{1,0},{2,3},{3,2},{4,5},{5,4},{6,7},{7,6},{8,9},{9,8},{10,11... | collective-permute-start | bytes 331784 | tf_op jit(solution)/shard_map/second/ppermute | solution.py:469
  14.7 1.4 %first.1 = f32[32,128]{1,0:T(8,128)S(1)} custom-call(bf16[4,1024,256]{2,1,0:T(8,128)(2,1)S(1)} %get-tuple-element.40.g_ext, bf16[128,3072]{1,0:T(8,128)(2,1)S(1)} %get-tuple-element.41.wb_ref, bf16[576,256]{1,0:T(8,128)(2,1)S(1)} %get-tuple-element.42.xt_near, f32[4,256,256]{2,1,0:T(8,128)S(1)} %get-tuple-element.43.z_near, ...), custom_call_target="tpu_custom_call" | custom-call | flops 4000000000 | bytes 6000000 | tf_op jit(solution)/shard_map/first/pallas_call | solution.py:471
  16.1 0.0 collective-permute-done.4
  16.2 3.5 %collective-permute-start.6 = (f32[248,128]{1,0:T(8,128)S(1)}, f32[248,128]{1,0:T(8,128)S(1)}, u32[]{:S(2)}, u32[]{:S(2)}) collective-permute-start(f32[248,128]{1,0:T(8,128)S(1)} %pad_maximum_fusion.1), channel_id=1, source_target_pairs={{0,18},{1,13},{2,14},{3,17},{4,8},{5,23},{6,20},{7,11},{8,4},{9,27... | collective-permute-start | bytes 380936 | tf_op jit(solution)/shard_map/total/ppermute | solution.py:395
  19.7 0.0 collective-permute-start.7
  19.7 0.4 collective-permute-start.5
  20.0 2.5 %collective-permute-done.6 = f32[248,128]{1,0:T(8,128)S(1)} collective-permute-done((f32[248,128]{1,0:T(8,128)S(1)}, f32[248,128]{1,0:T(8,128)S(1)}, u32[]{:S(2)}, u32[]{:S(2)}) %collective-permute-start.6) | collective-permute-done | bytes 127008 | tf_op jit(solution)/shard_map/total/ppermute | solution.py:395
  22.6 1.4 %collective-permute-done.7 = f32[248,128]{1,0:T(8,128)S(1)} collective-permute-done((f32[248,128]{1,0:T(8,128)S(1)}, f32[248,128]{1,0:T(8,128)S(1)}, u32[]{:S(2)}, u32[]{:S(2)}) %collective-permute-start.7) | collective-permute-done | bytes 127008 | tf_op jit(solution)/shard_map/total/ppermute | solution.py:395
  24.0 0.0 collective-permute-done.5
  24.1 4.0 %collective-permute-start.8 = (f32[248,128]{1,0:T(8,128)S(1)}, f32[248,128]{1,0:T(8,128)S(1)}, u32[]{:S(2)}, u32[]{:S(2)}) collective-permute-start(f32[248,128]{1,0:T(8,128)S(1)} %add_add_fusion.1), channel_id=1, source_target_pairs={{0,12},{1,19},{2,16},{3,15},{4,22},{5,9},{6,10},{7,21},{8,26},{9,5... | collective-permute-start | bytes 380936 | tf_op jit(solution)/shard_map/total/ppermute | solution.py:395
  28.0 0.0 collective-permute-start.10
  28.0 0.4 collective-permute-start.9
  28.4 0.8 %total.2 = bf16[256,64]{1,0:T(8,128)(2,1)} custom-call(bf16[64,256]{1,0:T(8,128)(2,1)S(1)} %get-tuple-element.48.feat_ref), custom_call_target="tpu_custom_call" | custom-call | flops 10000000 | bytes 1000000 | tf_op jit(solution)/shard_map/total/pallas_call | solution.py:398
  29.2 1.8 %collective-permute-done.8 = f32[248,128]{1,0:T(8,128)S(1)} collective-permute-done((f32[248,128]{1,0:T(8,128)S(1)}, f32[248,128]{1,0:T(8,128)S(1)}, u32[]{:S(2)}, u32[]{:S(2)}) %collective-permute-start.8) | collective-permute-done | bytes 127008 | tf_op jit(solution)/shard_map/total/ppermute | solution.py:395
  31.1 2.7 %collective-permute-done.10 = f32[248,128]{1,0:T(8,128)S(1)} collective-permute-done((f32[248,128]{1,0:T(8,128)S(1)}, f32[248,128]{1,0:T(8,128)S(1)}, u32[]{:S(2)}, u32[]{:S(2)}) %collective-permute-start.10) | collective-permute-done | bytes 127008 | tf_op jit(solution)/shard_map/total/ppermute | solution.py:395
  33.8 0.0 collective-permute-done.9
  33.8 0.5 %collective-permute-start.11 = (f32[248,128]{1,0:T(8,128)S(1)}, f32[248,128]{1,0:T(8,128)S(1)}, u32[]{:S(2)}, u32[]{:S(2)}) collective-permute-start(f32[248,128]{1,0:T(8,128)S(1)} %add_add_fusion.mine_ref), channel_id=1, source_target_pairs={{0,1},{1,0},{2,3},{3,2},{4,5},{5,4},{6,7},{7,6},{8,9},{9,8},{10,11... | collective-permute-start | bytes 380936 | tf_op jit(solution)/shard_map/total/ppermute | solution.py:405
  34.3 1.0 %collective-permute-done.11.other_ref = f32[248,128]{1,0:T(8,128)S(1)} collective-permute-done((f32[248,128]{1,0:T(8,128)S(1)}, f32[248,128]{1,0:T(8,128)S(1)}, u32[]{:S(2)}, u32[]{:S(2)}) %collective-permute-start.11) | collective-permute-done | bytes 127008 | tf_op jit(solution)/shard_map/total/ppermute | solution.py:405
  35.3 0.9 %total.3 = (f32[27,4,32]{2,1,0:T(4,128)}, f32[864,64]{1,0:T(8,128)}) custom-call(f32[248,128]{1,0:T(8,128)S(1)} %add_add_fusion.mine_ref, f32[248,128]{1,0:T(8,128)S(1)} %collective-permute-done.11.other_ref), custom_call_target="tpu_custom_call" | custom-call | tf_op jit(solution)/shard_map/total/pallas_call | solution.py:481
  (9 shorter events, 0.2 us)
Async XLA Ops:
  0.6 1.0 %copy-start = (bf16[1,4,4,64,64]{4,3,2,1,0:T(8,128)(2,1)S(1)}, bf16[1,4,4,64,64]{4,3,2,1,0:T(8,128)(2,1)}, u32[]{:S(2)}) copy-start(bf16[1,4,4,64,64]{4,3,2,1,0:T(8,128)(2,1)} %crop_ref.1) | copy-start | bytes 393220
  1.6 4.1 %copy-start.3 = (bf16[3,3,3,4,32]{4,3,2,1,0:T(4,128)(2,1)S(1)}, bf16[3,3,3,4,32]{4,3,2,1,0:T(4,128)(2,1)}, u32[]{:S(2)}) copy-start(bf16[3,3,3,4,32]{4,3,2,1,0:T(4,128)(2,1)} %param.5) | copy-start | bytes 20740
  1.6 4.1 %copy-start.2 = (bf16[1,64,1,16,16]{1,4,3,2,0:T(8,128)(2,1)S(1)}, bf16[1,64,1,16,16]{1,4,3,2,0:T(8,128)(2,1)}, u32[]{:S(2)}) copy-start(bf16[1,64,1,16,16]{1,4,3,2,0:T(8,128)(2,1)} %param.7) | copy-start | bytes 98308
  1.6 5.4 %copy-start.1 = (bf16[3,3,3,32,64]{4,3,2,1,0:T(8,128)(2,1)S(1)}, bf16[3,3,3,32,64]{4,3,2,1,0:T(8,128)(2,1)}, u32[]{:S(2)}) copy-start(bf16[3,3,3,32,64]{4,3,2,1,0:T(8,128)(2,1)} %param.6) | copy-start | bytes 331780
  2.5 3.2 %collective-permute-start = (bf16[320,256]{1,0:T(8,128)(2,1)S(1)}, bf16[320,256]{1,0:T(8,128)(2,1)S(1)}, u32[]{:S(2)}, u32[]{:S(2)}) collective-permute-start(bf16[320,256]{1,0:T(8,128)(2,1)S(1)} %blocks.1.own_ref), channel_id=1, source_target_pairs={{0,1},{1,0},{2,3},{3,2},{4,5},{5,4},{6,7},{7,6},{8,9},{9,8},{10,11... | collective-permute-start | bytes 491528 | tf_op jit(solution)/shard_map/halo/ppermute | solution.py:421
  3.1 5.5 %collective-permute-start.1 = (bf16[256,256]{1,0:T(8,128)(2,1)S(1)}, bf16[256,256]{1,0:T(8,128)(2,1)S(1)}, u32[]{:S(2)}, u32[]{:S(2)}) collective-permute-start(bf16[256,256]{1,0:T(8,128)(2,1)S(1)} %slice.6), channel_id=1, source_target_pairs={{1,2},{3,4},{5,6},{7,8},{9,10},{11,12},{13,14},{17,18},{19,20},{21... | collective-permute-start | bytes 393224 | tf_op jit(solution)/shard_map/halo/ppermute | solution.py:422
  5.8 4.3 %collective-permute-start.2 = (bf16[128,256]{1,0:T(8,128)(2,1)S(1)}, bf16[128,256]{1,0:T(8,128)(2,1)S(1)}, u32[]{:S(2)}, u32[]{:S(2)}) collective-permute-start(bf16[128,256]{1,0:T(8,128)(2,1)S(1)} %pad_maximum_fusion.2), channel_id=1, source_target_pairs={{1,2},{3,4},{5,6},{7,8},{9,10},{11,12},{13,14},{17,18},{19,20},{21... | collective-permute-start | bytes 196616 | tf_op jit(solution)/shard_map/halo/ppermute | solution.py:423
  10.2 1.5 %collective-permute-start.3 = (bf16[320,256]{1,0:T(8,128)(2,1)S(1)}, bf16[320,256]{1,0:T(8,128)(2,1)S(1)}, u32[]{:S(2)}, u32[]{:S(2)}) collective-permute-start(bf16[320,256]{1,0:T(8,128)(2,1)S(1)} %pad_maximum_fusion), channel_id=1, source_target_pairs={{0,1},{1,0},{2,3},{3,2},{4,5},{5,4},{6,7},{7,6},{8,9},{9,8},{10,11... | collective-permute-start | bytes 491528 | tf_op jit(solution)/shard_map/far/ppermute | solution.py:442
  14.3 1.8 %collective-permute-start.4 = (f32[216,128]{1,0:T(8,128)S(1)}, f32[216,128]{1,0:T(8,128)S(1)}, u32[]{:S(2)}, u32[]{:S(2)}) collective-permute-start(f32[216,128]{1,0:T(8,128)S(1)} %get-tuple-element.39), channel_id=1, source_target_pairs={{0,1},{1,0},{2,3},{3,2},{4,5},{5,4},{6,7},{7,6},{8,9},{9,8},{10,11... | collective-permute-start | bytes 331784 | tf_op jit(solution)/shard_map/second/ppermute | solution.py:469
  16.2 6.4 %collective-permute-start.6 = (f32[248,128]{1,0:T(8,128)S(1)}, f32[248,128]{1,0:T(8,128)S(1)}, u32[]{:S(2)}, u32[]{:S(2)}) collective-permute-start(f32[248,128]{1,0:T(8,128)S(1)} %pad_maximum_fusion.1), channel_id=1, source_target_pairs={{0,18},{1,13},{2,14},{3,17},{4,8},{5,23},{6,20},{7,11},{8,4},{9,27... | collective-permute-start | bytes 380936 | tf_op jit(solution)/shard_map/total/ppermute | solution.py:395
  19.7 4.3 %collective-permute-start.7 = (f32[248,128]{1,0:T(8,128)S(1)}, f32[248,128]{1,0:T(8,128)S(1)}, u32[]{:S(2)}, u32[]{:S(2)}) collective-permute-start(f32[248,128]{1,0:T(8,128)S(1)} %pad_maximum_fusion.1), channel_id=1, source_target_pairs={{0,3},{1,8},{2,11},{3,0},{4,13},{5,6},{6,5},{7,14},{8,1},{9,10},{1... | collective-permute-start | bytes 380936 | tf_op jit(solution)/shard_map/total/ppermute | solution.py:395
  19.7 4.3 %collective-permute-start.5 = (f32[248,128]{1,0:T(8,128)S(1)}, f32[248,128]{1,0:T(8,128)S(1)}, u32[]{:S(2)}, u32[]{:S(2)}) collective-permute-start(f32[248,128]{1,0:T(8,128)S(1)} %pad_maximum_fusion.1), channel_id=1, source_target_pairs={{0,17},{1,4},{2,7},{3,18},{4,1},{5,20},{6,23},{7,2},{8,13},{9,24},... | collective-permute-start | bytes 380936 | tf_op jit(solution)/shard_map/total/ppermute | solution.py:395
  24.1 7.0 %collective-permute-start.8 = (f32[248,128]{1,0:T(8,128)S(1)}, f32[248,128]{1,0:T(8,128)S(1)}, u32[]{:S(2)}, u32[]{:S(2)}) collective-permute-start(f32[248,128]{1,0:T(8,128)S(1)} %add_add_fusion.1), channel_id=1, source_target_pairs={{0,12},{1,19},{2,16},{3,15},{4,22},{5,9},{6,10},{7,21},{8,26},{9,5... | collective-permute-start | bytes 380936 | tf_op jit(solution)/shard_map/total/ppermute | solution.py:395
  28.0 5.7 %collective-permute-start.10 = (f32[248,128]{1,0:T(8,128)S(1)}, f32[248,128]{1,0:T(8,128)S(1)}, u32[]{:S(2)}, u32[]{:S(2)}) collective-permute-start(f32[248,128]{1,0:T(8,128)S(1)} %add_add_fusion.1), channel_id=1, source_target_pairs={{0,5},{1,16},{2,19},{3,6},{4,21},{5,0},{6,3},{7,22},{8,25},{9,12},... | collective-permute-start | bytes 380936 | tf_op jit(solution)/shard_map/total/ppermute | solution.py:395
  28.0 5.7 %collective-permute-start.9 = (f32[248,128]{1,0:T(8,128)S(1)}, f32[248,128]{1,0:T(8,128)S(1)}, u32[]{:S(2)}, u32[]{:S(2)}) collective-permute-start(f32[248,128]{1,0:T(8,128)S(1)} %add_add_fusion.1), channel_id=1, source_target_pairs={{0,9},{1,2},{2,1},{3,10},{4,7},{5,12},{6,15},{7,4},{8,11},{9,0},{1... | collective-permute-start | bytes 380936 | tf_op jit(solution)/shard_map/total/ppermute | solution.py:395
  33.8 1.5 %collective-permute-start.11 = (f32[248,128]{1,0:T(8,128)S(1)}, f32[248,128]{1,0:T(8,128)S(1)}, u32[]{:S(2)}, u32[]{:S(2)}) collective-permute-start(f32[248,128]{1,0:T(8,128)S(1)} %add_add_fusion.mine_ref), channel_id=1, source_target_pairs={{0,1},{1,0},{2,3},{3,2},{4,5},{5,4},{6,7},{7,6},{8,9},{9,8},{10,11... | collective-permute-start | bytes 380936 | tf_op jit(solution)/shard_map/total/ppermute | solution.py:405

commit v8 on v7

--- a/solution.py
+++ b/solution.py
@@ -10,7 +10,7 @@
 F32 = jnp.float32
 BF16 = jnp.bfloat16
 LANES = 256
-ORDERS = (((0, 2, 1), (0, 2, 1)), ((1, 0, 2), (1, 0, 2)))
+ORDERS = (((0, 2, 1), (0, 2, 1)), ((0, 2, 1), (1, 0, 2)))
 SHIFTS = [(1, 0), (-1, 0), (0, 1), (0, -1), (1, 1), (1, -1), (-1, 1), (-1, -1)]
 VMEM = pl.BlockSpec(memory_space=pltpu.VMEM)
 

time: 36.4 us -> 37.2 us (1.022)
  waiting for transfers between devices: 11.4 us -> 12.1 us
    ppermute x6, starting transfers between devices: 8.2 us -> 8.73 us  [total_over_mesh(): lax.ppermute(mine, axes, [(i, i ^ masks[shares[i]][k]) for i in range(siz...]
    ppermute x1, starting transfers between devices: 0.52 us -> 0.07 us  [total_over_mesh(): lax.ppermute(mine, axes, [(i, i ^ 1) for i in range(size)])]
  transfers between devices with their start and end apart: 12 -> 12, of which waited for: 7 -> 8; matrix products, arithmetic and copies ran while one was open for 0% -> 0% of each run, Pallas kernels for 12% -> 12%
where the time goes in v8:
time: 37.2 us; the launch traced here: 37 us
  starting transfers between devices  14 us (38%)
  waiting for transfers between devices  12.1 us (33%)
  Pallas kernels  9.06 us (24%)
  local copies, waits for them, and re-layouts  1.08 us (3%)
  between operations  0.75 us (2%)
    ppermute x6, waiting for transfers between devices, total_over_mesh(): lax.ppermute(mine, axes, [(i, i ^ masks[shares[i]][k]) for i in range(siz...  8.89 us
    ppermute x6, starting transfers between devices, total_over_mesh(): lax.ppermute(mine, axes, [(i, i ^ masks[shares[i]][k]) for i in range(siz...  8.73 us
    pallas_call x1, Pallas kernels, local(): call(second_kernel, (shape((64, LANES), BF16), shape((216, 128), F32), sh...  2.68 us
    ppermute x1, starting transfers between devices, local(): beyond = lax.ppermute(own[:256], ('dp', 'space'), across)  2.57 us
    ppermute x1, waiting for transfers between devices, local(): lax.ppermute(jnp.concatenate([beside[256:], cot], axis=0), ('dp', 'space'...  1.56 us
    pallas_call x1, Pallas kernels, local(): call(first_kernel, shape((32, 128), F32), [pltpu.VMEM((2, 128, LANES), F3...  1.39 us
    ppermute x1, waiting for transfers between devices, total_over_mesh(): lax.ppermute(mine, axes, [(i, i ^ 1) for i in range(size)])  1.33 us
    pallas_call x1, Pallas kernels, local(): call(near_kernel, (shape((512, 256), BF16), shape((256, 1536), BF16), sha...  1.32 us
  transfers between devices with their start and end apart: 12, of which 8 were waited for; matrix products, arithmetic and copies ran while one was open for 0% of the time, Pallas kernels for 12%

profile of v8, /device:TPU:0, one launch (start us, length us, event | category | flops | bytes accessed | tf_op | source)
XLA Modules:
  0.0 37.0 jit_solution(12773762395970452678)
XLA Ops:
  0.6 0.0 copy-start
  0.6 0.9 %copy-done = bf16[1,4,4,64,64]{4,3,2,1,0:T(8,128)(2,1)S(1)} copy-done((bf16[1,4,4,64,64]{4,3,2,1,0:T(8,128)(2,1)S(1)}, bf16[1,4,4,64,64]{4,3,2,1,0:T(8,128)(2,1)}, u32[]{:S(2)}) %copy-start) | copy-done | bytes 131096
  1.6 0.0 copy-start.3
  1.6 0.0 copy-start.2
  1.6 0.0 copy-start.1
  1.6 0.9 %blocks.1.own_ref = bf16[320,256]{1,0:T(8,128)(2,1)S(1)} custom-call(bf16[1,4,4,64,64]{4,3,2,1,0:T(8,128)(2,1)S(1)} %copy-done), custom_call_target="tpu_custom_call" | custom-call | flops 1000000000 | bytes 3000000 | tf_op jit(solution)/shard_map/blocks/pallas_call | solution.py:415
  2.5 0.5 %collective-permute-start = (bf16[320,256]{1,0:T(8,128)(2,1)S(1)}, bf16[320,256]{1,0:T(8,128)(2,1)S(1)}, u32[]{:S(2)}, u32[]{:S(2)}) collective-permute-start(bf16[320,256]{1,0:T(8,128)(2,1)S(1)} %blocks.1.own_ref), channel_id=1, source_target_pairs={{0,1},{1,0},{2,3},{3,2},{4,5},{5,4},{6,7},{7,6},{8,9},{9,8},{10,11... | collective-permute-start | bytes 491528 | tf_op jit(solution)/shard_map/halo/ppermute | solution.py:421
  3.1 2.6 %collective-permute-start.1 = (bf16[256,256]{1,0:T(8,128)(2,1)S(1)}, bf16[256,256]{1,0:T(8,128)(2,1)S(1)}, u32[]{:S(2)}, u32[]{:S(2)}) collective-permute-start(bf16[256,256]{1,0:T(8,128)(2,1)S(1)} %slice.6), channel_id=1, source_target_pairs={{1,2},{3,4},{5,6},{7,8},{9,10},{11,12},{13,14},{17,18},{19,20},{21... | collective-permute-start | bytes 393224 | tf_op jit(solution)/shard_map/halo/ppermute | solution.py:422
  5.6 0.0 copy-done.3
  5.7 0.0 copy-done.2
  5.7 0.1 copy.8
  5.8 0.0 collective-permute-done.near_ref
  5.8 1.2 %collective-permute-start.2 = (bf16[128,256]{1,0:T(8,128)(2,1)S(1)}, bf16[128,256]{1,0:T(8,128)(2,1)S(1)}, u32[]{:S(2)}, u32[]{:S(2)}) collective-permute-start(bf16[128,256]{1,0:T(8,128)(2,1)S(1)} %pad_maximum_fusion.2), channel_id=1, source_target_pairs={{1,2},{3,4},{5,6},{7,8},{9,10},{11,12},{13,14},{17,18},{19,20},{21... | collective-permute-start | bytes 196616 | tf_op jit(solution)/shard_map/halo/ppermute | solution.py:423
  7.0 0.0 copy-done.1
  7.0 1.3 %near.1 = (bf16[512,256]{1,0:T(8,128)(2,1)S(1)}, bf16[256,1536]{1,0:T(8,128)(2,1)S(1)}, bf16[128,3072]{1,0:T(8,128)(2,1)S(1)}, bf16[8,256,256]{2,1,0:T(8,128)(2,...) custom-call(bf16[320,256]{1,0:T(8,128)(2,1)S(1)} %blocks.1.own_ref, ...), custom_call_target="tpu_custom_call" | custom-call | flops 1000000000 | bytes 4000000 | tf_op jit(solution)/shard_map/near/pallas_call | solution.py:425
  8.3 0.2 collective-permute-done.1.far_ref
  8.6 1.6 %collective-permute-done.2.tail_ref = bf16[128,256]{1,0:T(8,128)(2,1)S(1)} collective-permute-done((bf16[128,256]{1,0:T(8,128)(2,1)S(1)}, bf16[128,256]{1,0:T(8,128)(2,1)S(1)}, u32[]{:S(2)}, u32[]{:S(2)}) %collective-permute-start.2) | collective-permute-done | bytes 65568 | tf_op jit(solution)/shard_map/halo/ppermute | solution.py:423
  10.2 0.4 %collective-permute-start.3 = (bf16[320,256]{1,0:T(8,128)(2,1)S(1)}, bf16[320,256]{1,0:T(8,128)(2,1)S(1)}, u32[]{:S(2)}, u32[]{:S(2)}) collective-permute-start(bf16[320,256]{1,0:T(8,128)(2,1)S(1)} %pad_maximum_fusion), channel_id=1, source_target_pairs={{0,1},{1,0},{2,3},{3,2},{4,5},{5,4},{6,7},{7,6},{8,9},{9,8},{10,11... | collective-permute-start | bytes 491528 | tf_op jit(solution)/shard_map/far/ppermute | solution.py:442
  10.6 1.0 %far.1 = (bf16[576,256]{1,0:T(8,128)(2,1)S(1)}, f32[4,256,256]{2,1,0:T(8,128)S(1)}, bf16[3,128,256]{2,1,0:T(8,128)(2,1)S(1)}) custom-call(bf16[320,256]{1,0:T(8,128)(2,1)S(1)} %blocks.1.own_ref, bf16[256,256]{1,0:T(8,128)(2,1)S(1)} %collective-permute-done.1.far_ref, bf16[128,256]{1,0:T(8,128)(2,1)S(1)} %collective-permute-done.2.tail_ref, ...), custom_call_target="tpu_custom_call" | custom-call | flops 1000000000 | bytes 3000000 | tf_op jit(solution)/shard_map/far/pallas_call | solution.py:443
  11.6 0.0 collective-permute-done.3.fwd_ref
  11.6 2.7 %second.1 = (bf16[64,256]{1,0:T(8,128)(2,1)S(1)}, f32[216,128]{1,0:T(8,128)S(1)}, f32[216,128]{1,0:T(8,128)S(1)}, bf16[4,1024,256]{2,1,0:T(8,128)(2,1)S(1)}) custom-call(bf16[320,256]{1,0:T(8,128)(2,1)S(1)} %collective-permute-done.near_ref, bf16[128,256]{1,0:T(8,128)(2,1)S(1)} %collective-permute-done.2.tail_ref, ...), custom_call_target="tpu_custom_call" | custom-call | flops 4000000000 | bytes 6000000 | tf_op jit(solution)/shard_map/second/pallas_call | solution.py:451
  14.3 0.4 %collective-permute-start.4 = (f32[216,128]{1,0:T(8,128)S(1)}, f32[216,128]{1,0:T(8,128)S(1)}, u32[]{:S(2)}, u32[]{:S(2)}) collective-permute-start(f32[216,128]{1,0:T(8,128)S(1)} %get-tuple-element.39), channel_id=1, source_target_pairs={{0,1},{1,0},{2,3},{3,2},{4,5},{5,4},{6,7},{7,6},{8,9},{9,8},{10,11... | collective-permute-start | bytes 331784 | tf_op jit(solution)/shard_map/second/ppermute | solution.py:469
  14.7 1.4 %first.1 = f32[32,128]{1,0:T(8,128)S(1)} custom-call(bf16[4,1024,256]{2,1,0:T(8,128)(2,1)S(1)} %get-tuple-element.40.g_ext, bf16[128,3072]{1,0:T(8,128)(2,1)S(1)} %get-tuple-element.41.wb_ref, bf16[576,256]{1,0:T(8,128)(2,1)S(1)} %get-tuple-element.42.xt_near, f32[4,256,256]{2,1,0:T(8,128)S(1)} %get-tuple-element.43.z_near, ...), custom_call_target="tpu_custom_call" | custom-call | flops 4000000000 | bytes 6000000 | tf_op jit(solution)/shard_map/first/pallas_call | solution.py:471
  16.1 0.0 collective-permute-done.4
  16.2 3.5 %collective-permute-start.6 = (f32[248,128]{1,0:T(8,128)S(1)}, f32[248,128]{1,0:T(8,128)S(1)}, u32[]{:S(2)}, u32[]{:S(2)}) collective-permute-start(f32[248,128]{1,0:T(8,128)S(1)} %pad_maximum_fusion.1), channel_id=1, source_target_pairs={{0,18},{1,13},{2,14},{3,17},{4,8},{5,23},{6,20},{7,11},{8,4},{9,27... | collective-permute-start | bytes 380936 | tf_op jit(solution)/shard_map/total/ppermute | solution.py:395
  19.7 0.0 collective-permute-start.7
  19.7 0.4 collective-permute-start.5
  20.0 2.5 %collective-permute-done.6 = f32[248,128]{1,0:T(8,128)S(1)} collective-permute-done((f32[248,128]{1,0:T(8,128)S(1)}, f32[248,128]{1,0:T(8,128)S(1)}, u32[]{:S(2)}, u32[]{:S(2)}) %collective-permute-start.6) | collective-permute-done | bytes 127008 | tf_op jit(solution)/shard_map/total/ppermute | solution.py:395
  22.6 1.4 %collective-permute-done.7 = f32[248,128]{1,0:T(8,128)S(1)} collective-permute-done((f32[248,128]{1,0:T(8,128)S(1)}, f32[248,128]{1,0:T(8,128)S(1)}, u32[]{:S(2)}, u32[]{:S(2)}) %collective-permute-start.7) | collective-permute-done | bytes 127008 | tf_op jit(solution)/shard_map/total/ppermute | solution.py:395
  24.0 0.0 collective-permute-done.5
  24.1 3.5 %collective-permute-start.8 = (f32[248,128]{1,0:T(8,128)S(1)}, f32[248,128]{1,0:T(8,128)S(1)}, u32[]{:S(2)}, u32[]{:S(2)}) collective-permute-start(f32[248,128]{1,0:T(8,128)S(1)} %add_add_fusion.1), channel_id=1, source_target_pairs={{0,9},{1,19},{2,16},{3,10},{4,22},{5,12},{6,15},{7,21},{8,26},{9,0... | collective-permute-start | bytes 380936 | tf_op jit(solution)/shard_map/total/ppermute | solution.py:395
  27.6 1.4 %collective-permute-start.10 = (f32[248,128]{1,0:T(8,128)S(1)}, f32[248,128]{1,0:T(8,128)S(1)}, u32[]{:S(2)}, u32[]{:S(2)}) collective-permute-start(f32[248,128]{1,0:T(8,128)S(1)} %add_add_fusion.1), channel_id=1, source_target_pairs={{0,12},{1,16},{2,19},{3,15},{4,21},{5,9},{6,10},{7,22},{8,25},{9,5... | collective-permute-start | bytes 380936 | tf_op jit(solution)/shard_map/total/ppermute | solution.py:395
  28.9 0.0 collective-permute-start.9
  28.9 0.8 %total.2 = bf16[256,64]{1,0:T(8,128)(2,1)} custom-call(bf16[64,256]{1,0:T(8,128)(2,1)S(1)} %get-tuple-element.48.feat_ref), custom_call_target="tpu_custom_call" | custom-call | flops 10000000 | bytes 1000000 | tf_op jit(solution)/shard_map/total/pallas_call | solution.py:398
  29.7 0.5 %collective-permute-done.8 = f32[248,128]{1,0:T(8,128)S(1)} collective-permute-done((f32[248,128]{1,0:T(8,128)S(1)}, f32[248,128]{1,0:T(8,128)S(1)}, u32[]{:S(2)}, u32[]{:S(2)}) %collective-permute-start.8) | collective-permute-done | bytes 127008 | tf_op jit(solution)/shard_map/total/ppermute | solution.py:395
  30.2 4.3 %collective-permute-done.10 = f32[248,128]{1,0:T(8,128)S(1)} collective-permute-done((f32[248,128]{1,0:T(8,128)S(1)}, f32[248,128]{1,0:T(8,128)S(1)}, u32[]{:S(2)}, u32[]{:S(2)}) %collective-permute-start.10) | collective-permute-done | bytes 127008 | tf_op jit(solution)/shard_map/total/ppermute | solution.py:395
  34.5 0.2 collective-permute-done.9
  34.7 0.1 collective-permute-start.11
  34.8 1.3 %collective-permute-done.11.other_ref = f32[248,128]{1,0:T(8,128)S(1)} collective-permute-done((f32[248,128]{1,0:T(8,128)S(1)}, f32[248,128]{1,0:T(8,128)S(1)}, u32[]{:S(2)}, u32[]{:S(2)}) %collective-permute-start.11) | collective-permute-done | bytes 127008 | tf_op jit(solution)/shard_map/total/ppermute | solution.py:405
  36.1 0.9 %total.3 = (f32[27,4,32]{2,1,0:T(4,128)}, f32[864,64]{1,0:T(8,128)}) custom-call(f32[248,128]{1,0:T(8,128)S(1)} %add_add_fusion.mine_ref, f32[248,128]{1,0:T(8,128)S(1)} %collective-permute-done.11.other_ref), custom_call_target="tpu_custom_call" | custom-call | tf_op jit(solution)/shard_map/total/pallas_call | solution.py:481
  (9 shorter events, 0.2 us)
Async XLA Ops:
  0.6 1.0 %copy-start = (bf16[1,4,4,64,64]{4,3,2,1,0:T(8,128)(2,1)S(1)}, bf16[1,4,4,64,64]{4,3,2,1,0:T(8,128)(2,1)}, u32[]{:S(2)}) copy-start(bf16[1,4,4,64,64]{4,3,2,1,0:T(8,128)(2,1)} %crop_ref.1) | copy-start | bytes 393220
  1.6 4.1 %copy-start.3 = (bf16[3,3,3,4,32]{4,3,2,1,0:T(4,128)(2,1)S(1)}, bf16[3,3,3,4,32]{4,3,2,1,0:T(4,128)(2,1)}, u32[]{:S(2)}) copy-start(bf16[3,3,3,4,32]{4,3,2,1,0:T(4,128)(2,1)} %param.5) | copy-start | bytes 20740
  1.6 4.1 %copy-start.2 = (bf16[1,64,1,16,16]{1,4,3,2,0:T(8,128)(2,1)S(1)}, bf16[1,64,1,16,16]{1,4,3,2,0:T(8,128)(2,1)}, u32[]{:S(2)}) copy-start(bf16[1,64,1,16,16]{1,4,3,2,0:T(8,128)(2,1)} %param.7) | copy-start | bytes 98308
  1.6 5.4 %copy-start.1 = (bf16[3,3,3,32,64]{4,3,2,1,0:T(8,128)(2,1)S(1)}, bf16[3,3,3,32,64]{4,3,2,1,0:T(8,128)(2,1)}, u32[]{:S(2)}) copy-start(bf16[3,3,3,32,64]{4,3,2,1,0:T(8,128)(2,1)} %param.6) | copy-start | bytes 331780
  2.5 3.2 %collective-permute-start = (bf16[320,256]{1,0:T(8,128)(2,1)S(1)}, bf16[320,256]{1,0:T(8,128)(2,1)S(1)}, u32[]{:S(2)}, u32[]{:S(2)}) collective-permute-start(bf16[320,256]{1,0:T(8,128)(2,1)S(1)} %blocks.1.own_ref), channel_id=1, source_target_pairs={{0,1},{1,0},{2,3},{3,2},{4,5},{5,4},{6,7},{7,6},{8,9},{9,8},{10,11... | collective-permute-start | bytes 491528 | tf_op jit(solution)/shard_map/halo/ppermute | solution.py:421
  3.1 5.5 %collective-permute-start.1 = (bf16[256,256]{1,0:T(8,128)(2,1)S(1)}, bf16[256,256]{1,0:T(8,128)(2,1)S(1)}, u32[]{:S(2)}, u32[]{:S(2)}) collective-permute-start(bf16[256,256]{1,0:T(8,128)(2,1)S(1)} %slice.6), channel_id=1, source_target_pairs={{1,2},{3,4},{5,6},{7,8},{9,10},{11,12},{13,14},{17,18},{19,20},{21... | collective-permute-start | bytes 393224 | tf_op jit(solution)/shard_map/halo/ppermute | solution.py:422
  5.8 4.3 %collective-permute-start.2 = (bf16[128,256]{1,0:T(8,128)(2,1)S(1)}, bf16[128,256]{1,0:T(8,128)(2,1)S(1)}, u32[]{:S(2)}, u32[]{:S(2)}) collective-permute-start(bf16[128,256]{1,0:T(8,128)(2,1)S(1)} %pad_maximum_fusion.2), channel_id=1, source_target_pairs={{1,2},{3,4},{5,6},{7,8},{9,10},{11,12},{13,14},{17,18},{19,20},{21... | collective-permute-start | bytes 196616 | tf_op jit(solution)/shard_map/halo/ppermute | solution.py:423
  10.2 1.5 %collective-permute-start.3 = (bf16[320,256]{1,0:T(8,128)(2,1)S(1)}, bf16[320,256]{1,0:T(8,128)(2,1)S(1)}, u32[]{:S(2)}, u32[]{:S(2)}) collective-permute-start(bf16[320,256]{1,0:T(8,128)(2,1)S(1)} %pad_maximum_fusion), channel_id=1, source_target_pairs={{0,1},{1,0},{2,3},{3,2},{4,5},{5,4},{6,7},{7,6},{8,9},{9,8},{10,11... | collective-permute-start | bytes 491528 | tf_op jit(solution)/shard_map/far/ppermute | solution.py:442
  14.3 1.8 %collective-permute-start.4 = (f32[216,128]{1,0:T(8,128)S(1)}, f32[216,128]{1,0:T(8,128)S(1)}, u32[]{:S(2)}, u32[]{:S(2)}) collective-permute-start(f32[216,128]{1,0:T(8,128)S(1)} %get-tuple-element.39), channel_id=1, source_target_pairs={{0,1},{1,0},{2,3},{3,2},{4,5},{5,4},{6,7},{7,6},{8,9},{9,8},{10,11... | collective-permute-start | bytes 331784 | tf_op jit(solution)/shard_map/second/ppermute | solution.py:469
  16.2 6.4 %collective-permute-start.6 = (f32[248,128]{1,0:T(8,128)S(1)}, f32[248,128]{1,0:T(8,128)S(1)}, u32[]{:S(2)}, u32[]{:S(2)}) collective-permute-start(f32[248,128]{1,0:T(8,128)S(1)} %pad_maximum_fusion.1), channel_id=1, source_target_pairs={{0,18},{1,13},{2,14},{3,17},{4,8},{5,23},{6,20},{7,11},{8,4},{9,27... | collective-permute-start | bytes 380936 | tf_op jit(solution)/shard_map/total/ppermute | solution.py:395
  19.7 4.3 %collective-permute-start.7 = (f32[248,128]{1,0:T(8,128)S(1)}, f32[248,128]{1,0:T(8,128)S(1)}, u32[]{:S(2)}, u32[]{:S(2)}) collective-permute-start(f32[248,128]{1,0:T(8,128)S(1)} %pad_maximum_fusion.1), channel_id=1, source_target_pairs={{0,3},{1,8},{2,11},{3,0},{4,13},{5,6},{6,5},{7,14},{8,1},{9,10},{1... | collective-permute-start | bytes 380936 | tf_op jit(solution)/shard_map/total/ppermute | solution.py:395
  19.7 4.3 %collective-permute-start.5 = (f32[248,128]{1,0:T(8,128)S(1)}, f32[248,128]{1,0:T(8,128)S(1)}, u32[]{:S(2)}, u32[]{:S(2)}) collective-permute-start(f32[248,128]{1,0:T(8,128)S(1)} %pad_maximum_fusion.1), channel_id=1, source_target_pairs={{0,17},{1,4},{2,7},{3,18},{4,1},{5,20},{6,23},{7,2},{8,13},{9,24},... | collective-permute-start | bytes 380936 | tf_op jit(solution)/shard_map/total/ppermute | solution.py:395
  24.1 6.1 %collective-permute-start.8 = (f32[248,128]{1,0:T(8,128)S(1)}, f32[248,128]{1,0:T(8,128)S(1)}, u32[]{:S(2)}, u32[]{:S(2)}) collective-permute-start(f32[248,128]{1,0:T(8,128)S(1)} %add_add_fusion.1), channel_id=1, source_target_pairs={{0,9},{1,19},{2,16},{3,10},{4,22},{5,12},{6,15},{7,21},{8,26},{9,0... | collective-permute-start | bytes 380936 | tf_op jit(solution)/shard_map/total/ppermute | solution.py:395
  27.6 6.9 %collective-permute-start.10 = (f32[248,128]{1,0:T(8,128)S(1)}, f32[248,128]{1,0:T(8,128)S(1)}, u32[]{:S(2)}, u32[]{:S(2)}) collective-permute-start(f32[248,128]{1,0:T(8,128)S(1)} %add_add_fusion.1), channel_id=1, source_target_pairs={{0,12},{1,16},{2,19},{3,15},{4,21},{5,9},{6,10},{7,22},{8,25},{9,5... | collective-permute-start | bytes 380936 | tf_op jit(solution)/shard_map/total/ppermute | solution.py:395
  28.9 5.7 %collective-permute-start.9 = (f32[248,128]{1,0:T(8,128)S(1)}, f32[248,128]{1,0:T(8,128)S(1)}, u32[]{:S(2)}, u32[]{:S(2)}) collective-permute-start(f32[248,128]{1,0:T(8,128)S(1)} %add_add_fusion.1), channel_id=1, source_target_pairs={{0,5},{1,2},{2,1},{3,6},{4,7},{5,0},{6,3},{7,4},{8,11},{9,12},{10,... | collective-permute-start | bytes 380936 | tf_op jit(solution)/shard_map/total/ppermute | solution.py:395
  34.7 1.4 %collective-permute-start.11 = (f32[248,128]{1,0:T(8,128)S(1)}, f32[248,128]{1,0:T(8,128)S(1)}, u32[]{:S(2)}, u32[]{:S(2)}) collective-permute-start(f32[248,128]{1,0:T(8,128)S(1)} %add_add_fusion.mine_ref), channel_id=1, source_target_pairs={{0,1},{1,0},{2,3},{3,2},{4,5},{5,4},{6,7},{7,6},{8,9},{9,8},{10,11... | collective-permute-start | bytes 380936 | tf_op jit(solution)/shard_map/total/ppermute | solution.py:405
